TPU v7x, 256 devices: a whole 4x4x8 slice. The times are simulated.
256 devices in a mesh: ctx: 64 (over z, y, core), tp: 4 (over x).
Axes of the slice: x: 4, y: 4, z: 8, core: 2. Of those that a mesh axis runs over, the one named last changes fastest.
Arguments:
- ctx_queries: bfloat16 [16384, 8192], P('ctx', 'tp'), may hold values from -16 to 16
- ctx_keys: bfloat16 [16384, 1024], P('ctx', 'tp'), may hold values from -18 to 18
- ctx_values: bfloat16 [16384, 1024], P('ctx', 'tp'), may hold values from -6 to 6
- block_map: int32 [64], replicated, may hold values from 0 to 63, each once
- cache_keys: bfloat16 [16384, 1024], P('ctx', 'tp'), may hold values from -18 to 18
- cache_values: bfloat16 [16384, 1024], P('ctx', 'tp'), may hold values from -6 to 6
- dec_queries: bfloat16 [4, 64, 8192], P(None, 'ctx', 'tp'), may hold values from -16 to 16
- new_keys: bfloat16 [4, 64, 1024], P(None, 'ctx', 'tp'), may hold values from -15 to 15
- new_values: bfloat16 [4, 64, 1024], P(None, 'ctx', 'tp'), may hold values from -6 to 6
- cache_lengths: int32 [64], replicated, may hold values from 2048 to 16384, as said below
- owner: int32 [64], replicated, may hold values from 0 to 63, each once
- out_weight: bfloat16 [8192, 8192], P('tp', 'ctx'), may hold values from -0.0625 to 0.0625
Outputs:
- ctx_out: bfloat16 [16384, 8192], P('ctx', 'tp')
- dec_out: bfloat16 [4, 64, 8192], P(None, 'tp', 'ctx')
Inputs may be any that keep to these rules, and one draw needn't show every extreme that they name: `cache_lengths`: one request has the whole cache of 16384 rows valid and one only 2048. `block_map`: each block number once. `owner`: each slot once.
All inputs are finite; a program needn't handle non-finite values.
Results may differ from a plain program's by a relative error of at most 0.005.
Values may be sent and summed in bfloat16 or wider, within the bound.
No kernel may reach another device: no remote copies, remote signals or barrier semaphores. Data moves between devices by JAX's collectives and lax.ppermute only.
A program may use at most 384 MiB of HBM per device.

v0:
```python
import math

import jax
import jax.numpy as jnp
from jax import lax
from jax.sharding import PartitionSpec as P

HD = 128
STEPS = 4


LOW_SCORE = -1e30
FLOOR_SCORE = -1e29


def spread(x, axis, root):
    mine = lax.axis_index(axis) == root
    return lax.psum(jnp.where(mine, x, jnp.zeros_like(x)), axis)


def joined(value, axis, join):
    pieces = jax.tree.map(lambda part: lax.all_gather(part, axis), value)
    head = jax.tree.map(lambda part: part[0], pieces)
    tail = jax.tree.map(lambda part: part[1:], pieces)
    total, _ = lax.scan(lambda total, slab: (join(total, slab), None), head, tail)
    return total


def combine(first, second):
    highest = jnp.maximum(first[0], second[0])
    first_factor = jnp.exp(first[0] - highest)
    second_factor = jnp.exp(second[0] - highest)
    return (
        highest,
        first[1] * first_factor + second[1] * second_factor,
        first[2] * first_factor[..., None] + second[2] * second_factor[..., None],
    )


def recent_part(step_queries, keys_seen, values_seen, score_scale):
    recent_scores = (
        jnp.einsum("pkgd,ipkd->pkgi", step_queries, keys_seen, preferred_element_type=jnp.float32)
        * score_scale
    )
    recent_top = jnp.max(recent_scores, -1)
    recent_weights = jnp.exp(recent_scores - recent_top[..., None])
    recent_total = jnp.sum(recent_weights, -1)
    recent_sum = jnp.einsum(
        "pkgi,ipkd->pkgd",
        recent_weights.astype(jnp.bfloat16),
        values_seen,
        preferred_element_type=jnp.float32,
    )
    return (recent_top, recent_total, recent_sum)


def on_device(
    ctx_queries,
    ctx_keys,
    ctx_values,
    block_map,
    cache_keys,
    cache_values,
    dec_queries,
    new_keys,
    new_values,
    cache_lengths,
    owner,
    out_weight,
):
    score_scale = 1.0 / math.sqrt(HD)
    block_rows = ctx_queries.shape[0]
    kv_local = ctx_keys.shape[1] // HD
    heads = ctx_queries.shape[1] // HD
    group_size = heads // kv_local
    device_count = lax.axis_size("ctx")
    anchor_index = jnp.sum(jnp.where(block_map == 0, jnp.arange(device_count, dtype=jnp.int32), 0))
    anchor_keys, anchor_values = (
        spread(ctx_keys, "ctx", anchor_index),
        spread(ctx_values, "ctx", anchor_index),
    )
    is_first = block_map[lax.axis_index("ctx")] == 0
    causal = jnp.arange(block_rows)[:, None] >= jnp.arange(block_rows)[None, :]
    queries = ctx_queries.reshape(block_rows, kv_local, group_size, HD)
    own_keys = ctx_keys.reshape(block_rows, kv_local, HD)
    own_values = ctx_values.reshape(block_rows, kv_local, HD)
    far_keys = anchor_keys.reshape(block_rows, kv_local, HD)
    far_values = anchor_values.reshape(block_rows, kv_local, HD)
    pieces = []
    for kv_head in range(kv_local):
        query_block = queries[:, kv_head]
        own_scores = (
            jnp.einsum(
                "tgd,sd->gts", query_block, own_keys[:, kv_head], preferred_element_type=jnp.float32
            )
            * score_scale
        )
        own_scores = jnp.where(causal, own_scores, LOW_SCORE)
        far_scores = (
            jnp.einsum(
                "tgd,sd->gts", query_block, far_keys[:, kv_head], preferred_element_type=jnp.float32
            )
            * score_scale
        )
        far_scores = jnp.where(is_first, LOW_SCORE, far_scores)
        highest = jnp.maximum(jnp.max(own_scores, -1), jnp.max(far_scores, -1))
        own_weights = jnp.exp(own_scores - highest[..., None])
        far_weights = jnp.exp(far_scores - highest[..., None])
        row_total = jnp.sum(own_weights, -1) + jnp.sum(far_weights, -1)
        weighted = jnp.einsum(
            "gts,sd->gtd",
            own_weights.astype(jnp.bfloat16),
            own_values[:, kv_head],
            preferred_element_type=jnp.float32,
        )
        weighted = weighted + jnp.einsum(
            "gts,sd->gtd",
            far_weights.astype(jnp.bfloat16),
            far_values[:, kv_head],
            preferred_element_type=jnp.float32,
        )
        pieces.append(jnp.transpose(weighted / row_total[..., None], (1, 0, 2)))
    ctx_out = jnp.stack(pieces, axis=1).reshape(block_rows, heads * HD).astype(jnp.bfloat16)
    gathered_queries, gathered_keys, gathered_values = (
        lax.all_gather(dec_queries, "ctx", axis=1, tiled=True),
        lax.all_gather(new_keys, "ctx", axis=1, tiled=True),
        lax.all_gather(new_values, "ctx", axis=1, tiled=True),
    )
    requests = gathered_queries.shape[1]
    cache_rows = cache_keys.shape[0]
    slot_match = owner[:, None] == jnp.arange(requests, dtype=jnp.int32)[None, :]
    slot_lengths = jnp.sum(jnp.where(slot_match, cache_lengths[:, None], 0), axis=0)
    positions = lax.axis_index("ctx") * cache_rows + jnp.arange(cache_rows, dtype=jnp.int32)
    valid_rows = (positions[None, :] < slot_lengths[:, None])[:, None, None, :]
    shard_keys = cache_keys.reshape(cache_rows, kv_local, HD)
    shard_values = cache_values.reshape(cache_rows, kv_local, HD)
    reorder = slot_match.astype(jnp.bfloat16)
    tp_rows = requests // lax.axis_size("tp")
    results = []
    for step in range(STEPS):
        step_queries = gathered_queries[step].reshape(requests, kv_local, group_size, HD)
        scores = (
            jnp.einsum(
                "pkgd,ckd->pkgc", step_queries, shard_keys, preferred_element_type=jnp.float32
            )
            * score_scale
        )
        scores = jnp.where(valid_rows, scores, LOW_SCORE)
        shard_top = jnp.max(scores, -1)
        weights = jnp.exp(scores - jnp.maximum(shard_top, FLOOR_SCORE)[..., None])
        shard_total = jnp.sum(weights, -1)
        shard_sum = jnp.einsum(
            "pkgc,ckd->pkgd",
            weights.astype(jnp.bfloat16),
            shard_values,
            preferred_element_type=jnp.float32,
        )
        merged = joined((shard_top, shard_total, shard_sum), "ctx", combine)
        keys_seen = gathered_keys[: step + 1].reshape(step + 1, requests, kv_local, HD)
        values_seen = gathered_values[: step + 1].reshape(step + 1, requests, kv_local, HD)
        final = combine(merged, recent_part(step_queries, keys_seen, values_seen, score_scale))
        attention = (
            (final[2] / final[1][..., None]).reshape(requests, heads * HD).astype(jnp.bfloat16)
        )
        ordered = jnp.dot(reorder, attention, preferred_element_type=jnp.float32).astype(
            jnp.bfloat16
        )

        def project(first_row, row_count, ordered=ordered):
            return jnp.dot(ordered, out_weight, preferred_element_type=jnp.float32)

        results.append(
            lax.psum_scatter(
                project(jnp.int32(0), lax.axis_size("tp") * tp_rows),
                "tp",
                scatter_dimension=0,
                tiled=True,
            ).astype(jnp.bfloat16)
        )
    dec_out = jnp.stack(results, axis=0)
    return (ctx_out, dec_out)


def solution(mesh):
    in_specs = (
        P("ctx", "tp"),
        P("ctx", "tp"),
        P("ctx", "tp"),
        P(),
        P("ctx", "tp"),
        P("ctx", "tp"),
        P(None, "ctx", "tp"),
        P(None, "ctx", "tp"),
        P(None, "ctx", "tp"),
        P(),
        P(),
        P("tp", "ctx"),
    )
    out_specs = (P("ctx", "tp"), P(None, "tp", "ctx"))
    return jax.shard_map(
        on_device, mesh=mesh, in_specs=in_specs, out_specs=out_specs, check_vma=False
    )
```

profile of v0, /device:TPU:1, one launch (start us, length us, event | category | flops | bytes accessed | tf_op | source)
XLA Modules:
  0.0 1619.7 jit_solution(5544613399921599329)
XLA Ops:
  15.6 75.8 %all-gather.18.cloned.1.call-done = bf16[4,64,2048]{2,0,1:T(4,128)(2,1)} async-done(((bf16[4,1,2048]{2,0,1:T(4,128)(2,1)}), bf16[4,64,2048]{2,0,1:T(4,128)(2,1)}) %all-gather.18.cloned.1.call-update) | async-done | bytes 1048592 | tf_op jit(solution)/shard_map/all_gather | solution.py:125
  91.4 7.4 slice_reduce_fusion.3
  108.8 48.3 %all_gather.88 = bf16[4,64,256]{2,0,1:T(4,128)(2,1)S(1)} all-gather(bf16[4,1,256]{2,0,1:T(4,128)(2,1)S(1)} %copy-done.59), channel_id=1, replica_groups=mesh['ctx'=64,'tp'=4] {'ctx'}, dimensions={1}, use_global_device_ids=true | all-gather | bytes 133120 | tf_op jit(solution)/shard_map/all_gather | solution.py:126
  157.1 47.9 %all_gather.89 = bf16[4,64,256]{2,0,1:T(4,128)(2,1)S(1)} all-gather(bf16[4,1,256]{2,0,1:T(4,128)(2,1)S(1)} %copy-done.60), channel_id=1, replica_groups=mesh['ctx'=64,'tp'=4] {'ctx'}, dimensions={1}, use_global_device_ids=true | all-gather | bytes 133120 | tf_op jit(solution)/shard_map/all_gather | solution.py:127
  210.2 57.8 %all-reduce.3.cloned.1.call-done = (bf16[256,2,128]{2,0,1:T(8,128)(2,1)}, bf16[256,2,128]{0,2,1:T(8,128)(2,1)}) async-done(((bf16[256,2,128]{2,0,1:T(8,128)(2,1)}, bf16[256,2,128]{0,2,1:T(8,128)(2,1)}), (bf16[256,2,128]{2,0,1:T(8,128)(2,1)}, bf16[256,2,128]{0,2,1:T(8,128)(2,1)})) %all-reduce.3.cloned.1.call-update) | async-done | bytes 262160 | tf_op jit(solution)/shard_map/psum | solution.py:18
  276.1 52.1 %all-gather.1 = f32[4096,2,8]{2,1,0:T(2,128)S(1)} all-gather(f32[64,2,8]{2,1,0:T(2,128)S(1)} %copy.439), channel_id=3, replica_groups=mesh['ctx'=64,'tp'=4] {'ctx'}, dimensions={0}, use_global_device_ids=true | all-gather | bytes 266240 | tf_op jit(solution)/shard_map/all_gather | solution.py:22
  331.5 55.9 %all-gather = f32[4096,2,8]{2,1,0:T(2,128)S(1)} all-gather(f32[64,2,8]{2,1,0:T(2,128)S(1)} %copy.438), channel_id=2, replica_groups=mesh['ctx'=64,'tp'=4] {'ctx'}, dimensions={0}, use_global_device_ids=true | all-gather | bytes 266240 | tf_op jit(solution)/shard_map/all_gather | solution.py:22
  390.8 53.8 %all-gather.4 = f32[4096,2,8]{2,1,0:T(2,128)S(1)} all-gather(f32[64,2,8]{2,1,0:T(2,128)S(1)} %copy.457), channel_id=6, replica_groups=mesh['ctx'=64,'tp'=4] {'ctx'}, dimensions={0}, use_global_device_ids=true | all-gather | bytes 266240 | tf_op jit(solution)/shard_map/all_gather | solution.py:22
  448.0 52.9 %all-gather.3 = f32[4096,2,8]{2,1,0:T(2,128)S(1)} all-gather(f32[64,2,8]{2,1,0:T(2,128)S(1)} %copy.456), channel_id=5, replica_groups=mesh['ctx'=64,'tp'=4] {'ctx'}, dimensions={0}, use_global_device_ids=true | all-gather | bytes 266240 | tf_op jit(solution)/shard_map/all_gather | solution.py:22
  504.2 56.3 %all-gather.7 = f32[4096,2,8]{2,1,0:T(2,128)S(1)} all-gather(f32[64,2,8]{2,1,0:T(2,128)S(1)} %copy.477), channel_id=9, replica_groups=mesh['ctx'=64,'tp'=4] {'ctx'}, dimensions={0}, use_global_device_ids=true | all-gather | bytes 266240 | tf_op jit(solution)/shard_map/all_gather | solution.py:22
  563.8 52.6 %all-gather.6 = f32[4096,2,8]{2,1,0:T(2,128)S(1)} all-gather(f32[64,2,8]{2,1,0:T(2,128)S(1)} %copy.476), channel_id=8, replica_groups=mesh['ctx'=64,'tp'=4] {'ctx'}, dimensions={0}, use_global_device_ids=true | all-gather | bytes 266240 | tf_op jit(solution)/shard_map/all_gather | solution.py:22
  620.6 55.1 %all-gather.10 = f32[4096,2,8]{2,1,0:T(2,128)S(1)} all-gather(f32[64,2,8]{2,1,0:T(2,128)S(1)} %copy.497), channel_id=12, replica_groups=mesh['ctx'=64,'tp'=4] {'ctx'}, dimensions={0}, use_global_device_ids=true | all-gather | bytes 266240 | tf_op jit(solution)/shard_map/all_gather | solution.py:22
  679.3 55.4 %all-gather.9 = f32[4096,2,8]{2,1,0:T(2,128)S(1)} all-gather(f32[64,2,8]{2,1,0:T(2,128)S(1)} %copy.496), channel_id=11, replica_groups=mesh['ctx'=64,'tp'=4] {'ctx'}, dimensions={0}, use_global_device_ids=true | all-gather | bytes 266240 | tf_op jit(solution)/shard_map/all_gather | solution.py:22
  738.0 4.4 copy.448
  742.5 5.4 copy.447
  749.6 4.4 copy.466
  754.7 5.4 copy.465
  762.8 5.4 copy.486
  768.3 5.4 copy.485
  776.5 4.4 copy.506
  781.0 5.4 copy.505
  791.2 22.6 %slice.216 = f32[4032,2,8,128]{3,2,0,1:T(8,128)} slice(f32[4096,2,8,128]{3,2,0,1:T(8,128)} %all-gather.20.cloned.1.call-done), slice={[64:4096], [0:2], [0:8], [0:128]} | slice | bytes 66060288 | tf_op jit(solution)/shard_map/slice | solution.py:24
  813.7 189.7 %while.56 = (s32[]{:T(128)}, f32[64,2,8]{0,2,1:T(8,128)}, f32[64,2,8]{0,2,1:T(8,128)S(1)}, f32[64,2,8,128]{3,2,1,0:T(8,128)S(1)}, f32[63,64,2,8]{1,3,2,0:T(8,128...) while((s32[]{:T(128)}, f32[64,2,8]{0,2,1:T(8,128)}, ...), condition=%wide.region_15.16_spmd, body=%wide.region_14.15_spmd.sunk | while | flops 399362 | bytes 1630809 | solution.py:25
  1006.3 22.4 %slice.225 = f32[4032,2,8,128]{3,2,0,1:T(8,128)} slice(f32[4096,2,8,128]{3,2,0,1:T(8,128)} %all-gather.22.cloned.1.call-done), slice={[64:4096], [0:2], [0:8], [0:128]} | slice | bytes 66060288 | tf_op jit(solution)/shard_map/slice | solution.py:24
  1028.8 151.2 %while.57 = (s32[]{:T(128)}, f32[64,2,8]{0,2,1:T(8,128)S(1)}, f32[64,2,8]{0,2,1:T(8,128)S(1)}, f32[64,2,8,128]{3,2,1,0:T(8,128)S(1)}, f32[63,64,2,8]{1,3,2,0:T(8...) while((s32[]{:T(128)}, f32[64,2,8]{0,2,1:T(8,128)S(1)}, ...), condition=%wide.region_20.21_spmd, body=%wide.region_19.20_spmd.sunk | while | flops 399362 | bytes 1630809 | solution.py:25
  1183.3 22.3 %slice.234 = f32[4032,2,8,128]{3,2,0,1:T(8,128)} slice(f32[4096,2,8,128]{3,2,0,1:T(8,128)} %all-gather.24.cloned.1.call-done), slice={[64:4096], [0:2], [0:8], [0:128]} | slice | bytes 66060288 | tf_op jit(solution)/shard_map/slice | solution.py:24
  1205.7 152.3 %while.58 = (s32[]{:T(128)}, f32[64,2,8]{0,2,1:T(8,128)S(1)}, f32[64,2,8]{0,2,1:T(8,128)S(1)}, f32[64,2,8,128]{3,2,1,0:T(8,128)S(1)}, f32[63,64,2,8]{1,3,2,0:T(8...) while((s32[]{:T(128)}, f32[64,2,8]{0,2,1:T(8,128)S(1)}, ...), condition=%wide.region_27.28_spmd, body=%wide.region_26.27_spmd.sunk | while | flops 399362 | bytes 1630809 | solution.py:25
  1367.3 22.4 %slice.243 = f32[4032,2,8,128]{3,2,0,1:T(8,128)} slice(f32[4096,2,8,128]{3,2,0,1:T(8,128)} %all-gather.26.cloned.1.call-done), slice={[64:4096], [0:2], [0:8], [0:128]} | slice | bytes 66060288 | tf_op jit(solution)/shard_map/slice | solution.py:24
  1389.7 151.2 %while.59 = (s32[]{:T(128)}, f32[64,2,8]{0,2,1:T(8,128)S(1)}, f32[64,2,8]{0,2,1:T(8,128)S(1)}, f32[64,2,8,128]{3,2,1,0:T(8,128)S(1)}, f32[63,64,2,8]{1,3,2,0:T(8...) while((s32[]{:T(128)}, f32[64,2,8]{0,2,1:T(8,128)S(1)}, ...), condition=%wide.region_34.35_spmd, body=%wide.region_33.34_spmd.sunk | while | flops 399362 | bytes 1630809 | solution.py:25
  1545.9 15.4 reduce-scatter.7.cloned.1.call-done
  1562.0 24.5 %reduce-scatter.9.cloned.1.call-done = f32[16,128]{1,0:T(8,128)} async-done(((f32[64,128]{1,0:T(8,128)}), f32[16,128]{1,0:T(8,128)}) %reduce-scatter.9.cloned.1.call-update) | async-done | bytes 8208 | tf_op jit(solution)/shard_map/reduce_scatter | solution.py:173
  1587.2 24.2 %reduce-scatter.11.cloned.1.call-done = f32[16,128]{1,0:T(8,128)} async-done(((f32[64,128]{1,0:T(8,128)}), f32[16,128]{1,0:T(8,128)}) %reduce-scatter.11.cloned.1.call-update) | async-done | bytes 8208 | tf_op jit(solution)/shard_map/reduce_scatter | solution.py:173
  (1303 shorter events, 728.6 us)
Async XLA Ops:
  7.2 1354.5 %copy-start = (bf16[2048,128]{1,0:T(8,128)(2,1)S(1)}, bf16[2048,128]{1,0:T(8,128)(2,1)}, u32[]{:S(2)}) copy-start(bf16[2048,128]{1,0:T(8,128)(2,1)} %param.31) | copy-start | bytes 1572868
  7.2 8.2 copy-start.62
  7.2 8.2 copy-start.57
  7.2 84.2 %all-gather.18.cloned.1.call-start = ((), (), s32[]{:S(2)}) async-start(), calls=%async_computation.4 | async-start | bytes 1064960 | tf_op jit(solution)/shard_map/all_gather | solution.py:125
  7.9 260.1 %all-reduce.3.cloned.1.call-start = ((), (), s32[]{:S(2)}) async-start(), calls=%async_computation.13 | async-start | bytes 524288 | tf_op jit(solution)/shard_map/psum | solution.py:18
  13.4 776.6 %all-gather.20.cloned.1.call-start = ((), (), s32[]{:S(2)}) async-start(), calls=%async_computation.9 | async-start | bytes 34078720 | tf_op jit(solution)/shard_map/all_gather | solution.py:22
  15.6 87.7 %copy-start.55 = (pred[64,256]{1,0:T(8,128)(4,1)}, pred[64,256]{1,0:T(8,128)(4,1)S(1)}, u32[]{:S(2)}) copy-start(pred[64,256]{1,0:T(8,128)(4,1)S(1)} %broadcast_compare_fusion) | copy-start | bytes 49156
  101.0 904.1 %all-gather.22.cloned.1.call-start = ((), (), s32[]{:S(2)}) async-start(), calls=%async_computation.10 | async-start | bytes 34078720 | tf_op jit(solution)/shard_map/all_gather | solution.py:22
  103.2 1079.0 %all-gather.24.cloned.1.call-start = ((), (), s32[]{:S(2)}) async-start(), calls=%async_computation.11 | async-start | bytes 34078720 | tf_op jit(solution)/shard_map/all_gather | solution.py:22
  104.8 52.3 %copy-start.60 = (bf16[4,1,256]{2,0,1:T(4,128)(2,1)S(1)}, bf16[4,1,256]{2,0,1:T(4,128)(2,1)}, u32[]{:S(2)}) copy-start(bf16[4,1,256]{2,0,1:T(4,128)(2,1)} %param.28) | copy-start | bytes 6148
  106.1 1260.1 %all-gather.26.cloned.1.call-start = ((), (), s32[]{:S(2)}) async-start(), calls=%async_computation.12 | async-start | bytes 34078720 | tf_op jit(solution)/shard_map/all_gather | solution.py:22
  108.0 99.8 %copy-start.10 = (bf16[256,2048]{0,1:T(8,128)(2,1)S(1)}, bf16[256,2048]{0,1:T(8,128)(2,1)}, u32[]{:S(2)}) copy-start(bf16[256,2048]{0,1:T(8,128)(2,1)} %copy.424) | copy-start | bytes 3145732
  157.1 617.3 %copy-start.15 = (bf16[4,64,256]{2,0,1:T(4,128)(2,1)}, bf16[4,64,256]{2,0,1:T(4,128)(2,1)S(1)}, u32[]{:S(2)}) copy-start(bf16[4,64,256]{2,0,1:T(4,128)(2,1)S(1)} %all_gather.88) | copy-start | bytes 393220
  761.2 7.0 copy-start.35
  789.8 755.4 %reduce-scatter.5.cloned.1.call-start = ((), (), s32[]{:S(2)}) async-start(), calls=%async_computation.5 | async-start | bytes 40960 | tf_op jit(solution)/shard_map/reduce_scatter | solution.py:173
  813.7 189.7 %copy-start.48 = (f32[64,2,1,8]{0,3,1,2:T(8,128)S(1)}, f32[64,2,1,8]{0,3,1,2:T(8,128)}, u32[]{:S(2)}) copy-start(f32[64,2,1,8]{0,3,1,2:T(8,128)} %copy.522) | copy-start | bytes 12292
  1006.3 22.4 %copy-start.18 = (f32[64,2,8]{0,2,1:T(8,128)S(1)}, f32[64,2,8]{0,2,1:T(8,128)}, u32[]{:S(2)}) copy-start(f32[64,2,8]{0,2,1:T(8,128)} %copy.463) | copy-start | bytes 12292
  1006.3 22.4 %copy-start.19 = (f32[64,2,8]{0,2,1:T(8,128)S(1)}, f32[64,2,8]{0,2,1:T(8,128)}, u32[]{:S(2)}) copy-start(f32[64,2,8]{0,2,1:T(8,128)} %copy.462) | copy-start | bytes 12292
  1028.7 151.2 %copy-start.46 = (f32[64,2,8]{0,2,1:T(8,128)S(1)}, f32[64,2,8]{0,2,1:T(8,128)}, u32[]{:S(2)}) copy-start(f32[64,2,8]{0,2,1:T(8,128)} %copy.468) | copy-start | bytes 12292
  1028.7 151.2 %copy-start.47 = (f32[64,2,8]{0,2,1:T(8,128)S(1)}, f32[64,2,8]{0,2,1:T(8,128)}, u32[]{:S(2)}) copy-start(f32[64,2,8]{0,2,1:T(8,128)} %copy.472) | copy-start | bytes 12292
  1183.3 22.3 %copy-start.17 = (f32[64,2,8]{0,2,1:T(8,128)S(1)}, f32[64,2,8]{0,2,1:T(8,128)}, u32[]{:S(2)}) copy-start(f32[64,2,8]{0,2,1:T(8,128)} %copy.482) | copy-start | bytes 12292
  1205.6 152.4 %copy-start.44 = (f32[64,2,8]{0,2,1:T(8,128)S(1)}, f32[64,2,8]{0,2,1:T(8,128)}, u32[]{:S(2)}) copy-start(f32[64,2,8]{0,2,1:T(8,128)} %copy.488) | copy-start | bytes 12292
  1205.7 152.4 %copy-start.45 = (f32[64,2,8]{0,2,1:T(8,128)S(1)}, f32[64,2,8]{0,2,1:T(8,128)}, u32[]{:S(2)}) copy-start(f32[64,2,8]{0,2,1:T(8,128)} %copy.492) | copy-start | bytes 12292
  1205.7 154.6 %copy-start.22 = (f32[1,64,256]{2,0,1:T(1,128)S(1)}, f32[1,64,256]{2,0,1:T(1,128)}, u32[]{:S(2)}) copy-start(f32[1,64,256]{2,0,1:T(1,128)} %slice_convert_fusion) | copy-start | bytes 196612
  1366.1 195.2 %reduce-scatter.7.cloned.1.call-start = ((), (), s32[]{:S(2)}) async-start(), calls=%async_computation.6 | async-start | bytes 40960 | tf_op jit(solution)/shard_map/reduce_scatter | solution.py:173
  1389.7 151.3 %copy-start.24 = (f32[64,2,8,3]{2,3,1,0:T(4,128)S(1)}, f32[64,2,8,3]{2,3,1,0:T(4,128)}, u32[]{:S(2)}) copy-start(f32[64,2,8,3]{2,3,1,0:T(4,128)} %copy-done.23) | copy-start | bytes 36868
  1389.7 151.3 %copy-start.32 = (f32[64,2,8]{2,1,0:T(2,128)S(1)}, f32[64,2,8]{2,1,0:T(2,128)}, u32[]{:S(2)}) copy-start(f32[64,2,8]{2,1,0:T(2,128)} %copy-done.31) | copy-start | bytes 12292
  1389.7 151.3 %copy-start.36 = (f32[64,2,8]{2,1,0:T(2,128)S(1)}, f32[64,2,8]{2,1,0:T(2,128)}, u32[]{:S(2)}) copy-start(f32[64,2,8]{2,1,0:T(2,128)} %copy.489) | copy-start | bytes 12292
  1389.7 151.3 %copy-start.37 = (f32[64,2,8]{2,1,0:T(2,128)S(1)}, f32[64,2,8]{2,1,0:T(2,128)}, u32[]{:S(2)}) copy-start(f32[64,2,8]{2,1,0:T(2,128)} %copy.491) | copy-start | bytes 12292
  1389.7 151.3 %copy-start.38 = (f32[64,2,8]{2,1,0:T(2,128)S(1)}, f32[64,2,8]{2,1,0:T(2,128)}, u32[]{:S(2)}) copy-start(f32[64,2,8]{2,1,0:T(2,128)} %copy.493) | copy-start | bytes 12292
  1542.7 43.8 %reduce-scatter.9.cloned.1.call-start = ((), (), s32[]{:S(2)}) async-start(), calls=%async_computation.7 | async-start | bytes 40960 | tf_op jit(solution)/shard_map/reduce_scatter | solution.py:173
  1543.4 68.0 %reduce-scatter.11.cloned.1.call-start = ((), (), s32[]{:S(2)}) async-start(), calls=%async_computation.8 | async-start | bytes 40960 | tf_op jit(solution)/shard_map/reduce_scatter | solution.py:173
  (50 other events, 164.5 us)
Sparse Core Ops, SparseCore 0:
  10.8 80.5 all-gather.17
  95.0 173.0 all-reduce.2
  271.3 160.1 all-gather.19
  434.5 155.8 all-gather.21
  593.5 159.6 all-gather.23
  789.9 140.5 all-gather.25
  1366.2 18.4 reduce-scatter.4
  1542.8 18.4 reduce-scatter.6
  1564.0 22.4 reduce-scatter.8
  1588.8 22.5 reduce-scatter.10
where the time goes:
time: 1650 us; the launch traced here: 1620 us
  other arithmetic  597 us (36%)
  blocking collectives  530 us (32%)
  local copies, waits for them, and re-layouts  243 us (15%)
  waiting for transfers between devices  199 us (12%)
  matrix products  24.5 us (1%)
  between operations  16.8 us (1%)
    all_gather x8, blocking collectives, joined(): pieces = jax.tree.map(lambda part: lax.all_gather(part, axis), value)  434 us
    add x252, other arithmetic, combine(): first[2] * first_factor[..., None] + second[2] * second_factor[..., None]  365 us
    add x255, other arithmetic, combine(): first[1] * first_factor + second[1] * second_factor  219 us
    slice x12, local copies, waits for them, and re-layouts, joined(): tail = jax.tree.map(lambda part: part[1:], pieces)  116 us
    all_gather x1, waiting for transfers between devices, on_device(): lax.all_gather(dec_queries, 'ctx', axis=1, tiled=True)  75.8 us
    reduce_scatter x4, waiting for transfers between devices, on_device(): lax.psum_scatter(project(jnp.int32(0), lax.axis_size('tp') * tp_rows), 't...  64.1 us
    psum x1, waiting for transfers between devices, spread(): return lax.psum(jnp.where(mine, x, jnp.zeros_like(x)), axis)  57.8 us
    all_gather x1, blocking collectives, on_device(): lax.all_gather(new_keys, 'ctx', axis=1, tiled=True)  48.3 us
  transfers between devices with their start and end apart: 10, of which 5 were waited for; matrix products, arithmetic and copies ran while one was open for 53% of the time, Pallas kernels for 0%

commit v1 on v0

v1 whole, which is shorter than its diff:
```python
import functools
import math

import jax
import jax.numpy as jnp
from jax import lax
from jax.experimental import pallas as pl
from jax.experimental.pallas import tpu as pltpu
from jax.sharding import Mesh, PartitionSpec as P

HD = 128
STEPS = 4
NZ, NY, NC, NX = 8, 4, 2, 4
ROWS = 256
SLOTS = 64
SCALE2 = math.log2(math.e) / math.sqrt(HD)
LOW = -1e29
FLOOR = -1e28
F32 = jnp.float32
BF16 = jnp.bfloat16
VMEM = pl.BlockSpec(memory_space=pltpu.VMEM)
SMEM = pl.BlockSpec(memory_space=pltpu.SMEM)
NT = (((1,), (1,)), ((), ()))
NN = (((1,), (0,)), ((), ()))


def iota(shape, dim):
    return lax.broadcasted_iota(jnp.int32, shape, dim)


def dot(a, b, dims=NN):
    return lax.dot_general(a, b, dims, preferred_element_type=F32)


def params(mib=20):
    return pltpu.CompilerParams(vmem_limit_bytes=mib * 2**20)


def cost(flops, moved, trans=0):
    return pl.CostEstimate(flops=flops, bytes_accessed=moved, transcendentals=trans)


def prep_kernel(dq, nk, nv, ck, cv, xk, xv, q_out, p0, p1, p2, p3, scratch, dq_v, nk_v, nv_v, xk_v, xv_v, sems):
    y = lax.axis_index("y")
    copies = [
        (dq, dq_v),
        (nk, nk_v),
        (nv, nv_v),
        (ck, p0.at[0:ROWS, :]),
        (cv, p0.at[ROWS : 2 * ROWS, :]),
        (xk, xk_v),
        (xv, xv_v),
    ]
    copies = [pltpu.make_async_copy(src, dst, sems.at[i]) for i, (src, dst) in enumerate(copies)]
    for copy in copies:
        copy.start()
    scratch[...] = jnp.zeros_like(scratch)
    row, col = iota((80, 160), 0), iota((80, 160), 1)
    pick = (col == (row // 4) * 8 + row % 4).astype(F32).astype(BF16)
    for copy in copies[:3]:
        copy.wait()
    for h in range(16):
        scratch[h * 8 : h * 8 + 4, :] = dq_v[:, h * HD : (h + 1) * HD].astype(F32)
    for i, ref in enumerate((nk_v, nv_v)):
        for k in range(2):
            at = 128 + (i * 2 + k) * 8
            scratch[at : at + 4, :] = ref[:, k * HD : (k + 1) * HD].astype(F32)
    packed = dot(pick, scratch[...].astype(BF16)).astype(BF16)
    for s in range(NZ):
        q_out[s] = packed
    for copy in copies[3:]:
        copy.wait()
    shard = p0[0 : 2 * ROWS, :]
    for out in (p1, p2, p3):
        out[0 : 2 * ROWS, :] = shard
    for s, out in enumerate((p0, p1, p2, p3)):
        for i in range(8):
            source, k = (xk_v, xv_v)[i // 4], (i % 4) // 2
            for core in range(2):
                at = lax.rem(y + s, NY) * 64 + core * 32 + (i % 2) * 16
                tile = source[pl.ds(pl.multiple_of(at, 16), 16), k * HD : (k + 1) * HD]
                out[512 + i * 16 : 528 + i * 16, core * HD : (core + 1) * HD] = tile


def prep(*args):
    args = [pltpu.with_memory_space_constraint(a, pltpu.HBM) for a in args]
    payload = jax.ShapeDtypeStruct((640, 256), BF16)
    return pl.pallas_call(
        prep_kernel,
        out_shape=(jax.ShapeDtypeStruct((NZ, 80, HD), BF16),) + (payload,) * 4,
        in_specs=[pl.BlockSpec(memory_space=pltpu.HBM)] * 7,
        out_specs=(VMEM,) * 5,
        scratch_shapes=[
            pltpu.VMEM((160, HD), F32),
            pltpu.VMEM((STEPS, 2048), BF16),
            pltpu.VMEM((STEPS, 256), BF16),
            pltpu.VMEM((STEPS, 256), BF16),
            pltpu.VMEM((ROWS, 256), BF16),
            pltpu.VMEM((ROWS, 256), BF16),
            pltpu.SemaphoreType.DMA((7,)),
        ],
        compiler_params=params(),
        cost_estimate=cost(1 << 20, 1 << 20),
        name="prep",
    )(*args)


def line_kernel(g, owner, lengths, blocks, q_out, ro_out, rm_out, rl_out, meta):
    z, y, c = lax.axis_index("z"), lax.axis_index("y"), lax.axis_index("c")
    line = y * NC + c
    for s in range(8):
        meta[s] = 0

    def scan_slots(r, root):
        slot = owner[r]

        @pl.when(lax.rem(slot, 8) == line)
        def _():
            meta[slot // 8] = lengths[r]

        return jnp.where(blocks[r] == 0, r, root)

    root = lax.fori_loop(0, SLOTS, scan_slots, jnp.int32(0))
    meta[8] = root // 8
    meta[9] = lax.rem(root, 8) // 2
    meta[10] = lax.rem(root, 2)

    row, col = iota((256, 256), 0), iota((256, 256), 1)
    source = lax.rem(row // 4, 8) * 32 + (row // 32) * 4 + lax.rem(row, 4)
    pick = (col == source).astype(F32).astype(BF16)
    for k in range(2):
        natural = jnp.concatenate([g[s, k * 32 : (k + 1) * 32, :] for s in range(NZ)], axis=0)
        q_out[k * 256 : (k + 1) * 256, :] = dot(pick, natural).astype(BF16)
    mine = q_out[pl.ds(pl.multiple_of(z * 64, 64), 64), :]
    tokens = jnp.concatenate([g[s, 64:80, :] for s in range(NZ)], axis=0)
    wide = tokens.astype(F32)
    values = jnp.concatenate([wide[8:], wide[:8]], axis=0).astype(BF16)
    scores = dot(mine, tokens, NT) * SCALE2
    row, col = iota((64, 128), 0), iota((64, 128), 1)
    seen = (
        (lax.rem(row // 4, 8) == col // 16)
        & (lax.rem(col, 16) // 4 == z // 4)
        & (lax.rem(col, 4) <= lax.rem(row, 4))
    )
    scores = jnp.where(seen, scores, LOW)
    top = jnp.max(scores, axis=1, keepdims=True)
    weights = jnp.exp2(scores - top)
    rm_out[...] = jnp.broadcast_to(top, (64, HD))
    rl_out[...] = jnp.broadcast_to(jnp.sum(weights, axis=1, keepdims=True), (64, HD))
    ro_out[...] = dot(weights.astype(BF16), values)


def line_part(gathered, owner, lengths, blocks):
    part = jax.ShapeDtypeStruct((64, HD), F32)
    return pl.pallas_call(
        line_kernel,
        out_shape=(
            jax.ShapeDtypeStruct((512, HD), BF16),
            part,
            part,
            part,
            jax.ShapeDtypeStruct((16,), jnp.int32),
        ),
        in_specs=[VMEM, SMEM, SMEM, SMEM],
        out_specs=(VMEM, VMEM, VMEM, VMEM, SMEM),
        compiler_params=params(),
        cost_estimate=cost(1 << 24, 1 << 20),
        name="line_part",
    )(gathered, owner, lengths, blocks)


def shard_kernel(meta, q, *refs):
    bufs, out, scores = refs[:8], refs[8], refs[9]
    z, y, c = lax.axis_index("z"), lax.axis_index("y"), lax.axis_index("c")
    rowslot = iota((32, HD), 0) // 4
    length = jnp.zeros((32, HD), jnp.int32)
    for s in range(8):
        length = jnp.where(rowslot == s, meta[s], length)
    lane = iota((32, HD), 1)
    for k in range(2):
        qk = q[k * 256 : (k + 1) * 256, :]
        tops = []
        for b in range(8):
            shift, swap = b % 4, b // 4
            shard = z * 8 + lax.rem(y - shift + NY, NY) * NC + (c if swap == 0 else 1 - c)
            room = length - shard * ROWS
            keep = jnp.concatenate([lane < room, lane + HD < room], axis=1)
            raw = dot(qk, bufs[b][0:ROWS, k * HD : (k + 1) * HD], NT)
            raw = jnp.where(keep[None], raw.reshape(8, 32, 256), LOW).reshape(256, 256)
            scores[b] = raw
            tops.append(
                jnp.max(jnp.maximum(raw[:, :HD], raw[:, HD:]), axis=1, keepdims=True)
            )
        top = functools.reduce(jnp.maximum, tops) * SCALE2
        top = top.astype(BF16).astype(F32)
        total = jnp.zeros((256, HD), F32)
        weighted = jnp.zeros((256, HD), F32)
        for b in range(8):
            weights = jnp.exp2((scores[b] - jnp.maximum(tops[b], FLOOR)) * SCALE2)
            factor = jnp.exp2(jnp.minimum(tops[b] * SCALE2 - top, 64.0))
            total = total + (weights[:, :HD] + weights[:, HD:]) * factor
            weighted = weighted + factor * dot(
                weights.astype(BF16), bufs[b][ROWS : 2 * ROWS, k * HD : (k + 1) * HD]
            )
        total = jnp.sum(total, axis=1, keepdims=True)
        total_high = total.astype(BF16).astype(F32)
        total_low = total - total_high
        column = iota((256, HD), 1)
        stats = jnp.where(
            column == 0, top, jnp.where(column == 1, total_high, jnp.where(column == 2, total_low, 0.0))
        )
        weighted = weighted.astype(BF16)
        for pair in range(2):
            flipped = jnp.transpose(stats[pair * 128 : (pair + 1) * 128])[:16].astype(BF16)
            out[k * 4 + pair * 2, 64:80, :] = flipped
            out[k * 4 + pair * 2 + 1, 64:80, :] = flipped
        for part in range(4):
            out[k * 4 + part, 0:64, :] = weighted[part * 64 : (part + 1) * 64]
    root_shift = lax.rem(y - meta[9] + NY, NY)
    root_swap = jnp.where(meta[10] == c, 0, 1)
    for b in range(8):
        for core in range(2):

            @pl.when((root_shift == b % 4) & (root_swap == b // 4) & (c == core))
            def _(b=b, core=core):
                for piece in range(NZ):
                    out[piece, 80:96, :] = bufs[b][
                        512 + piece * 16 : 528 + piece * 16, core * HD : (core + 1) * HD
                    ]


def shard_part(meta, q, bufs):
    return pl.pallas_call(
        shard_kernel,
        out_shape=jax.ShapeDtypeStruct((NZ, 96, HD), BF16),
        in_specs=[SMEM] + [VMEM] * 9,
        out_specs=VMEM,
        scratch_shapes=[pltpu.VMEM((8, 256, 256), F32)],
        compiler_params=params(),
        cost_estimate=cost(1 << 30, 4 << 20, 1 << 20),
        name="shard_part",
    )(meta, q, *bufs)


def merge_kernel(meta, parts, ro, rm, rl, out, scratch):
    z = lax.axis_index("z")
    stats = jnp.concatenate([parts[j, 64:80, :] for j in range(NZ)], axis=0).astype(F32)
    scratch[...] = jnp.transpose(stats)
    mine = scratch[pl.ds(pl.multiple_of(lax.rem(z, 2) * 64, 64), 64), :]
    tops = [mine[:, j * 16 : j * 16 + 1] for j in range(NZ)]
    totals = [mine[:, j * 16 + 1 : j * 16 + 2] + mine[:, j * 16 + 2 : j * 16 + 3] for j in range(NZ)]
    top = rm[...]
    for t in tops:
        top = jnp.maximum(top, t)
    factor = jnp.exp2(rm[...] - top)
    total = rl[...] * factor
    weighted = ro[...] * factor
    for j in range(NZ):
        factor = jnp.exp2(tops[j] - top)
        total = total + totals[j] * factor
        weighted = weighted + parts[j, 0:64, :].astype(F32) * factor
    attention = (weighted / total).astype(BF16)
    anchor = parts[meta[8], 80:96, :]
    for s in range(NZ):
        out[s, 0:64, :] = attention
        out[s, 64:80, :] = anchor


def merge(meta, parts, ro, rm, rl):
    return pl.pallas_call(
        merge_kernel,
        out_shape=jax.ShapeDtypeStruct((NZ, 80, HD), BF16),
        in_specs=[SMEM] + [VMEM] * 4,
        out_specs=VMEM,
        scratch_shapes=[pltpu.VMEM((HD, HD), F32)],
        compiler_params=params(),
        cost_estimate=cost(1 << 20, 1 << 19),
        name="merge",
    )(meta, parts, ro, rm, rl)


def project_kernel(owner, w, *refs):
    bufs, outs = refs[:8], refs[8:12]
    y, c, x = lax.axis_index("y"), lax.axis_index("c"), lax.axis_index("x")
    total = jnp.zeros((256, HD), F32)
    for zz in range(NZ):
        left = jnp.concatenate([b[zz, 0:32, :] for b in bufs], axis=0)
        right = jnp.concatenate([b[zz, 32:64, :] for b in bufs], axis=0)
        total = total + dot(
            jnp.concatenate([left, right], axis=1), w[zz * 256 : (zz + 1) * 256, :]
        )
    high = total.astype(BF16)
    low = (total - high.astype(F32)).astype(BF16)
    col = iota((64, 256), 1)
    buf = col // 32
    slot = (
        lax.rem(col // 4, 8) * 8
        + lax.rem(y - lax.rem(buf, 4) + NY, NY) * NC
        + jnp.where(buf >= 4, 1 - c, c)
    )
    row = iota((64, 256), 0)
    same_step = lax.rem(col, 4) == row // 16
    request = lax.rem(row, 16)
    for s, out in enumerate(outs):
        first = lax.rem(x + s, NX) * 16
        wanted = jnp.zeros((64, 256), jnp.int32)
        for j in range(16):
            wanted = jnp.where(request == j, owner[first + j], wanted)
        pick = ((wanted == slot) & same_step).astype(F32).astype(BF16)
        out[...] = dot(pick, high) + dot(pick, low)


def project(owner, w, bufs):
    return pl.pallas_call(
        project_kernel,
        out_shape=(jax.ShapeDtypeStruct((64, HD), F32),) * 4,
        in_specs=[SMEM] + [VMEM] * 9,
        out_specs=(VMEM,) * 4,
        compiler_params=params(),
        cost_estimate=cost(1 << 28, 2 << 20),
        name="project",
    )(owner, w, *bufs)


def own_kernel(q, xk, xv, out, lse, values):
    for k in range(2):
        values[k, :, 0:HD] = xv[:, k * HD : (k + 1) * HD]
        values[k, :, HD:] = jnp.ones((ROWS, HD), BF16)
    causal = iota((128, 128), 0) >= iota((128, 128), 1)
    for group in range(4):
        units = [(group * 4 + h, half) for h in range(4) for half in range(2)]
        tiles, tops = [], []
        for h, half in units:
            near = (half + 1) * 128
            keys = xk[0:near, (h // 8) * HD : (h // 8 + 1) * HD]
            own = dot(q[near - 128 : near, h * HD : (h + 1) * HD], keys, NT)
            diagonal = jnp.where(causal, own[:, near - 128 :], LOW)
            tiles.append([own[:, :HD], diagonal] if half else [diagonal])
        for parts in tiles:
            tops.append(
                jnp.max(functools.reduce(jnp.maximum, parts), axis=1, keepdims=True) * SCALE2
            )
        for (h, half), parts, top in zip(units, tiles, tops):
            near = (half + 1) * 128
            weights = [jnp.exp2(t * SCALE2 - top).astype(BF16) for t in parts]
            weights = jnp.concatenate(weights, axis=1) if half else weights[0]
            summed = dot(weights, values[h // 8, 0:near, :])
            rows, lanes = slice(near - 128, near), slice(h * HD, (h + 1) * HD)
            out[rows, lanes] = summed[:, :HD] / summed[:, HD:]
            lse[rows, lanes] = top + jnp.log2(summed[:, HD:])


def context_own(q, xk, xv):
    whole = jax.ShapeDtypeStruct((ROWS, 2048), F32)
    return pl.pallas_call(
        own_kernel,
        out_shape=(whole, whole),
        in_specs=[VMEM] * 3,
        out_specs=(VMEM, VMEM),
        scratch_shapes=[pltpu.VMEM((2, ROWS, 2 * HD), BF16)],
        compiler_params=params(),
        cost_estimate=cost(1 << 30, 6 << 20, 1 << 20),
        name="context_own",
    )(q, xk, xv)


def far_kernel(blocks, q, own, lse, *refs):
    bufs, (out, keys, values, staged, sems) = refs[:8], refs[8:]
    index = (lax.axis_index("z") * NY + lax.axis_index("y")) * NC + lax.axis_index("c")
    hide = jnp.where(blocks[index] == 0, LOW, 0.0).astype(F32)
    for k in range(2):
        values[k, :, HD:] = jnp.ones((ROWS, HD), BF16)
        for j, buf in enumerate(bufs):
            for half in range(2):
                at, tile = j * 32 + half * 16, k * 2 + half
                keys[k, at : at + 16, :] = buf[tile, 64:80, :]
                values[k, at : at + 16, 0:HD] = buf[4 + tile, 64:80, :]
    copies = []
    for group in range(4):
        units = [(group * 4 + h, half) for h in range(4) for half in range(2)]
        tiles = []
        for h, half in units:
            queries = q[half * 128 : (half + 1) * 128, h * HD : (h + 1) * HD]
            far = dot(queries, keys[h // 8], NT) + hide
            tiles.append([far[:, :HD], far[:, HD:]])
        tops = [jnp.max(jnp.maximum(*t), axis=1, keepdims=True) * SCALE2 for t in tiles]
        for (h, half), parts, top in zip(units, tiles, tops):
            rows, lanes = slice(half * 128, (half + 1) * 128), slice(h * HD, (h + 1) * HD)
            near = lse[rows, lanes]
            top = jnp.maximum(top, near)
            weights = [jnp.exp2(t * SCALE2 - top).astype(BF16) for t in parts]
            summed = dot(jnp.concatenate(weights, axis=1), values[h // 8])
            factor = jnp.exp2(near - top)
            joint = summed[:, :HD] + factor * own[rows, lanes]
            staged[rows, lanes] = (joint / (summed[:, HD:] + factor)).astype(BF16)
        lanes = slice(group * 512, (group + 1) * 512)
        copies.append(pltpu.make_async_copy(staged.at[:, lanes], out.at[:, lanes], sems.at[group]))
        copies[-1].start()
    for copy in copies:
        copy.wait()


def context_far(blocks, q, own, lse, bufs):
    return pl.pallas_call(
        far_kernel,
        out_shape=jax.ShapeDtypeStruct((ROWS, 2048), BF16),
        in_specs=[SMEM] + [VMEM] * 11,
        out_specs=pl.BlockSpec(memory_space=pl.ANY),
        scratch_shapes=[
            pltpu.VMEM((2, ROWS, HD), BF16),
            pltpu.VMEM((2, ROWS, 2 * HD), BF16),
            pltpu.VMEM((ROWS, 2048), BF16),
            pltpu.SemaphoreType.DMA((4,)),
        ],
        compiler_params=params(),
        cost_estimate=cost(1 << 30, 6 << 20, 1 << 20),
        name="context_far",
    )(blocks, q, own, lse, *bufs)


def shifted(value, axis, size, shift):
    return lax.ppermute(value, axis, [(i, (i + shift) % size) for i in range(size)])


def on_device(
    ctx_queries,
    ctx_keys,
    ctx_values,
    block_map,
    cache_keys,
    cache_values,
    dec_queries,
    new_keys,
    new_values,
    cache_lengths,
    owner,
    out_weight,
):
    packed, *payloads = prep(
        dec_queries.reshape(STEPS, -1),
        new_keys.reshape(STEPS, -1),
        new_values.reshape(STEPS, -1),
        cache_keys,
        cache_values,
        ctx_keys,
        ctx_values,
    )
    shards = [shifted(payloads[s], "y", NY, s) for s in range(1, NY)]
    gathered = lax.all_to_all(packed, "z", 0, 0, tiled=True)
    own, lse = context_own(ctx_queries, ctx_keys, ctx_values)
    gathered, own, lse, *shards = lax.optimization_barrier((gathered, own, lse, *shards))
    shards = [payloads[0]] + shards
    shards = shards + [shifted(b, "c", NC, 1) for b in shards]
    q, ro, rm, rl, meta = line_part(gathered, owner, cache_lengths, block_map)
    parts = lax.all_to_all(shard_part(meta, q, shards), "z", 0, 0, tiled=True)
    merged = lax.all_to_all(merge(meta, parts, ro, rm, rl), "z", 0, 0, tiled=True)
    lines = [merged] + [shifted(merged, "y", NY, s) for s in range(1, NY)]
    everything = lines + [shifted(b, "c", NC, 1) for b in lines]
    ctx_out = context_far(block_map, ctx_queries, own, lse, everything)
    mine, *others = project(owner, out_weight, everything)
    total = mine
    for s, part in enumerate(others):
        total = total + shifted(part, "x", NX, s + 1)
    dec_out = total.astype(BF16).reshape(STEPS, 16, HD)
    return (ctx_out, dec_out)


def solution(mesh):
    grid = Mesh(mesh.devices.reshape(NZ, NY, NC, NX), ("z", "y", "c", "x"))
    ctx = ("z", "y", "c")
    in_specs = (
        P(ctx, "x"),
        P(ctx, "x"),
        P(ctx, "x"),
        P(),
        P(ctx, "x"),
        P(ctx, "x"),
        P(None, ctx, "x"),
        P(None, ctx, "x"),
        P(None, ctx, "x"),
        P(),
        P(),
        P("x", ctx),
    )
    out_specs = (P(ctx, "x"), P(None, "x", ctx))
    return jax.shard_map(on_device, mesh=grid, in_specs=in_specs, out_specs=out_specs, check_vma=False)
```

time: 1650 us -> 86.6 us (0.05); the launches traced: 1620 us -> 86.3 us
  other arithmetic: 597 us -> 0.62 us
  blocking collectives: 530 us -> 23.8 us
  local copies, waits for them, and re-layouts: 243 us -> 4.41 us
  waiting for transfers between devices: 199 us -> 1.56 us
  starting transfers between devices: 0.58 us -> 39.1 us
  matrix products: 24.5 us -> 0 us
    add x510 -> x0, other arithmetic: 584 us -> none  [the longest x252 365 us: combine(): first[2] * first_factor[..., None] + second[2] * second_factor[..., None]]
    all_gather x10 -> x0, blocking collectives: 530 us -> none  [the longest x8 434 us: joined(): pieces = jax.tree.map(lambda part: lax.all_gather(part, axis), value)]
    slice x33 -> x0, local copies, waits for them, and re-layouts: 127 us -> none  [the longest x12 116 us: joined(): tail = jax.tree.map(lambda part: part[1:], pieces)]
    all_gather x5 -> x0, waiting for transfers between devices: 75.9 us -> none  [the longest x1 75.8 us: on_device(): lax.all_gather(dec_queries, 'ctx', axis=1, tiled=True)]
    reduce_scatter x4 -> x0, waiting for transfers between devices: 64.1 us -> none  [on_device(): lax.psum_scatter(project(jnp.int32(0), lax.axis_size('tp') * tp_rows), 't...]
    psum x1 -> x0, waiting for transfers between devices: 57.8 us -> none  [spread(): return lax.psum(jnp.where(mine, x, jnp.zeros_like(x)), axis)]
    exp x512 -> x0, local copies, waits for them, and re-layouts: 55.1 us -> none  [the longest x256 28.1 us: combine(): first_factor = jnp.exp(first[0] - highest)]
    while x20 -> x0, local copies, waits for them, and re-layouts: 43.5 us -> none  [joined(): lax.scan(lambda total, slab: (join(total, slab), None), head, tail)]
  transfers between devices with their start and end apart: 10 -> 18, of which waited for: 5 -> 3; matrix products, arithmetic and copies ran while one was open for 53% -> 0% of each run, Pallas kernels for 0% -> 9%
where the time goes in v1:
time: 86.6 us; the launch traced here: 86.3 us
  starting transfers between devices  39.1 us (45%)
  blocking collectives  23.8 us (27%)
  Pallas kernels  15.9 us (18%)
  local copies, waits for them, and re-layouts  4.41 us (5%)
  waiting for transfers between devices  1.56 us (2%)
    ppermute x17, starting transfers between devices, shifted(): lax.ppermute(value, axis, [(i, (i + shift) % size) for i in range(size)])  30.8 us
    all_to_all x1, blocking collectives, on_device(): parts = lax.all_to_all(shard_part(meta, q, shards), 'z', 0, 0, tiled=True)  13 us
    all_to_all x1, blocking collectives, on_device(): lax.all_to_all(merge(meta, parts, ro, rm, rl), 'z', 0, 0, tiled=True)  10.8 us
    all_to_all x1, starting transfers between devices, on_device(): gathered = lax.all_to_all(packed, 'z', 0, 0, tiled=True)  8.32 us
    unnamed x20, local copies, waits for them, and re-layouts  4.41 us
    pallas_call x1, Pallas kernels, shard_part(): pl.pallas_call(shard_kernel, out_shape=jax.ShapeDtypeStruct((NZ, 96, HD),...  3.66 us
    pallas_call x1, Pallas kernels, context_far(): pl.pallas_call(far_kernel, out_shape=jax.ShapeDtypeStruct((ROWS, 2048), B...  3.58 us
    pallas_call x1, Pallas kernels, line_part(): pl.pallas_call(line_kernel, out_shape=(jax.ShapeDtypeStruct((512, HD), BF...  2.59 us
  transfers between devices with their start and end apart: 18, of which 3 were waited for; matrix products, arithmetic and copies ran while one was open for 0% of the time, Pallas kernels for 9%

profile of v1, /device:TPU:1, one launch (start us, length us, event | category | flops | bytes accessed | tf_op | source)
XLA Modules:
  0.0 86.3 jit_solution(2146113621695889679)
XLA Ops:
  0.6 2.3 %prep.1 = (bf16[8,80,128]{2,1,0:T(8,128)(2,1)}, bf16[640,256]{1,0:T(8,128)(2,1)S(1)}, bf16[640,256]{1,0:T(8,128)(2,1)}, bf16[640,256]{1,0:T(8,128)(2,1)}, bf16[640,256]{1,0:T(8,128)(2,1)}) custom-call(bf16[4,2048]{1,0:T(4,128)(2,1)} %bitcast.4, bf16[4,256]{1,0:T(4,128)(2,1)} %bitcast.6, bf16[4,256]{1,0:T(4,128)(2,1)} %bitcast.7, bf16[256,256]{1,0:T(8,128)(2,1)} %ck.1, ...), custom_call_target="tpu_custom_call" | custom-call | flops 1048576 | bytes 1048576 | tf_op jit(solution)/shard_map/prep/pallas_call | solution.py:88
  2.9 2.2 %collective-permute-start = (bf16[640,256]{1,0:T(8,128)(2,1)}, bf16[640,256]{1,0:T(8,128)(2,1)S(1)}, u32[]{:S(2)}, u32[]{:S(2)}) collective-permute-start(bf16[640,256]{1,0:T(8,128)(2,1)} %get-tuple-element.27), channel_id=1, source_target_pairs={{0,8},{8,16},{16,24},{24,0},{1,9},{9,17},{17,25},{25,1},{2,10},{10... | collective-permute-start | bytes 983048 | tf_op jit(solution)/shard_map/ppermute | solution.py:422
  5.1 2.6 %collective-permute-start.1 = (bf16[640,256]{1,0:T(8,128)(2,1)}, bf16[640,256]{1,0:T(8,128)(2,1)S(1)}, u32[]{:S(2)}, u32[]{:S(2)}) collective-permute-start(bf16[640,256]{1,0:T(8,128)(2,1)} %get-tuple-element.28), channel_id=1, source_target_pairs={{0,16},{8,24},{16,0},{24,8},{1,17},{9,25},{17,1},{25,9},{2,18},{10... | collective-permute-start | bytes 983048 | tf_op jit(solution)/shard_map/ppermute | solution.py:422
  7.7 1.1 %collective-permute-start.2 = (bf16[640,256]{1,0:T(8,128)(2,1)}, bf16[640,256]{1,0:T(8,128)(2,1)}, u32[]{:S(2)}, u32[]{:S(2)}) collective-permute-start(bf16[640,256]{1,0:T(8,128)(2,1)} %get-tuple-element.29), channel_id=1, source_target_pairs={{0,24},{8,0},{16,8},{24,16},{1,25},{9,1},{17,9},{25,17},{2,26},{10... | collective-permute-start | bytes 983048 | tf_op jit(solution)/shard_map/ppermute | solution.py:422
  8.8 8.3 %all-to-all-start = ((bf16[8,80,128]{2,1,0:T(8,128)(2,1)}), bf16[8,80,128]{2,1,0:T(8,128)(2,1)S(1)}, u32[]{:S(2)}, u32[]{:S(2)}) async-start(bf16[8,80,128]{2,1,0:T(8,128)(2,1)} %get-tuple-element.24), calls=%async_computation | async-start | bytes 327680 | tf_op jit(solution)/shard_map/all_to_all | solution.py:449
  17.1 1.8 %collective-permute-start.3 = (bf16[640,256]{1,0:T(8,128)(2,1)S(1)}, bf16[640,256]{1,0:T(8,128)(2,1)}, u32[]{:S(2)}, u32[]{:S(2)}) collective-permute-start(bf16[640,256]{1,0:T(8,128)(2,1)S(1)} %get-tuple-element.35.refs_0_), channel_id=1, source_target_pairs={{0,4},{4,0},{1,5},{5,1},{2,6},{6,2},{3,7},{7,3},{8,12},{12,8},{9,1... | collective-permute-start | bytes 983048 | tf_op jit(solution)/shard_map/ppermute | solution.py:422
  18.9 1.2 %copy-done.2 = bf16[256,2048]{1,0:T(8,128)(2,1)S(1)} copy-done((bf16[256,2048]{1,0:T(8,128)(2,1)S(1)}, bf16[256,2048]{1,0:T(8,128)(2,1)}, u32[]{:S(2)}) %copy-start.2) | copy-done | bytes 1048600
  20.2 0.9 %copy-done.5 = bf16[256,256]{1,0:T(8,128)(2,1)S(1)} copy-done((bf16[256,256]{1,0:T(8,128)(2,1)S(1)}, bf16[256,256]{1,0:T(8,128)(2,1)}, u32[]{:S(2)}) %copy-start.5) | copy-done | bytes 131096
  21.1 0.9 %copy-done.6 = bf16[256,256]{1,0:T(8,128)(2,1)S(1)} copy-done((bf16[256,256]{1,0:T(8,128)(2,1)S(1)}, bf16[256,256]{1,0:T(8,128)(2,1)}, u32[]{:S(2)}) %copy-start.6) | copy-done | bytes 131096
  22.0 1.7 %context_own.1 = (f32[256,2048]{1,0:T(8,128)S(1)}, f32[256,2048]{1,0:T(8,128)S(1)}) custom-call(bf16[256,2048]{1,0:T(8,128)(2,1)S(1)} %copy-done.2, bf16[256,256]{1,0:T(8,128)(2,1)S(1)} %copy-done.5, bf16[256,256]{1,0:T(8,128)(2,1)S(1)} %copy-done.6), custom_call_target="tpu_custom_call" | custom-call | flops 1073741824 | bytes 6291456 | tf_op jit(solution)/shard_map/context_own/pallas_call | solution.py:355
  23.7 1.4 %copy-done = f32[256,2048]{1,0:T(8,128)} copy-done((f32[256,2048]{1,0:T(8,128)}, f32[256,2048]{1,0:T(8,128)S(1)}, u32[]{:S(2)}) %copy-start) | copy-done | bytes 2097176
  25.0 0.4 all-to-all-done.g
  25.5 3.0 %collective-permute-start.4 = (bf16[640,256]{1,0:T(8,128)(2,1)S(1)}, bf16[640,256]{1,0:T(8,128)(2,1)S(1)}, u32[]{:S(2)}, u32[]{:S(2)}) collective-permute-start(bf16[640,256]{1,0:T(8,128)(2,1)S(1)} %collective-permute-done.refs_1_), channel_id=1, source_target_pairs={{0,4},{4,0},{1,5},{5,1},{2,6},{6,2},{3,7},{7,3},{8,12},{12,8},{9,1... | collective-permute-start | bytes 983048 | tf_op jit(solution)/shard_map/ppermute | solution.py:422
  28.6 0.4 collective-permute-start.6
  29.0 2.6 %line_part.1 = (bf16[512,128]{1,0:T(8,128)(2,1)S(1)}, f32[64,128]{1,0:T(8,128)S(1)}, f32[64,128]{1,0:T(8,128)S(1)}, f32[64,128]{1,0:T(8,128)S(1)}, s32[16]{0:T(128)S(1)}) custom-call(bf16[8,80,128]{2,1,0:T(8,128)(2,1)S(1)} %all-to-all-done.g, s32[64]{0:T(128)S(1)} %copy-done.8, s32[64]{0:T(128)S(1)} %copy-done.9, s32[64]{0:T(128)S(1)} %copy-done.7), custom_call_target="tpu_custom_call" | custom-call | flops 16777216 | bytes 1048576 | tf_op jit(solution)/shard_map/line_part/pallas_call | solution.py:155
  31.6 3.7 %shard_part.1 = bf16[8,96,128]{2,1,0:T(8,128)(2,1)S(1)} custom-call(s32[16]{0:T(128)S(1)} %get-tuple-element.33.meta, bf16[512,128]{1,0:T(8,128)(2,1)S(1)} %get-tuple-element.34.q, bf16[640,256]{1,0:T(8,128)(2,1)S(1)} %get-tuple-element.35.refs_0_, bf16[640,256]{1,0:T(8,128)(2,1)S(1)} %collective-permute-done.refs_1_, ...), custom_call_target="tpu_custom_call" | custom-call | flops 1073741824 | bytes 4194304 | tf_op jit(solution)/shard_map/shard_part/pallas_call | solution.py:233
  35.3 13.0 %all_to_all.15.parts = bf16[8,96,128]{2,1,0:T(8,128)(2,1)S(1)} all-to-all(bf16[8,96,128]{2,1,0:T(8,128)(2,1)S(1)} %shard_part.1), channel_id=1, replica_groups=mesh['z'=8,'y'=4,'c'=2,'x'=4] {'z'}, dimensions={0} | all-to-all | bytes 393216 | tf_op jit(solution)/shard_map/all_to_all | solution.py:455
  48.4 0.9 %merge.1 = bf16[8,80,128]{2,1,0:T(8,128)(2,1)S(1)} custom-call(s32[16]{0:T(128)S(1)} %get-tuple-element.33.meta, bf16[8,96,128]{2,1,0:T(8,128)(2,1)S(1)} %all_to_all.15.parts, f32[64,128]{1,0:T(8,128)S(1)} %get-tuple-element.39.ro, f32[64,128]{1,0:T(8,128)S(1)} %get-tuple-element.40.rm, f32[64,128]{1,0:T(8,128)S(1)} %get-tuple-element.41.rl), custom_call_target="tpu_custom_call" | custom-call | flops 1048576 | bytes 524288 | tf_op jit(solution)/shard_map/merge/pallas_call | solution.py:270
  49.3 10.8 %all_to_all.16.refs_0_ = bf16[8,80,128]{2,1,0:T(8,128)(2,1)S(1)} all-to-all(bf16[8,80,128]{2,1,0:T(8,128)(2,1)S(1)} %merge.1), channel_id=1, replica_groups=mesh['z'=8,'y'=4,'c'=2,'x'=4] {'z'}, dimensions={0} | all-to-all | bytes 327680 | tf_op jit(solution)/shard_map/all_to_all | solution.py:456
  60.1 3.2 %collective-permute-start.9 = (bf16[8,80,128]{2,1,0:T(8,128)(2,1)S(1)}, bf16[8,80,128]{2,1,0:T(8,128)(2,1)S(1)}, u32[]{:S(2)}, u32[]{:S(2)}) collective-permute-start(bf16[8,80,128]{2,1,0:T(8,128)(2,1)S(1)} %all_to_all.16.refs_0_), channel_id=1, source_target_pairs={{0,24},{8,0},{16,8},{24,16},{1,25},{9,1},{17,9},{25,17},{2,26},{10... | collective-permute-start | bytes 491528 | tf_op jit(solution)/shard_map/ppermute | solution.py:422
  63.4 0.9 collective-permute-start.7
  64.3 3.2 %collective-permute-start.10 = (bf16[8,80,128]{2,1,0:T(8,128)(2,1)S(1)}, bf16[8,80,128]{2,1,0:T(8,128)(2,1)S(1)}, u32[]{:S(2)}, u32[]{:S(2)}) collective-permute-start(bf16[8,80,128]{2,1,0:T(8,128)(2,1)S(1)} %all_to_all.16.refs_0_), channel_id=1, source_target_pairs={{0,4},{4,0},{1,5},{5,1},{2,6},{6,2},{3,7},{7,3},{8,12},{12,8},{9,1... | collective-permute-start | bytes 491528 | tf_op jit(solution)/shard_map/ppermute | solution.py:422
  67.6 3.7 %collective-permute-start.13 = (bf16[8,80,128]{2,1,0:T(8,128)(2,1)S(1)}, bf16[8,80,128]{2,1,0:T(8,128)(2,1)S(1)}, u32[]{:S(2)}, u32[]{:S(2)}) collective-permute-start(bf16[8,80,128]{2,1,0:T(8,128)(2,1)S(1)} %collective-permute-done.9.refs_3_), channel_id=1, source_target_pairs={{0,4},{4,0},{1,5},{5,1},{2,6},{6,2},{3,7},{7,3},{8,12},{12,8},{9,1... | collective-permute-start | bytes 491528 | tf_op jit(solution)/shard_map/ppermute | solution.py:422
  71.2 2.1 %collective-permute-start.12 = (bf16[8,80,128]{2,1,0:T(8,128)(2,1)S(1)}, bf16[8,80,128]{2,1,0:T(8,128)(2,1)S(1)}, u32[]{:S(2)}, u32[]{:S(2)}) collective-permute-start(bf16[8,80,128]{2,1,0:T(8,128)(2,1)S(1)} %collective-permute-done.8.refs_2_), channel_id=1, source_target_pairs={{0,4},{4,0},{1,5},{5,1},{2,6},{6,2},{3,7},{7,3},{8,12},{12,8},{9,1... | collective-permute-start | bytes 491528 | tf_op jit(solution)/shard_map/ppermute | solution.py:422
  73.3 1.4 %collective-permute-start.11 = (bf16[8,80,128]{2,1,0:T(8,128)(2,1)S(1)}, bf16[8,80,128]{2,1,0:T(8,128)(2,1)S(1)}, u32[]{:S(2)}, u32[]{:S(2)}) collective-permute-start(bf16[8,80,128]{2,1,0:T(8,128)(2,1)S(1)} %collective-permute-done.7.refs_1_), channel_id=1, source_target_pairs={{0,4},{4,0},{1,5},{5,1},{2,6},{6,2},{3,7},{7,3},{8,12},{12,8},{9,1... | collective-permute-start | bytes 491528 | tf_op jit(solution)/shard_map/ppermute | solution.py:422
  74.7 1.0 %collective-permute-done.11.refs_5_ = bf16[8,80,128]{2,1,0:T(8,128)(2,1)S(1)} collective-permute-done((bf16[8,80,128]{2,1,0:T(8,128)(2,1)S(1)}, bf16[8,80,128]{2,1,0:T(8,128)(2,1)S(1)}, u32[]{:S(2)}, u32[]{:S(2)}) %collective-permute-start.11) | collective-permute-done | bytes 163872 | tf_op jit(solution)/shard_map/ppermute | solution.py:422
  75.8 1.2 %project.1 = (f32[64,128]{1,0:T(8,128)S(1)}, f32[64,128]{1,0:T(8,128)S(1)}, f32[64,128]{1,0:T(8,128)S(1)}, f32[64,128]{1,0:T(8,128)S(1)}) custom-call(s32[64]{0:T(128)S(1)} %copy-done.8, bf16[2048,128]{1,0:T(8,128)(2,1)S(1)} %copy-done.4, bf16[8,80,128]{2,1,0:T(8,128)(2,1)S(1)} %all_to_all.16.refs_0_, ...), custom_call_target="tpu_custom_call" | custom-call | flops 268435456 | bytes 2097152 | tf_op jit(solution)/shard_map/project/pallas_call | solution.py:314
  76.9 1.5 %collective-permute-start.14 = (f32[64,128]{1,0:T(8,128)S(1)}, f32[64,128]{1,0:T(8,128)S(1)}, u32[]{:S(2)}, u32[]{:S(2)}) collective-permute-start(f32[64,128]{1,0:T(8,128)S(1)} %get-tuple-element.43), channel_id=1, source_target_pairs={{0,1},{1,2},{2,3},{3,0},{4,5},{5,6},{6,7},{7,4},{8,9},{9,10},{10,1... | collective-permute-start | bytes 98312 | tf_op jit(solution)/shard_map/ppermute | solution.py:422
  78.5 2.1 %collective-permute-start.15 = (f32[64,128]{1,0:T(8,128)S(1)}, f32[64,128]{1,0:T(8,128)S(1)}, u32[]{:S(2)}, u32[]{:S(2)}) collective-permute-start(f32[64,128]{1,0:T(8,128)S(1)} %get-tuple-element.44), channel_id=1, source_target_pairs={{0,2},{1,3},{2,0},{3,1},{4,6},{5,7},{6,4},{7,5},{8,10},{9,11},{10,... | collective-permute-start | bytes 98312 | tf_op jit(solution)/shard_map/ppermute | solution.py:422
  80.6 1.4 %collective-permute-start.16 = (f32[64,128]{1,0:T(8,128)S(1)}, f32[64,128]{1,0:T(8,128)S(1)}, u32[]{:S(2)}, u32[]{:S(2)}) collective-permute-start(f32[64,128]{1,0:T(8,128)S(1)} %get-tuple-element.45), channel_id=1, source_target_pairs={{0,3},{1,0},{2,1},{3,2},{4,7},{5,4},{6,5},{7,6},{8,11},{9,8},{10,9... | collective-permute-start | bytes 98312 | tf_op jit(solution)/shard_map/ppermute | solution.py:422
  82.0 3.6 %context_far.1 = bf16[256,2048]{1,0:T(8,128)(2,1)} custom-call(s32[64]{0:T(128)S(1)} %copy-done.7, bf16[256,2048]{1,0:T(8,128)(2,1)S(1)} %copy-done.3, f32[256,2048]{1,0:T(8,128)S(1)} %get-tuple-element.30.own, f32[256,2048]{1,0:T(8,128)S(1)} %copy-done.1, bf16[8,80,128]{2,1,0:T(8,128)(2,1)S(1)} %all_to_all.16.refs_0_, ...), custom_call_target="tpu_custom_call" | custom-call | flops 1073741824 | bytes 6291456 | tf_op jit(solution)/shard_map/context_far/pallas_call | solution.py:404
  85.6 0.6 add_convert_fusion
  (34 shorter events, 0.4 us)
Async XLA Ops:
  2.9 22.5 %collective-permute-start = (bf16[640,256]{1,0:T(8,128)(2,1)}, bf16[640,256]{1,0:T(8,128)(2,1)S(1)}, u32[]{:S(2)}, u32[]{:S(2)}) collective-permute-start(bf16[640,256]{1,0:T(8,128)(2,1)} %get-tuple-element.27), channel_id=1, source_target_pairs={{0,8},{8,16},{16,24},{24,0},{1,9},{9,17},{17,25},{25,1},{2,10},{10... | collective-permute-start | bytes 983048 | tf_op jit(solution)/shard_map/ppermute | solution.py:422
  5.1 20.3 %collective-permute-start.1 = (bf16[640,256]{1,0:T(8,128)(2,1)}, bf16[640,256]{1,0:T(8,128)(2,1)S(1)}, u32[]{:S(2)}, u32[]{:S(2)}) collective-permute-start(bf16[640,256]{1,0:T(8,128)(2,1)} %get-tuple-element.28), channel_id=1, source_target_pairs={{0,16},{8,24},{16,0},{24,8},{1,17},{9,25},{17,1},{25,9},{2,18},{10... | collective-permute-start | bytes 983048 | tf_op jit(solution)/shard_map/ppermute | solution.py:422
  7.7 17.7 %collective-permute-start.2 = (bf16[640,256]{1,0:T(8,128)(2,1)}, bf16[640,256]{1,0:T(8,128)(2,1)}, u32[]{:S(2)}, u32[]{:S(2)}) collective-permute-start(bf16[640,256]{1,0:T(8,128)(2,1)} %get-tuple-element.29), channel_id=1, source_target_pairs={{0,24},{8,0},{16,8},{24,16},{1,25},{9,1},{17,9},{25,17},{2,26},{10... | collective-permute-start | bytes 983048 | tf_op jit(solution)/shard_map/ppermute | solution.py:422
  8.8 20.2 %copy-start.7 = (s32[64]{0:T(128)S(1)}, s32[64]{0:T(128)}, u32[]{:S(2)}) copy-start(s32[64]{0:T(128)} %blocks.3) | copy-start | bytes 772
  8.8 20.2 %copy-start.8 = (s32[64]{0:T(128)S(1)}, s32[64]{0:T(128)}, u32[]{:S(2)}) copy-start(s32[64]{0:T(128)} %owner.3) | copy-start | bytes 772
  8.8 20.2 %copy-start.9 = (s32[64]{0:T(128)S(1)}, s32[64]{0:T(128)}, u32[]{:S(2)}) copy-start(s32[64]{0:T(128)} %lengths.1) | copy-start | bytes 772
  8.8 16.6 %all-to-all-start = ((bf16[8,80,128]{2,1,0:T(8,128)(2,1)}), bf16[8,80,128]{2,1,0:T(8,128)(2,1)S(1)}, u32[]{:S(2)}, u32[]{:S(2)}) async-start(bf16[8,80,128]{2,1,0:T(8,128)(2,1)} %get-tuple-element.24), calls=%async_computation | async-start | bytes 327680 | tf_op jit(solution)/shard_map/all_to_all | solution.py:449
  17.1 14.4 %collective-permute-start.3 = (bf16[640,256]{1,0:T(8,128)(2,1)S(1)}, bf16[640,256]{1,0:T(8,128)(2,1)}, u32[]{:S(2)}, u32[]{:S(2)}) collective-permute-start(bf16[640,256]{1,0:T(8,128)(2,1)S(1)} %get-tuple-element.35.refs_0_), channel_id=1, source_target_pairs={{0,4},{4,0},{1,5},{5,1},{2,6},{6,2},{3,7},{7,3},{8,12},{12,8},{9,1... | collective-permute-start | bytes 983048 | tf_op jit(solution)/shard_map/ppermute | solution.py:422
  18.9 1.2 %copy-start.2 = (bf16[256,2048]{1,0:T(8,128)(2,1)S(1)}, bf16[256,2048]{1,0:T(8,128)(2,1)}, u32[]{:S(2)}) copy-start(bf16[256,2048]{1,0:T(8,128)(2,1)} %q.3) | copy-start | bytes 3145732
  20.2 0.9 %copy-start.5 = (bf16[256,256]{1,0:T(8,128)(2,1)S(1)}, bf16[256,256]{1,0:T(8,128)(2,1)}, u32[]{:S(2)}) copy-start(bf16[256,256]{1,0:T(8,128)(2,1)} %xk.3) | copy-start | bytes 393220
  21.1 0.9 %copy-start.6 = (bf16[256,256]{1,0:T(8,128)(2,1)S(1)}, bf16[256,256]{1,0:T(8,128)(2,1)}, u32[]{:S(2)}) copy-start(bf16[256,256]{1,0:T(8,128)(2,1)} %xv.3) | copy-start | bytes 393220
  23.7 1.4 %copy-start = (f32[256,2048]{1,0:T(8,128)}, f32[256,2048]{1,0:T(8,128)S(1)}, u32[]{:S(2)}) copy-start(f32[256,2048]{1,0:T(8,128)S(1)} %get-tuple-element.31.lse) | copy-start | bytes 6291460
  25.5 6.1 %collective-permute-start.4 = (bf16[640,256]{1,0:T(8,128)(2,1)S(1)}, bf16[640,256]{1,0:T(8,128)(2,1)S(1)}, u32[]{:S(2)}, u32[]{:S(2)}) collective-permute-start(bf16[640,256]{1,0:T(8,128)(2,1)S(1)} %collective-permute-done.refs_1_), channel_id=1, source_target_pairs={{0,4},{4,0},{1,5},{5,1},{2,6},{6,2},{3,7},{7,3},{8,12},{12,8},{9,1... | collective-permute-start | bytes 983048 | tf_op jit(solution)/shard_map/ppermute | solution.py:422
  28.5 3.1 %collective-permute-start.5 = (bf16[640,256]{1,0:T(8,128)(2,1)S(1)}, bf16[640,256]{1,0:T(8,128)(2,1)S(1)}, u32[]{:S(2)}, u32[]{:S(2)}) collective-permute-start(bf16[640,256]{1,0:T(8,128)(2,1)S(1)} %collective-permute-done.1.refs_2_), channel_id=1, source_target_pairs={{0,4},{4,0},{1,5},{5,1},{2,6},{6,2},{3,7},{7,3},{8,12},{12,8},{9,1... | collective-permute-start | bytes 983048 | tf_op jit(solution)/shard_map/ppermute | solution.py:422
  28.6 3.1 %collective-permute-start.6 = (bf16[640,256]{1,0:T(8,128)(2,1)}, bf16[640,256]{1,0:T(8,128)(2,1)S(1)}, u32[]{:S(2)}, u32[]{:S(2)}) collective-permute-start(bf16[640,256]{1,0:T(8,128)(2,1)} %collective-permute-done.2.refs_3_), channel_id=1, source_target_pairs={{0,4},{4,0},{1,5},{5,1},{2,6},{6,2},{3,7},{7,3},{8,12},{12,8},{9,1... | collective-permute-start | bytes 983048 | tf_op jit(solution)/shard_map/ppermute | solution.py:422
  31.6 44.2 %copy-start.4 = (bf16[2048,128]{1,0:T(8,128)(2,1)S(1)}, bf16[2048,128]{1,0:T(8,128)(2,1)}, u32[]{:S(2)}) copy-start(bf16[2048,128]{1,0:T(8,128)(2,1)} %w.1) | copy-start | bytes 1572868
  31.6 50.4 %copy-start.3 = (bf16[256,2048]{1,0:T(8,128)(2,1)S(1)}, bf16[256,2048]{1,0:T(8,128)(2,1)}, u32[]{:S(2)}) copy-start(bf16[256,2048]{1,0:T(8,128)(2,1)} %q.3) | copy-start | bytes 3145732
  35.3 46.7 %copy-start.1 = (f32[256,2048]{1,0:T(8,128)S(1)}, f32[256,2048]{1,0:T(8,128)}, u32[]{:S(2)}) copy-start(f32[256,2048]{1,0:T(8,128)} %copy-done) | copy-start | bytes 6291460
  60.1 7.5 %collective-permute-start.9 = (bf16[8,80,128]{2,1,0:T(8,128)(2,1)S(1)}, bf16[8,80,128]{2,1,0:T(8,128)(2,1)S(1)}, u32[]{:S(2)}, u32[]{:S(2)}) collective-permute-start(bf16[8,80,128]{2,1,0:T(8,128)(2,1)S(1)} %all_to_all.16.refs_0_), channel_id=1, source_target_pairs={{0,24},{8,0},{16,8},{24,16},{1,25},{9,1},{17,9},{25,17},{2,26},{10... | collective-permute-start | bytes 491528 | tf_op jit(solution)/shard_map/ppermute | solution.py:422
  63.3 8.0 %collective-permute-start.8 = (bf16[8,80,128]{2,1,0:T(8,128)(2,1)S(1)}, bf16[8,80,128]{2,1,0:T(8,128)(2,1)S(1)}, u32[]{:S(2)}, u32[]{:S(2)}) collective-permute-start(bf16[8,80,128]{2,1,0:T(8,128)(2,1)S(1)} %all_to_all.16.refs_0_), channel_id=1, source_target_pairs={{0,16},{8,24},{16,0},{24,8},{1,17},{9,25},{17,1},{25,9},{2,18},{10... | collective-permute-start | bytes 491528 | tf_op jit(solution)/shard_map/ppermute | solution.py:422
  63.4 9.9 %collective-permute-start.7 = (bf16[8,80,128]{2,1,0:T(8,128)(2,1)S(1)}, bf16[8,80,128]{2,1,0:T(8,128)(2,1)S(1)}, u32[]{:S(2)}, u32[]{:S(2)}) collective-permute-start(bf16[8,80,128]{2,1,0:T(8,128)(2,1)S(1)} %all_to_all.16.refs_0_), channel_id=1, source_target_pairs={{0,8},{8,16},{16,24},{24,0},{1,9},{9,17},{17,25},{25,1},{2,10},{10... | collective-permute-start | bytes 491528 | tf_op jit(solution)/shard_map/ppermute | solution.py:422
  64.3 10.5 %collective-permute-start.10 = (bf16[8,80,128]{2,1,0:T(8,128)(2,1)S(1)}, bf16[8,80,128]{2,1,0:T(8,128)(2,1)S(1)}, u32[]{:S(2)}, u32[]{:S(2)}) collective-permute-start(bf16[8,80,128]{2,1,0:T(8,128)(2,1)S(1)} %all_to_all.16.refs_0_), channel_id=1, source_target_pairs={{0,4},{4,0},{1,5},{5,1},{2,6},{6,2},{3,7},{7,3},{8,12},{12,8},{9,1... | collective-permute-start | bytes 491528 | tf_op jit(solution)/shard_map/ppermute | solution.py:422
  67.6 7.2 %collective-permute-start.13 = (bf16[8,80,128]{2,1,0:T(8,128)(2,1)S(1)}, bf16[8,80,128]{2,1,0:T(8,128)(2,1)S(1)}, u32[]{:S(2)}, u32[]{:S(2)}) collective-permute-start(bf16[8,80,128]{2,1,0:T(8,128)(2,1)S(1)} %collective-permute-done.9.refs_3_), channel_id=1, source_target_pairs={{0,4},{4,0},{1,5},{5,1},{2,6},{6,2},{3,7},{7,3},{8,12},{12,8},{9,1... | collective-permute-start | bytes 491528 | tf_op jit(solution)/shard_map/ppermute | solution.py:422
  71.2 3.5 %collective-permute-start.12 = (bf16[8,80,128]{2,1,0:T(8,128)(2,1)S(1)}, bf16[8,80,128]{2,1,0:T(8,128)(2,1)S(1)}, u32[]{:S(2)}, u32[]{:S(2)}) collective-permute-start(bf16[8,80,128]{2,1,0:T(8,128)(2,1)S(1)} %collective-permute-done.8.refs_2_), channel_id=1, source_target_pairs={{0,4},{4,0},{1,5},{5,1},{2,6},{6,2},{3,7},{7,3},{8,12},{12,8},{9,1... | collective-permute-start | bytes 491528 | tf_op jit(solution)/shard_map/ppermute | solution.py:422
  73.3 2.5 %collective-permute-start.11 = (bf16[8,80,128]{2,1,0:T(8,128)(2,1)S(1)}, bf16[8,80,128]{2,1,0:T(8,128)(2,1)S(1)}, u32[]{:S(2)}, u32[]{:S(2)}) collective-permute-start(bf16[8,80,128]{2,1,0:T(8,128)(2,1)S(1)} %collective-permute-done.7.refs_1_), channel_id=1, source_target_pairs={{0,4},{4,0},{1,5},{5,1},{2,6},{6,2},{3,7},{7,3},{8,12},{12,8},{9,1... | collective-permute-start | bytes 491528 | tf_op jit(solution)/shard_map/ppermute | solution.py:422
  76.9 8.7 %collective-permute-start.14 = (f32[64,128]{1,0:T(8,128)S(1)}, f32[64,128]{1,0:T(8,128)S(1)}, u32[]{:S(2)}, u32[]{:S(2)}) collective-permute-start(f32[64,128]{1,0:T(8,128)S(1)} %get-tuple-element.43), channel_id=1, source_target_pairs={{0,1},{1,2},{2,3},{3,0},{4,5},{5,6},{6,7},{7,4},{8,9},{9,10},{10,1... | collective-permute-start | bytes 98312 | tf_op jit(solution)/shard_map/ppermute | solution.py:422
  78.5 7.2 %collective-permute-start.15 = (f32[64,128]{1,0:T(8,128)S(1)}, f32[64,128]{1,0:T(8,128)S(1)}, u32[]{:S(2)}, u32[]{:S(2)}) collective-permute-start(f32[64,128]{1,0:T(8,128)S(1)} %get-tuple-element.44), channel_id=1, source_target_pairs={{0,2},{1,3},{2,0},{3,1},{4,6},{5,7},{6,4},{7,5},{8,10},{9,11},{10,... | collective-permute-start | bytes 98312 | tf_op jit(solution)/shard_map/ppermute | solution.py:422
  80.6 5.1 %collective-permute-start.16 = (f32[64,128]{1,0:T(8,128)S(1)}, f32[64,128]{1,0:T(8,128)S(1)}, u32[]{:S(2)}, u32[]{:S(2)}) collective-permute-start(f32[64,128]{1,0:T(8,128)S(1)} %get-tuple-element.45), channel_id=1, source_target_pairs={{0,3},{1,0},{2,1},{3,2},{4,7},{5,4},{6,5},{7,6},{8,11},{9,8},{10,9... | collective-permute-start | bytes 98312 | tf_op jit(solution)/shard_map/ppermute | solution.py:422

commit v2 on v1

--- a/solution.py
+++ b/solution.py
@@ -15,7 +15,7 @@
 SLOTS = 64
 SCALE2 = math.log2(math.e) / math.sqrt(HD)
 LOW = -1e29
-FLOOR = -1e28
+FLOOR = -(2.0**80)
 F32 = jnp.float32
 BF16 = jnp.bfloat16
 VMEM = pl.BlockSpec(memory_space=pltpu.VMEM)
@@ -32,7 +32,7 @@
     return lax.dot_general(a, b, dims, preferred_element_type=F32)
 
 
-def params(mib=20):
+def params(mib=16):
     return pltpu.CompilerParams(vmem_limit_bytes=mib * 2**20)
 
 
@@ -105,26 +105,8 @@
     )(*args)
 
 
-def line_kernel(g, owner, lengths, blocks, q_out, ro_out, rm_out, rl_out, meta):
-    z, y, c = lax.axis_index("z"), lax.axis_index("y"), lax.axis_index("c")
-    line = y * NC + c
-    for s in range(8):
-        meta[s] = 0
-
-    def scan_slots(r, root):
-        slot = owner[r]
-
-        @pl.when(lax.rem(slot, 8) == line)
-        def _():
-            meta[slot // 8] = lengths[r]
-
-        return jnp.where(blocks[r] == 0, r, root)
-
-    root = lax.fori_loop(0, SLOTS, scan_slots, jnp.int32(0))
-    meta[8] = root // 8
-    meta[9] = lax.rem(root, 8) // 2
-    meta[10] = lax.rem(root, 2)
-
+def line_kernel(g, q_out, ro_out, rm_out, rl_out):
+    z = lax.axis_index("z")
     row, col = iota((256, 256), 0), iota((256, 256), 1)
     source = lax.rem(row // 4, 8) * 32 + (row // 32) * 4 + lax.rem(row, 4)
     pick = (col == source).astype(F32).astype(BF16)
@@ -150,62 +132,90 @@
     ro_out[...] = dot(weights.astype(BF16), values)
 
 
-def line_part(gathered, owner, lengths, blocks):
+def line_part(gathered):
     part = jax.ShapeDtypeStruct((64, HD), F32)
     return pl.pallas_call(
         line_kernel,
-        out_shape=(
-            jax.ShapeDtypeStruct((512, HD), BF16),
-            part,
-            part,
-            part,
-            jax.ShapeDtypeStruct((16,), jnp.int32),
-        ),
-        in_specs=[VMEM, SMEM, SMEM, SMEM],
-        out_specs=(VMEM, VMEM, VMEM, VMEM, SMEM),
+        out_shape=(jax.ShapeDtypeStruct((512, HD), BF16), part, part, part),
+        in_specs=[VMEM],
+        out_specs=(VMEM,) * 4,
         compiler_params=params(),
         cost_estimate=cost(1 << 24, 1 << 20),
         name="line_part",
-    )(gathered, owner, lengths, blocks)
-
-
-def shard_kernel(meta, q, *refs):
-    bufs, out, scores = refs[:8], refs[8], refs[9]
-    z, y, c = lax.axis_index("z"), lax.axis_index("y"), lax.axis_index("c")
+    )(gathered)
+
+
+def shard_scores(meta, q, bufs, k, core, scores):
+    z, y = lax.axis_index("z"), lax.axis_index("y")
     rowslot = iota((32, HD), 0) // 4
     length = jnp.zeros((32, HD), jnp.int32)
     for s in range(8):
         length = jnp.where(rowslot == s, meta[s], length)
     lane = iota((32, HD), 1)
+    tops = []
+    for b in range(4):
+        room = length - (z * 8 + lax.rem(y - b + NY, NY) * NC + core) * ROWS
+        keep = jnp.concatenate([lane < room, lane + HD < room], axis=1)
+        raw = dot(q[k * 256 : (k + 1) * 256, :], bufs[b][0:ROWS, k * HD : (k + 1) * HD], NT)
+        raw = jnp.where(keep[None], raw.reshape(8, 32, 256), LOW).reshape(256, 256)
+        scores[k, b] = raw
+        tops.append(jnp.max(jnp.maximum(raw[:, :HD], raw[:, HD:]), axis=1, keepdims=True))
+    return tops
+
+
+def shard_sums(bufs, k, tops, top, scores, total, weighted):
+    for b in range(4):
+        weights = jnp.exp2((scores[k, b] - tops[b]) * SCALE2)
+        factor = jnp.exp2(tops[b] * SCALE2 - top)
+        total = total + (weights[:, :HD] + weights[:, HD:]) * factor
+        weighted = weighted + factor * dot(
+            weights.astype(BF16), bufs[b][ROWS : 2 * ROWS, k * HD : (k + 1) * HD]
+        )
+    return total, weighted
+
+
+def first_kernel(meta, q, *refs):
+    bufs, (o_out, m_out, l_out, scores) = refs[:4], refs[4:]
+    core = lax.axis_index("c")
+    tops = [shard_scores(meta, q, bufs, k, core, scores) for k in range(2)]
+    zeros = jnp.zeros((256, HD), F32)
     for k in range(2):
-        qk = q[k * 256 : (k + 1) * 256, :]
-        tops = []
-        for b in range(8):
-            shift, swap = b % 4, b // 4
-            shard = z * 8 + lax.rem(y - shift + NY, NY) * NC + (c if swap == 0 else 1 - c)
-            room = length - shard * ROWS
-            keep = jnp.concatenate([lane < room, lane + HD < room], axis=1)
-            raw = dot(qk, bufs[b][0:ROWS, k * HD : (k + 1) * HD], NT)
-            raw = jnp.where(keep[None], raw.reshape(8, 32, 256), LOW).reshape(256, 256)
-            scores[b] = raw
-            tops.append(
-                jnp.max(jnp.maximum(raw[:, :HD], raw[:, HD:]), axis=1, keepdims=True)
-            )
-        top = functools.reduce(jnp.maximum, tops) * SCALE2
+        rows = slice(k * 256, (k + 1) * 256)
+        top = jnp.maximum(functools.reduce(jnp.maximum, tops[k]) * SCALE2, FLOOR)
+        l_out[rows, :], o_out[rows, :] = shard_sums(bufs, k, tops[k], top, scores, zeros, zeros)
+        m_out[rows, :] = jnp.broadcast_to(top, (256, HD))
+
+
+def first_part(meta, q, bufs):
+    part = jax.ShapeDtypeStruct((512, HD), F32)
+    return pl.pallas_call(
+        first_kernel,
+        out_shape=(part,) * 3,
+        in_specs=[SMEM] + [VMEM] * 5,
+        out_specs=(VMEM,) * 3,
+        scratch_shapes=[pltpu.VMEM((2, 4, 256, 256), F32)],
+        compiler_params=params(),
+        cost_estimate=cost(1 << 29, 2 << 20, 1 << 19),
+        name="first_part",
+    )(meta, q, *bufs)
+
+
+def second_kernel(meta, q, o, m, l, *refs):
+    all_bufs, bufs, (out, scores) = refs[:8], refs[4:8], refs[8:]
+    core = 1 - lax.axis_index("c")
+    tops = [shard_scores(meta, q, bufs, k, core, scores) for k in range(2)]
+    column = iota((256, HD), 1)
+    for k in range(2):
+        rows = slice(k * 256, (k + 1) * 256)
+        top = jnp.maximum(functools.reduce(jnp.maximum, tops[k]) * SCALE2, m[rows, :])
         top = top.astype(BF16).astype(F32)
-        total = jnp.zeros((256, HD), F32)
-        weighted = jnp.zeros((256, HD), F32)
-        for b in range(8):
-            weights = jnp.exp2((scores[b] - jnp.maximum(tops[b], FLOOR)) * SCALE2)
-            factor = jnp.exp2(jnp.minimum(tops[b] * SCALE2 - top, 64.0))
-            total = total + (weights[:, :HD] + weights[:, HD:]) * factor
-            weighted = weighted + factor * dot(
-                weights.astype(BF16), bufs[b][ROWS : 2 * ROWS, k * HD : (k + 1) * HD]
-            )
+        factor = jnp.exp2(m[rows, :] - top)
+        total, weighted = shard_sums(
+            bufs, k, tops[k], top, scores, l[rows, :] * factor, o[rows, :] * factor
+        )
         total = jnp.sum(total, axis=1, keepdims=True)
         total_high = total.astype(BF16).astype(F32)
         total_low = total - total_high
-        column = iota((256, HD), 1)
         stats = jnp.where(
             column == 0, top, jnp.where(column == 1, total_high, jnp.where(column == 2, total_low, 0.0))
         )
@@ -216,30 +226,31 @@
             out[k * 4 + pair * 2 + 1, 64:80, :] = flipped
         for part in range(4):
             out[k * 4 + part, 0:64, :] = weighted[part * 64 : (part + 1) * 64]
+    y, c = lax.axis_index("y"), lax.axis_index("c")
     root_shift = lax.rem(y - meta[9] + NY, NY)
-    root_swap = jnp.where(meta[10] == c, 0, 1)
     for b in range(8):
-        for core in range(2):
-
-            @pl.when((root_shift == b % 4) & (root_swap == b // 4) & (c == core))
-            def _(b=b, core=core):
+        for lane_half in range(2):
+            swapped = b // 4
+            from_core = jnp.where(meta[10] == c, 0, 1)
+
+            @pl.when((root_shift == b % 4) & (from_core == swapped) & (c == lane_half))
+            def _(b=b, lane_half=lane_half):
+                lanes = slice(lane_half * HD, (lane_half + 1) * HD)
                 for piece in range(NZ):
-                    out[piece, 80:96, :] = bufs[b][
-                        512 + piece * 16 : 528 + piece * 16, core * HD : (core + 1) * HD
-                    ]
-
-
-def shard_part(meta, q, bufs):
-    return pl.pallas_call(
-        shard_kernel,
+                    out[piece, 80:96, :] = all_bufs[b][512 + piece * 16 : 528 + piece * 16, lanes]
+
+
+def second_part(meta, q, state, bufs):
+    return pl.pallas_call(
+        second_kernel,
         out_shape=jax.ShapeDtypeStruct((NZ, 96, HD), BF16),
-        in_specs=[SMEM] + [VMEM] * 9,
+        in_specs=[SMEM] + [VMEM] * 12,
         out_specs=VMEM,
-        scratch_shapes=[pltpu.VMEM((8, 256, 256), F32)],
-        compiler_params=params(),
-        cost_estimate=cost(1 << 30, 4 << 20, 1 << 20),
-        name="shard_part",
-    )(meta, q, *bufs)
+        scratch_shapes=[pltpu.VMEM((2, 4, 256, 256), F32)],
+        compiler_params=params(),
+        cost_estimate=cost(1 << 29, 2 << 20, 1 << 19),
+        name="second_part",
+    )(meta, q, *state, *bufs)
 
 
 def merge_kernel(meta, parts, ro, rm, rl, out, scratch):
@@ -322,18 +333,49 @@
     )(owner, w, *bufs)
 
 
-def own_kernel(q, xk, xv, out, lse, values):
+def find_places(owner, lengths, blocks, meta):
+    z, y, c = lax.axis_index("z"), lax.axis_index("y"), lax.axis_index("c")
+    line = y * NC + c
+    root = jnp.int32(0)
+    for r in range(SLOTS):
+        slot = owner[r]
+        meta[jnp.where(slot & 7 == line, slot >> 3, 15)] = lengths[r]
+        root = jnp.where(blocks[r] == 0, r, root)
+    meta[8] = root // 8
+    meta[9] = lax.rem(root, 8) // 2
+    meta[10] = lax.rem(root, 2)
+    meta[11] = jnp.where(root == z * 8 + line, 1, 0)
+
+
+def own_kernel(
+    q, xk, xv, owner, lengths, blocks, out, lse, meta, values, staged, lse_v, q_v, xk_v, xv_v, owner_s, lengths_s, blocks_s, sems
+):
+    copies = [(xk, xk_v), (xv, xv_v)]
+    for group in range(4):
+        lanes = slice(group * 512, (group + 1) * 512)
+        copies.append((q.at[:, lanes], q_v.at[:, lanes]))
+    copies += [(owner, owner_s), (lengths, lengths_s), (blocks, blocks_s)]
+    copies = [pltpu.make_async_copy(src, dst, sems.at[i]) for i, (src, dst) in enumerate(copies)]
+    for copy in copies:
+        copy.start()
+    causal = iota((128, 128), 0) >= iota((128, 128), 1)
+    results = []
+    for copy in copies[6:]:
+        copy.wait()
+    find_places(owner_s, lengths_s, blocks_s, meta)
+    copies[0].wait()
+    copies[1].wait()
     for k in range(2):
-        values[k, :, 0:HD] = xv[:, k * HD : (k + 1) * HD]
+        values[k, :, 0:HD] = xv_v[:, k * HD : (k + 1) * HD]
         values[k, :, HD:] = jnp.ones((ROWS, HD), BF16)
-    causal = iota((128, 128), 0) >= iota((128, 128), 1)
     for group in range(4):
         units = [(group * 4 + h, half) for h in range(4) for half in range(2)]
         tiles, tops = [], []
+        copies[2 + group].wait()
         for h, half in units:
             near = (half + 1) * 128
-            keys = xk[0:near, (h // 8) * HD : (h // 8 + 1) * HD]
-            own = dot(q[near - 128 : near, h * HD : (h + 1) * HD], keys, NT)
+            keys = xk_v[0:near, (h // 8) * HD : (h // 8 + 1) * HD]
+            own = dot(q_v[near - 128 : near, h * HD : (h + 1) * HD], keys, NT)
             diagonal = jnp.where(causal, own[:, near - 128 :], LOW)
             tiles.append([own[:, :HD], diagonal] if half else [diagonal])
         for parts in tiles:
@@ -346,28 +388,49 @@
             weights = jnp.concatenate(weights, axis=1) if half else weights[0]
             summed = dot(weights, values[h // 8, 0:near, :])
             rows, lanes = slice(near - 128, near), slice(h * HD, (h + 1) * HD)
-            out[rows, lanes] = summed[:, :HD] / summed[:, HD:]
-            lse[rows, lanes] = top + jnp.log2(summed[:, HD:])
-
-
-def context_own(q, xk, xv):
-    whole = jax.ShapeDtypeStruct((ROWS, 2048), F32)
+            staged[rows, lanes] = summed[:, :HD] / summed[:, HD:]
+            lse_v[rows, lanes] = top + jnp.log2(summed[:, HD:])
+        lanes = slice(group * 512, (group + 1) * 512)
+        for i, (src, dst) in enumerate(((staged, out), (lse_v, lse))):
+            sem = sems.at[9 + group * 2 + i]
+            results.append(pltpu.make_async_copy(src.at[:, lanes], dst.at[:, lanes], sem))
+            results[-1].start()
+    for copy in results:
+        copy.wait()
+
+
+def context_own(*args):
+    args = [pltpu.with_memory_space_constraint(a, pltpu.HBM) for a in args]
     return pl.pallas_call(
         own_kernel,
-        out_shape=(whole, whole),
-        in_specs=[VMEM] * 3,
-        out_specs=(VMEM, VMEM),
-        scratch_shapes=[pltpu.VMEM((2, ROWS, 2 * HD), BF16)],
+        out_shape=(
+            pltpu.HBM((ROWS, 2048), F32),
+            pltpu.HBM((ROWS, 2048), F32),
+            jax.ShapeDtypeStruct((16,), jnp.int32),
+        ),
+        in_specs=[pl.BlockSpec(memory_space=pltpu.HBM)] * 6,
+        out_specs=(pl.BlockSpec(memory_space=pltpu.HBM),) * 2 + (SMEM,),
+        scratch_shapes=[
+            pltpu.VMEM((2, ROWS, 2 * HD), BF16),
+            pltpu.VMEM((ROWS, 2048), F32),
+            pltpu.VMEM((ROWS, 2048), F32),
+            pltpu.VMEM((ROWS, 2048), BF16),
+            pltpu.VMEM((ROWS, 256), BF16),
+            pltpu.VMEM((ROWS, 256), BF16),
+            pltpu.SMEM((SLOTS,), jnp.int32),
+            pltpu.SMEM((SLOTS,), jnp.int32),
+            pltpu.SMEM((SLOTS,), jnp.int32),
+            pltpu.SemaphoreType.DMA((17,)),
+        ],
         compiler_params=params(),
         cost_estimate=cost(1 << 30, 6 << 20, 1 << 20),
         name="context_own",
-    )(q, xk, xv)
-
-
-def far_kernel(blocks, q, own, lse, *refs):
+    )(*args)
+
+
+def far_kernel(meta, q, own, lse, *refs):
     bufs, (out, keys, values, staged, sems) = refs[:8], refs[8:]
-    index = (lax.axis_index("z") * NY + lax.axis_index("y")) * NC + lax.axis_index("c")
-    hide = jnp.where(blocks[index] == 0, LOW, 0.0).astype(F32)
+    hide = jnp.where(meta[11] == 1, -LOW, 0.0).astype(F32)
     for k in range(2):
         values[k, :, HD:] = jnp.ones((ROWS, HD), BF16)
         for j, buf in enumerate(bufs):
@@ -377,22 +440,27 @@
                 values[k, at : at + 16, 0:HD] = buf[4 + tile, 64:80, :]
     copies = []
     for group in range(4):
-        units = [(group * 4 + h, half) for h in range(4) for half in range(2)]
-        tiles = []
-        for h, half in units:
-            queries = q[half * 128 : (half + 1) * 128, h * HD : (h + 1) * HD]
-            far = dot(queries, keys[h // 8], NT) + hide
-            tiles.append([far[:, :HD], far[:, HD:]])
-        tops = [jnp.max(jnp.maximum(*t), axis=1, keepdims=True) * SCALE2 for t in tiles]
-        for (h, half), parts, top in zip(units, tiles, tops):
-            rows, lanes = slice(half * 128, (half + 1) * 128), slice(h * HD, (h + 1) * HD)
-            near = lse[rows, lanes]
-            top = jnp.maximum(top, near)
-            weights = [jnp.exp2(t * SCALE2 - top).astype(BF16) for t in parts]
-            summed = dot(jnp.concatenate(weights, axis=1), values[h // 8])
+        k = group // 2
+        heads = [slice(h * HD, (h + 1) * HD) for h in range(group * 4, group * 4 + 4)]
+        scores = dot(jnp.concatenate([q[:, lanes] for lanes in heads], axis=0), keys[k], NT)
+        tiles = [scores[i * ROWS : (i + 1) * ROWS] for i in range(4)]
+        tops = [
+            jnp.max(jnp.maximum(t[:, :HD], t[:, HD:]), axis=1, keepdims=True) * SCALE2 - hide
+            for t in tiles
+        ]
+        nears = [lse[:, lanes] for lanes in heads]
+        tops = [jnp.maximum(top, near) for top, near in zip(tops, nears)]
+        weights = []
+        for t, top in zip(tiles, tops):
+            top = top + hide
+            halves = [jnp.exp2(half * SCALE2 - top).astype(BF16) for half in (t[:, :HD], t[:, HD:])]
+            weights.append(jnp.concatenate(halves, axis=1))
+        summed = dot(jnp.concatenate(weights, axis=0), values[k])
+        for i, (top, near, lanes) in enumerate(zip(tops, nears, heads)):
+            part = summed[i * ROWS : (i + 1) * ROWS]
             factor = jnp.exp2(near - top)
-            joint = summed[:, :HD] + factor * own[rows, lanes]
-            staged[rows, lanes] = (joint / (summed[:, HD:] + factor)).astype(BF16)
+            joint = part[:, :HD] + factor * own[:, lanes]
+            staged[:, lanes] = (joint / (part[:, HD:] + factor)).astype(BF16)
         lanes = slice(group * 512, (group + 1) * 512)
         copies.append(pltpu.make_async_copy(staged.at[:, lanes], out.at[:, lanes], sems.at[group]))
         copies[-1].start()
@@ -400,7 +468,7 @@
         copy.wait()
 
 
-def context_far(blocks, q, own, lse, bufs):
+def context_far(meta, q, own, lse, bufs):
     return pl.pallas_call(
         far_kernel,
         out_shape=jax.ShapeDtypeStruct((ROWS, 2048), BF16),
@@ -415,7 +483,7 @@
         compiler_params=params(),
         cost_estimate=cost(1 << 30, 6 << 20, 1 << 20),
         name="context_far",
-    )(blocks, q, own, lse, *bufs)
+    )(meta, q, own, lse, *bufs)
 
 
 def shifted(value, axis, size, shift):
@@ -447,16 +515,19 @@
     )
     shards = [shifted(payloads[s], "y", NY, s) for s in range(1, NY)]
     gathered = lax.all_to_all(packed, "z", 0, 0, tiled=True)
-    own, lse = context_own(ctx_queries, ctx_keys, ctx_values)
-    gathered, own, lse, *shards = lax.optimization_barrier((gathered, own, lse, *shards))
+    own, lse, meta = context_own(ctx_queries, ctx_keys, ctx_values, owner, cache_lengths, block_map)
+    q, ro, rm, rl = line_part(gathered)
+    q, ro, rm, rl, own, lse, meta, *shards = lax.optimization_barrier(
+        (q, ro, rm, rl, own, lse, meta, *shards)
+    )
     shards = [payloads[0]] + shards
+    state = first_part(meta, q, shards)
     shards = shards + [shifted(b, "c", NC, 1) for b in shards]
-    q, ro, rm, rl, meta = line_part(gathered, owner, cache_lengths, block_map)
-    parts = lax.all_to_all(shard_part(meta, q, shards), "z", 0, 0, tiled=True)
+    parts = lax.all_to_all(second_part(meta, q, state, shards), "z", 0, 0, tiled=True)
     merged = lax.all_to_all(merge(meta, parts, ro, rm, rl), "z", 0, 0, tiled=True)
     lines = [merged] + [shifted(merged, "y", NY, s) for s in range(1, NY)]
     everything = lines + [shifted(b, "c", NC, 1) for b in lines]
-    ctx_out = context_far(block_map, ctx_queries, own, lse, everything)
+    ctx_out = context_far(meta, ctx_queries, own, lse, everything)
     mine, *others = project(owner, out_weight, everything)
     total = mine
     for s, part in enumerate(others):

time: 86.6 us -> 81.9 us (0.946)
  local copies, waits for them, and re-layouts: 4.41 us -> 0.03 us
  starting transfers between devices: 39.1 us -> 37.6 us
  waiting for transfers between devices: 1.56 us -> 2.47 us
    unnamed x20 -> x10, local copies, waits for them, and re-layouts: 4.41 us -> 0.03 us
    pallas_call x2 -> x3, Pallas kernels: 5.36 us -> 8.79 us  [the longest x1 5.1 us: context_own(): pl.pallas_call(own_kernel, out_shape=(pltpu.HBM((ROWS, 2048), F32), pltpu...]
    pallas_call x1, Pallas kernels: 2.59 us -> 0.54 us  [line_part(): pl.pallas_call(line_kernel, out_shape=(jax.ShapeDtypeStruct((512, HD), BF...]
    ppermute x17, starting transfers between devices: 30.8 us -> 29.4 us  [shifted(): lax.ppermute(value, axis, [(i, (i + shift) % size) for i in range(size)])]
    all_to_all x1, waiting for transfers between devices: 0.42 us -> 1.41 us  [on_device(): gathered = lax.all_to_all(packed, 'z', 0, 0, tiled=True)]
  transfers between devices with their start and end apart: 18 -> 18, of which waited for: 3 -> 2; matrix products, arithmetic and copies ran while one was open for 0% -> 0% of each run, Pallas kernels for 9% -> 13%
where the time goes in v2:
time: 81.9 us; the launch traced here: 81.6 us
  starting transfers between devices  37.6 us (46%)
  blocking collectives  23.3 us (28%)
  Pallas kernels  16.7 us (20%)
  waiting for transfers between devices  2.47 us (3%)
    ppermute x17, starting transfers between devices, shifted(): lax.ppermute(value, axis, [(i, (i + shift) % size) for i in range(size)])  29.4 us
    all_to_all x1, blocking collectives, on_device(): lax.all_to_all(second_part(meta, q, state, shards), 'z', 0, 0, tiled=True)  12.6 us
    all_to_all x1, blocking collectives, on_device(): lax.all_to_all(merge(meta, parts, ro, rm, rl), 'z', 0, 0, tiled=True)  10.8 us
    all_to_all x1, starting transfers between devices, on_device(): gathered = lax.all_to_all(packed, 'z', 0, 0, tiled=True)  8.19 us
    pallas_call x1, Pallas kernels, context_own(): pl.pallas_call(own_kernel, out_shape=(pltpu.HBM((ROWS, 2048), F32), pltpu...  5.1 us
    pallas_call x1, Pallas kernels, context_far(): pl.pallas_call(far_kernel, out_shape=jax.ShapeDtypeStruct((ROWS, 2048), B...  3.34 us
    pallas_call x1, Pallas kernels, second_part(): pl.pallas_call(second_kernel, out_shape=jax.ShapeDtypeStruct((NZ, 96, HD)...  2.01 us
    pallas_call x1, Pallas kernels, prep(): pl.pallas_call(prep_kernel, out_shape=(jax.ShapeDtypeStruct((NZ, 80, HD),...  1.96 us
  transfers between devices with their start and end apart: 18, of which 2 were waited for; matrix products, arithmetic and copies ran while one was open for 0% of the time, Pallas kernels for 13%

profile of v2, /device:TPU:1, one launch (start us, length us, event | category | flops | bytes accessed | tf_op | source)
XLA Modules:
  0.0 81.6 jit_solution(449702629607993706)
XLA Ops:
  0.6 2.0 %prep.1 = (bf16[8,80,128]{2,1,0:T(8,128)(2,1)}, bf16[640,256]{1,0:T(8,128)(2,1)S(1)}, bf16[640,256]{1,0:T(8,128)(2,1)S(1)}, bf16[640,256]{1,0:T(8,128)(2,1)S(1)}, bf16[640,256]{1,0:T(8,128)(2,1)S(1)}) custom-call(bf16[4,2048]{1,0:T(4,128)(2,1)} %bitcast.4, bf16[4,256]{1,0:T(4,128)(2,1)} %bitcast.6, bf16[4,256]{1,0:T(4,128)(2,1)} %bitcast.7, ...), custom_call_target="tpu_custom_call" | custom-call | flops 1048576 | bytes 1048576 | tf_op jit(solution)/shard_map/prep/pallas_call | solution.py:88
  2.6 2.2 %collective-permute-start = (bf16[640,256]{1,0:T(8,128)(2,1)S(1)}, bf16[640,256]{1,0:T(8,128)(2,1)S(1)}, u32[]{:S(2)}, u32[]{:S(2)}) collective-permute-start(bf16[640,256]{1,0:T(8,128)(2,1)S(1)} %get-tuple-element.39), channel_id=1, source_target_pairs={{0,8},{8,16},{16,24},{24,0},{1,9},{9,17},{17,25},{25,1},{2,10},{10... | collective-permute-start | bytes 983048 | tf_op jit(solution)/shard_map/ppermute | solution.py:490
  4.8 2.6 %collective-permute-start.1 = (bf16[640,256]{1,0:T(8,128)(2,1)S(1)}, bf16[640,256]{1,0:T(8,128)(2,1)S(1)}, u32[]{:S(2)}, u32[]{:S(2)}) collective-permute-start(bf16[640,256]{1,0:T(8,128)(2,1)S(1)} %get-tuple-element.40), channel_id=1, source_target_pairs={{0,16},{8,24},{16,0},{24,8},{1,17},{9,25},{17,1},{25,9},{2,18},{10... | collective-permute-start | bytes 983048 | tf_op jit(solution)/shard_map/ppermute | solution.py:490
  7.4 1.1 %collective-permute-start.2 = (bf16[640,256]{1,0:T(8,128)(2,1)S(1)}, bf16[640,256]{1,0:T(8,128)(2,1)S(1)}, u32[]{:S(2)}, u32[]{:S(2)}) collective-permute-start(bf16[640,256]{1,0:T(8,128)(2,1)S(1)} %get-tuple-element.41), channel_id=1, source_target_pairs={{0,24},{8,0},{16,8},{24,16},{1,25},{9,1},{17,9},{25,17},{2,26},{10... | collective-permute-start | bytes 983048 | tf_op jit(solution)/shard_map/ppermute | solution.py:490
  8.5 8.2 %all-to-all-start = ((bf16[8,80,128]{2,1,0:T(8,128)(2,1)}), bf16[8,80,128]{2,1,0:T(8,128)(2,1)S(1)}, u32[]{:S(2)}, u32[]{:S(2)}) async-start(bf16[8,80,128]{2,1,0:T(8,128)(2,1)} %get-tuple-element.31), calls=%async_computation | async-start | bytes 327680 | tf_op jit(solution)/shard_map/all_to_all | solution.py:517
  16.7 1.8 %collective-permute-start.3 = (bf16[640,256]{1,0:T(8,128)(2,1)S(1)}, bf16[640,256]{1,0:T(8,128)(2,1)S(1)}, u32[]{:S(2)}, u32[]{:S(2)}) collective-permute-start(bf16[640,256]{1,0:T(8,128)(2,1)S(1)} %get-tuple-element.46.refs_0_), channel_id=1, source_target_pairs={{0,4},{4,0},{1,5},{5,1},{2,6},{6,2},{3,7},{7,3},{8,12},{12,8},{9,1... | collective-permute-start | bytes 983048 | tf_op jit(solution)/shard_map/ppermute | solution.py:490
  18.5 5.1 %context_own.1 = (f32[256,2048]{1,0:T(8,128)}, f32[256,2048]{1,0:T(8,128)}, s32[16]{0:T(128)S(1)}) custom-call(bf16[256,2048]{1,0:T(8,128)(2,1)} %q.3, bf16[256,256]{1,0:T(8,128)(2,1)} %xk.3, bf16[256,256]{1,0:T(8,128)(2,1)} %xv.3, s32[64]{0:T(128)} %owner.3, s32[64]{0:T(128)} %lengths.1, s32[64]{0:T(128)} %blocks.1), custom_call_target="tpu_custom_call" | custom-call | flops 1073741824 | bytes 6291456 | tf_op jit(solution)/shard_map/context_own/pallas_call | solution.py:404
  23.6 1.4 %all-to-all-done.g = bf16[8,80,128]{2,1,0:T(8,128)(2,1)S(1)} async-done(((bf16[8,80,128]{2,1,0:T(8,128)(2,1)}), bf16[8,80,128]{2,1,0:T(8,128)(2,1)S(1)}, u32[]{:S(2)}, u32[]{:S(2)}) %all-to-all-start) | async-done | bytes 163872 | tf_op jit(solution)/shard_map/all_to_all | solution.py:517
  25.0 0.5 line_part.1
  25.6 3.0 %collective-permute-start.4 = (bf16[640,256]{1,0:T(8,128)(2,1)S(1)}, bf16[640,256]{1,0:T(8,128)(2,1)S(1)}, u32[]{:S(2)}, u32[]{:S(2)}) collective-permute-start(bf16[640,256]{1,0:T(8,128)(2,1)S(1)} %collective-permute-done.refs_1_), channel_id=1, source_target_pairs={{0,4},{4,0},{1,5},{5,1},{2,6},{6,2},{3,7},{7,3},{8,12},{12,8},{9,1... | collective-permute-start | bytes 983048 | tf_op jit(solution)/shard_map/ppermute | solution.py:490
  28.6 0.1 collective-permute-start.5
  28.7 0.4 collective-permute-start.6
  29.1 1.7 %first_part.1 = (f32[512,128]{1,0:T(8,128)S(1)}, f32[512,128]{1,0:T(8,128)S(1)}, f32[512,128]{1,0:T(8,128)S(1)}) custom-call(s32[16]{0:T(128)S(1)} %get-tuple-element.42.meta, bf16[512,128]{1,0:T(8,128)(2,1)S(1)} %get-tuple-element.45.q, bf16[640,256]{1,0:T(8,128)(2,1)S(1)} %get-tuple-element.46.refs_0_, bf16[640,256]{1,0:T(8,128)(2,1)S(1)} %collective-permute-done.refs_1_, ...), custom_call_target="tpu_custom_call" | custom-call | flops 536870912 | bytes 2097152 | tf_op jit(solution)/shard_map/first_part/pallas_call | solution.py:191
  30.8 0.0 copy-start.3
  30.8 2.0 %second_part.1 = bf16[8,96,128]{2,1,0:T(8,128)(2,1)S(1)} custom-call(s32[16]{0:T(128)S(1)} %get-tuple-element.42.meta, bf16[512,128]{1,0:T(8,128)(2,1)S(1)} %get-tuple-element.45.q, f32[512,128]{1,0:T(8,128)S(1)} %get-tuple-element.50.o, f32[512,128]{1,0:T(8,128)S(1)} %get-tuple-element.51.m, f32[512,128]{1,0:T(8,128)S(1)} %get-tuple-element.52.l, ...), custom_call_target="tpu_custom_call" | custom-call | flops 536870912 | bytes 2097152 | tf_op jit(solution)/shard_map/second_part/pallas_call | solution.py:244
  32.9 12.6 %all_to_all.15.parts = bf16[8,96,128]{2,1,0:T(8,128)(2,1)S(1)} all-to-all(bf16[8,96,128]{2,1,0:T(8,128)(2,1)S(1)} %second_part.1), channel_id=1, replica_groups=mesh['z'=8,'y'=4,'c'=2,'x'=4] {'z'}, dimensions={0} | all-to-all | bytes 393216 | tf_op jit(solution)/shard_map/all_to_all | solution.py:526
  45.4 0.9 %merge.1 = bf16[8,80,128]{2,1,0:T(8,128)(2,1)S(1)} custom-call(s32[16]{0:T(128)S(1)} %get-tuple-element.42.meta, bf16[8,96,128]{2,1,0:T(8,128)(2,1)S(1)} %all_to_all.15.parts, f32[64,128]{1,0:T(8,128)S(1)} %get-tuple-element.53.ro, f32[64,128]{1,0:T(8,128)S(1)} %get-tuple-element.54.rm, f32[64,128]{1,0:T(8,128)S(1)} %get-tuple-element.55.rl), custom_call_target="tpu_custom_call" | custom-call | flops 1048576 | bytes 524288 | tf_op jit(solution)/shard_map/merge/pallas_call | solution.py:281
  46.4 10.8 %all_to_all.16.refs_0_ = bf16[8,80,128]{2,1,0:T(8,128)(2,1)S(1)} all-to-all(bf16[8,80,128]{2,1,0:T(8,128)(2,1)S(1)} %merge.1), channel_id=1, replica_groups=mesh['z'=8,'y'=4,'c'=2,'x'=4] {'z'}, dimensions={0} | all-to-all | bytes 327680 | tf_op jit(solution)/shard_map/all_to_all | solution.py:527
  57.1 1.6 %collective-permute-start.9 = (bf16[8,80,128]{2,1,0:T(8,128)(2,1)S(1)}, bf16[8,80,128]{2,1,0:T(8,128)(2,1)S(1)}, u32[]{:S(2)}, u32[]{:S(2)}) collective-permute-start(bf16[8,80,128]{2,1,0:T(8,128)(2,1)S(1)} %all_to_all.16.refs_0_), channel_id=1, source_target_pairs={{0,24},{8,0},{16,8},{24,16},{1,25},{9,1},{17,9},{25,17},{2,26},{10... | collective-permute-start | bytes 491528 | tf_op jit(solution)/shard_map/ppermute | solution.py:490
  58.7 0.9 %collective-permute-start.8 = (bf16[8,80,128]{2,1,0:T(8,128)(2,1)S(1)}, bf16[8,80,128]{2,1,0:T(8,128)(2,1)S(1)}, u32[]{:S(2)}, u32[]{:S(2)}) collective-permute-start(bf16[8,80,128]{2,1,0:T(8,128)(2,1)S(1)} %all_to_all.16.refs_0_), channel_id=1, source_target_pairs={{0,16},{8,24},{16,0},{24,8},{1,17},{9,25},{17,1},{25,9},{2,18},{10... | collective-permute-start | bytes 491528 | tf_op jit(solution)/shard_map/ppermute | solution.py:490
  59.6 0.4 collective-permute-start.7
  60.0 3.7 %collective-permute-start.10 = (bf16[8,80,128]{2,1,0:T(8,128)(2,1)S(1)}, bf16[8,80,128]{2,1,0:T(8,128)(2,1)S(1)}, u32[]{:S(2)}, u32[]{:S(2)}) collective-permute-start(bf16[8,80,128]{2,1,0:T(8,128)(2,1)S(1)} %all_to_all.16.refs_0_), channel_id=1, source_target_pairs={{0,4},{4,0},{1,5},{5,1},{2,6},{6,2},{3,7},{7,3},{8,12},{12,8},{9,1... | collective-permute-start | bytes 491528 | tf_op jit(solution)/shard_map/ppermute | solution.py:490
  63.7 2.9 %collective-permute-start.13 = (bf16[8,80,128]{2,1,0:T(8,128)(2,1)S(1)}, bf16[8,80,128]{2,1,0:T(8,128)(2,1)S(1)}, u32[]{:S(2)}, u32[]{:S(2)}) collective-permute-start(bf16[8,80,128]{2,1,0:T(8,128)(2,1)S(1)} %collective-permute-done.9.refs_3_), channel_id=1, source_target_pairs={{0,4},{4,0},{1,5},{5,1},{2,6},{6,2},{3,7},{7,3},{8,12},{12,8},{9,1... | collective-permute-start | bytes 491528 | tf_op jit(solution)/shard_map/ppermute | solution.py:490
  66.7 2.1 %collective-permute-start.12 = (bf16[8,80,128]{2,1,0:T(8,128)(2,1)S(1)}, bf16[8,80,128]{2,1,0:T(8,128)(2,1)S(1)}, u32[]{:S(2)}, u32[]{:S(2)}) collective-permute-start(bf16[8,80,128]{2,1,0:T(8,128)(2,1)S(1)} %collective-permute-done.8.refs_2_), channel_id=1, source_target_pairs={{0,4},{4,0},{1,5},{5,1},{2,6},{6,2},{3,7},{7,3},{8,12},{12,8},{9,1... | collective-permute-start | bytes 491528 | tf_op jit(solution)/shard_map/ppermute | solution.py:490
  68.8 1.7 %collective-permute-start.11 = (bf16[8,80,128]{2,1,0:T(8,128)(2,1)S(1)}, bf16[8,80,128]{2,1,0:T(8,128)(2,1)S(1)}, u32[]{:S(2)}, u32[]{:S(2)}) collective-permute-start(bf16[8,80,128]{2,1,0:T(8,128)(2,1)S(1)} %collective-permute-done.7.refs_1_), channel_id=1, source_target_pairs={{0,4},{4,0},{1,5},{5,1},{2,6},{6,2},{3,7},{7,3},{8,12},{12,8},{9,1... | collective-permute-start | bytes 491528 | tf_op jit(solution)/shard_map/ppermute | solution.py:490
  70.5 1.0 %collective-permute-done.11.refs_5_ = bf16[8,80,128]{2,1,0:T(8,128)(2,1)S(1)} collective-permute-done((bf16[8,80,128]{2,1,0:T(8,128)(2,1)S(1)}, bf16[8,80,128]{2,1,0:T(8,128)(2,1)S(1)}, u32[]{:S(2)}, u32[]{:S(2)}) %collective-permute-start.11) | collective-permute-done | bytes 163872 | tf_op jit(solution)/shard_map/ppermute | solution.py:490
  71.5 1.2 %project.1 = (f32[64,128]{1,0:T(8,128)S(1)}, f32[64,128]{1,0:T(8,128)S(1)}, f32[64,128]{1,0:T(8,128)S(1)}, f32[64,128]{1,0:T(8,128)S(1)}) custom-call(s32[64]{0:T(128)S(1)} %copy-done.4, bf16[2048,128]{1,0:T(8,128)(2,1)S(1)} %copy-done.3, bf16[8,80,128]{2,1,0:T(8,128)(2,1)S(1)} %all_to_all.16.refs_0_, ...), custom_call_target="tpu_custom_call" | custom-call | flops 268435456 | bytes 2097152 | tf_op jit(solution)/shard_map/project/pallas_call | solution.py:325
  72.7 1.3 %collective-permute-start.14 = (f32[64,128]{1,0:T(8,128)S(1)}, f32[64,128]{1,0:T(8,128)S(1)}, u32[]{:S(2)}, u32[]{:S(2)}) collective-permute-start(f32[64,128]{1,0:T(8,128)S(1)} %get-tuple-element.57), channel_id=1, source_target_pairs={{0,1},{1,2},{2,3},{3,0},{4,5},{5,6},{6,7},{7,4},{8,9},{9,10},{10,1... | collective-permute-start | bytes 98312 | tf_op jit(solution)/shard_map/ppermute | solution.py:490
  74.0 2.5 %collective-permute-start.15 = (f32[64,128]{1,0:T(8,128)S(1)}, f32[64,128]{1,0:T(8,128)S(1)}, u32[]{:S(2)}, u32[]{:S(2)}) collective-permute-start(f32[64,128]{1,0:T(8,128)S(1)} %get-tuple-element.58), channel_id=1, source_target_pairs={{0,2},{1,3},{2,0},{3,1},{4,6},{5,7},{6,4},{7,5},{8,10},{9,11},{10,... | collective-permute-start | bytes 98312 | tf_op jit(solution)/shard_map/ppermute | solution.py:490
  76.4 1.2 %collective-permute-start.16 = (f32[64,128]{1,0:T(8,128)S(1)}, f32[64,128]{1,0:T(8,128)S(1)}, u32[]{:S(2)}, u32[]{:S(2)}) collective-permute-start(f32[64,128]{1,0:T(8,128)S(1)} %get-tuple-element.59), channel_id=1, source_target_pairs={{0,3},{1,0},{2,1},{3,2},{4,7},{5,4},{6,5},{7,6},{8,11},{9,8},{10,9... | collective-permute-start | bytes 98312 | tf_op jit(solution)/shard_map/ppermute | solution.py:490
  77.6 3.3 %context_far.1 = bf16[256,2048]{1,0:T(8,128)(2,1)} custom-call(s32[16]{0:T(128)S(1)} %get-tuple-element.42.meta, bf16[256,2048]{1,0:T(8,128)(2,1)S(1)} %copy-done.2, f32[256,2048]{1,0:T(8,128)S(1)} %copy-done, f32[256,2048]{1,0:T(8,128)S(1)} %copy-done.1, bf16[8,80,128]{2,1,0:T(8,128)(2,1)S(1)} %all_to_all.16.refs_0_, ...), custom_call_target="tpu_custom_call" | custom-call | flops 1073741824 | bytes 6291456 | tf_op jit(solution)/shard_map/context_far/pallas_call | solution.py:472
  81.0 0.6 add_convert_fusion
  (25 shorter events, 0.1 us)
Async XLA Ops:
  2.6 22.9 %collective-permute-start = (bf16[640,256]{1,0:T(8,128)(2,1)S(1)}, bf16[640,256]{1,0:T(8,128)(2,1)S(1)}, u32[]{:S(2)}, u32[]{:S(2)}) collective-permute-start(bf16[640,256]{1,0:T(8,128)(2,1)S(1)} %get-tuple-element.39), channel_id=1, source_target_pairs={{0,8},{8,16},{16,24},{24,0},{1,9},{9,17},{17,25},{25,1},{2,10},{10... | collective-permute-start | bytes 983048 | tf_op jit(solution)/shard_map/ppermute | solution.py:490
  4.8 20.7 %collective-permute-start.1 = (bf16[640,256]{1,0:T(8,128)(2,1)S(1)}, bf16[640,256]{1,0:T(8,128)(2,1)S(1)}, u32[]{:S(2)}, u32[]{:S(2)}) collective-permute-start(bf16[640,256]{1,0:T(8,128)(2,1)S(1)} %get-tuple-element.40), channel_id=1, source_target_pairs={{0,16},{8,24},{16,0},{24,8},{1,17},{9,25},{17,1},{25,9},{2,18},{10... | collective-permute-start | bytes 983048 | tf_op jit(solution)/shard_map/ppermute | solution.py:490
  7.4 18.1 %collective-permute-start.2 = (bf16[640,256]{1,0:T(8,128)(2,1)S(1)}, bf16[640,256]{1,0:T(8,128)(2,1)S(1)}, u32[]{:S(2)}, u32[]{:S(2)}) collective-permute-start(bf16[640,256]{1,0:T(8,128)(2,1)S(1)} %get-tuple-element.41), channel_id=1, source_target_pairs={{0,24},{8,0},{16,8},{24,16},{1,25},{9,1},{17,9},{25,17},{2,26},{10... | collective-permute-start | bytes 983048 | tf_op jit(solution)/shard_map/ppermute | solution.py:490
  8.5 16.5 %all-to-all-start = ((bf16[8,80,128]{2,1,0:T(8,128)(2,1)}), bf16[8,80,128]{2,1,0:T(8,128)(2,1)S(1)}, u32[]{:S(2)}, u32[]{:S(2)}) async-start(bf16[8,80,128]{2,1,0:T(8,128)(2,1)} %get-tuple-element.31), calls=%async_computation | async-start | bytes 327680 | tf_op jit(solution)/shard_map/all_to_all | solution.py:517
  16.7 14.1 %collective-permute-start.3 = (bf16[640,256]{1,0:T(8,128)(2,1)S(1)}, bf16[640,256]{1,0:T(8,128)(2,1)S(1)}, u32[]{:S(2)}, u32[]{:S(2)}) collective-permute-start(bf16[640,256]{1,0:T(8,128)(2,1)S(1)} %get-tuple-element.46.refs_0_), channel_id=1, source_target_pairs={{0,4},{4,0},{1,5},{5,1},{2,6},{6,2},{3,7},{7,3},{8,12},{12,8},{9,1... | collective-permute-start | bytes 983048 | tf_op jit(solution)/shard_map/ppermute | solution.py:490
  25.6 5.2 %collective-permute-start.4 = (bf16[640,256]{1,0:T(8,128)(2,1)S(1)}, bf16[640,256]{1,0:T(8,128)(2,1)S(1)}, u32[]{:S(2)}, u32[]{:S(2)}) collective-permute-start(bf16[640,256]{1,0:T(8,128)(2,1)S(1)} %collective-permute-done.refs_1_), channel_id=1, source_target_pairs={{0,4},{4,0},{1,5},{5,1},{2,6},{6,2},{3,7},{7,3},{8,12},{12,8},{9,1... | collective-permute-start | bytes 983048 | tf_op jit(solution)/shard_map/ppermute | solution.py:490
  28.6 2.2 %collective-permute-start.5 = (bf16[640,256]{1,0:T(8,128)(2,1)S(1)}, bf16[640,256]{1,0:T(8,128)(2,1)S(1)}, u32[]{:S(2)}, u32[]{:S(2)}) collective-permute-start(bf16[640,256]{1,0:T(8,128)(2,1)S(1)} %collective-permute-done.1.refs_2_), channel_id=1, source_target_pairs={{0,4},{4,0},{1,5},{5,1},{2,6},{6,2},{3,7},{7,3},{8,12},{12,8},{9,1... | collective-permute-start | bytes 983048 | tf_op jit(solution)/shard_map/ppermute | solution.py:490
  28.7 2.1 %collective-permute-start.6 = (bf16[640,256]{1,0:T(8,128)(2,1)S(1)}, bf16[640,256]{1,0:T(8,128)(2,1)S(1)}, u32[]{:S(2)}, u32[]{:S(2)}) collective-permute-start(bf16[640,256]{1,0:T(8,128)(2,1)S(1)} %collective-permute-done.2.refs_3_), channel_id=1, source_target_pairs={{0,4},{4,0},{1,5},{5,1},{2,6},{6,2},{3,7},{7,3},{8,12},{12,8},{9,1... | collective-permute-start | bytes 983048 | tf_op jit(solution)/shard_map/ppermute | solution.py:490
  30.8 40.7 %copy-start.3 = (bf16[2048,128]{1,0:T(8,128)(2,1)S(1)}, bf16[2048,128]{1,0:T(8,128)(2,1)}, u32[]{:S(2)}) copy-start(bf16[2048,128]{1,0:T(8,128)(2,1)} %w.1) | copy-start | bytes 1572868
  30.8 40.7 %copy-start.4 = (s32[64]{0:T(128)S(1)}, s32[64]{0:T(128)}, u32[]{:S(2)}) copy-start(s32[64]{0:T(128)} %owner.3) | copy-start | bytes 772
  30.8 46.8 %copy-start.1 = (f32[256,2048]{1,0:T(8,128)S(1)}, f32[256,2048]{1,0:T(8,128)}, u32[]{:S(2)}) copy-start(f32[256,2048]{1,0:T(8,128)} %get-tuple-element.44.lse) | copy-start | bytes 6291460
  30.8 46.8 %copy-start.2 = (bf16[256,2048]{1,0:T(8,128)(2,1)S(1)}, bf16[256,2048]{1,0:T(8,128)(2,1)}, u32[]{:S(2)}) copy-start(bf16[256,2048]{1,0:T(8,128)(2,1)} %q.3) | copy-start | bytes 3145732
  32.9 44.7 %copy-start = (f32[256,2048]{1,0:T(8,128)S(1)}, f32[256,2048]{1,0:T(8,128)}, u32[]{:S(2)}) copy-start(f32[256,2048]{1,0:T(8,128)} %get-tuple-element.43.own) | copy-start | bytes 6291460
  57.1 6.6 %collective-permute-start.9 = (bf16[8,80,128]{2,1,0:T(8,128)(2,1)S(1)}, bf16[8,80,128]{2,1,0:T(8,128)(2,1)S(1)}, u32[]{:S(2)}, u32[]{:S(2)}) collective-permute-start(bf16[8,80,128]{2,1,0:T(8,128)(2,1)S(1)} %all_to_all.16.refs_0_), channel_id=1, source_target_pairs={{0,24},{8,0},{16,8},{24,16},{1,25},{9,1},{17,9},{25,17},{2,26},{10... | collective-permute-start | bytes 491528 | tf_op jit(solution)/shard_map/ppermute | solution.py:490
  58.7 8.0 %collective-permute-start.8 = (bf16[8,80,128]{2,1,0:T(8,128)(2,1)S(1)}, bf16[8,80,128]{2,1,0:T(8,128)(2,1)S(1)}, u32[]{:S(2)}, u32[]{:S(2)}) collective-permute-start(bf16[8,80,128]{2,1,0:T(8,128)(2,1)S(1)} %all_to_all.16.refs_0_), channel_id=1, source_target_pairs={{0,16},{8,24},{16,0},{24,8},{1,17},{9,25},{17,1},{25,9},{2,18},{10... | collective-permute-start | bytes 491528 | tf_op jit(solution)/shard_map/ppermute | solution.py:490
  59.6 9.2 %collective-permute-start.7 = (bf16[8,80,128]{2,1,0:T(8,128)(2,1)S(1)}, bf16[8,80,128]{2,1,0:T(8,128)(2,1)S(1)}, u32[]{:S(2)}, u32[]{:S(2)}) collective-permute-start(bf16[8,80,128]{2,1,0:T(8,128)(2,1)S(1)} %all_to_all.16.refs_0_), channel_id=1, source_target_pairs={{0,8},{8,16},{16,24},{24,0},{1,9},{9,17},{17,25},{25,1},{2,10},{10... | collective-permute-start | bytes 491528 | tf_op jit(solution)/shard_map/ppermute | solution.py:490
  60.0 10.5 %collective-permute-start.10 = (bf16[8,80,128]{2,1,0:T(8,128)(2,1)S(1)}, bf16[8,80,128]{2,1,0:T(8,128)(2,1)S(1)}, u32[]{:S(2)}, u32[]{:S(2)}) collective-permute-start(bf16[8,80,128]{2,1,0:T(8,128)(2,1)S(1)} %all_to_all.16.refs_0_), channel_id=1, source_target_pairs={{0,4},{4,0},{1,5},{5,1},{2,6},{6,2},{3,7},{7,3},{8,12},{12,8},{9,1... | collective-permute-start | bytes 491528 | tf_op jit(solution)/shard_map/ppermute | solution.py:490
  63.7 6.8 %collective-permute-start.13 = (bf16[8,80,128]{2,1,0:T(8,128)(2,1)S(1)}, bf16[8,80,128]{2,1,0:T(8,128)(2,1)S(1)}, u32[]{:S(2)}, u32[]{:S(2)}) collective-permute-start(bf16[8,80,128]{2,1,0:T(8,128)(2,1)S(1)} %collective-permute-done.9.refs_3_), channel_id=1, source_target_pairs={{0,4},{4,0},{1,5},{5,1},{2,6},{6,2},{3,7},{7,3},{8,12},{12,8},{9,1... | collective-permute-start | bytes 491528 | tf_op jit(solution)/shard_map/ppermute | solution.py:490
  66.7 3.8 %collective-permute-start.12 = (bf16[8,80,128]{2,1,0:T(8,128)(2,1)S(1)}, bf16[8,80,128]{2,1,0:T(8,128)(2,1)S(1)}, u32[]{:S(2)}, u32[]{:S(2)}) collective-permute-start(bf16[8,80,128]{2,1,0:T(8,128)(2,1)S(1)} %collective-permute-done.8.refs_2_), channel_id=1, source_target_pairs={{0,4},{4,0},{1,5},{5,1},{2,6},{6,2},{3,7},{7,3},{8,12},{12,8},{9,1... | collective-permute-start | bytes 491528 | tf_op jit(solution)/shard_map/ppermute | solution.py:490
  68.8 2.7 %collective-permute-start.11 = (bf16[8,80,128]{2,1,0:T(8,128)(2,1)S(1)}, bf16[8,80,128]{2,1,0:T(8,128)(2,1)S(1)}, u32[]{:S(2)}, u32[]{:S(2)}) collective-permute-start(bf16[8,80,128]{2,1,0:T(8,128)(2,1)S(1)} %collective-permute-done.7.refs_1_), channel_id=1, source_target_pairs={{0,4},{4,0},{1,5},{5,1},{2,6},{6,2},{3,7},{7,3},{8,12},{12,8},{9,1... | collective-permute-start | bytes 491528 | tf_op jit(solution)/shard_map/ppermute | solution.py:490
  72.7 8.3 %collective-permute-start.14 = (f32[64,128]{1,0:T(8,128)S(1)}, f32[64,128]{1,0:T(8,128)S(1)}, u32[]{:S(2)}, u32[]{:S(2)}) collective-permute-start(f32[64,128]{1,0:T(8,128)S(1)} %get-tuple-element.57), channel_id=1, source_target_pairs={{0,1},{1,2},{2,3},{3,0},{4,5},{5,6},{6,7},{7,4},{8,9},{9,10},{10,1... | collective-permute-start | bytes 98312 | tf_op jit(solution)/shard_map/ppermute | solution.py:490
  74.0 7.0 %collective-permute-start.15 = (f32[64,128]{1,0:T(8,128)S(1)}, f32[64,128]{1,0:T(8,128)S(1)}, u32[]{:S(2)}, u32[]{:S(2)}) collective-permute-start(f32[64,128]{1,0:T(8,128)S(1)} %get-tuple-element.58), channel_id=1, source_target_pairs={{0,2},{1,3},{2,0},{3,1},{4,6},{5,7},{6,4},{7,5},{8,10},{9,11},{10,... | collective-permute-start | bytes 98312 | tf_op jit(solution)/shard_map/ppermute | solution.py:490
  76.4 4.5 %collective-permute-start.16 = (f32[64,128]{1,0:T(8,128)S(1)}, f32[64,128]{1,0:T(8,128)S(1)}, u32[]{:S(2)}, u32[]{:S(2)}) collective-permute-start(f32[64,128]{1,0:T(8,128)S(1)} %get-tuple-element.59), channel_id=1, source_target_pairs={{0,3},{1,0},{2,1},{3,2},{4,7},{5,4},{6,5},{7,6},{8,11},{9,8},{10,9... | collective-permute-start | bytes 98312 | tf_op jit(solution)/shard_map/ppermute | solution.py:490

commit v3 on v2

--- a/solution.py
+++ b/solution.py
@@ -290,18 +290,8 @@
     )(meta, parts, ro, rm, rl)
 
 
-def project_kernel(owner, w, *refs):
-    bufs, outs = refs[:8], refs[8:12]
+def picks_kernel(owner, out):
     y, c, x = lax.axis_index("y"), lax.axis_index("c"), lax.axis_index("x")
-    total = jnp.zeros((256, HD), F32)
-    for zz in range(NZ):
-        left = jnp.concatenate([b[zz, 0:32, :] for b in bufs], axis=0)
-        right = jnp.concatenate([b[zz, 32:64, :] for b in bufs], axis=0)
-        total = total + dot(
-            jnp.concatenate([left, right], axis=1), w[zz * 256 : (zz + 1) * 256, :]
-        )
-    high = total.astype(BF16)
-    low = (total - high.astype(F32)).astype(BF16)
     col = iota((64, 256), 1)
     buf = col // 32
     slot = (
@@ -312,25 +302,73 @@
     row = iota((64, 256), 0)
     same_step = lax.rem(col, 4) == row // 16
     request = lax.rem(row, 16)
-    for s, out in enumerate(outs):
+    for s in range(NX):
         first = lax.rem(x + s, NX) * 16
         wanted = jnp.zeros((64, 256), jnp.int32)
         for j in range(16):
             wanted = jnp.where(request == j, owner[first + j], wanted)
-        pick = ((wanted == slot) & same_step).astype(F32).astype(BF16)
-        out[...] = dot(pick, high) + dot(pick, low)
-
-
-def project(owner, w, bufs):
+        out[s] = ((wanted == slot) & same_step).astype(F32).astype(BF16)
+
+
+def make_picks(owner):
+    return pl.pallas_call(
+        picks_kernel,
+        out_shape=jax.ShapeDtypeStruct((NX, 64, 256), BF16),
+        in_specs=[SMEM],
+        out_specs=VMEM,
+        compiler_params=params(),
+        cost_estimate=cost(1 << 22, 1 << 18),
+        name="picks",
+    )(owner)
+
+
+def line_product(w, bufs):
+    total = jnp.zeros((128, HD), F32)
+    for zz in range(NZ):
+        left = jnp.concatenate([b[zz, 0:32, :] for b in bufs], axis=0)
+        right = jnp.concatenate([b[zz, 32:64, :] for b in bufs], axis=0)
+        total = total + dot(
+            jnp.concatenate([left, right], axis=1), w[zz * 256 : (zz + 1) * 256, :]
+        )
+    high = total.astype(BF16)
+    return high, (total - high.astype(F32)).astype(BF16)
+
+
+def near_kernel(w, *refs):
+    refs[4][0], refs[4][1] = line_product(w, refs[:4])
+
+
+def project_near(w, bufs):
+    return pl.pallas_call(
+        near_kernel,
+        out_shape=jax.ShapeDtypeStruct((2, 128, HD), BF16),
+        in_specs=[VMEM] * 5,
+        out_specs=VMEM,
+        compiler_params=params(),
+        cost_estimate=cost(1 << 26, 1 << 20),
+        name="project_near",
+    )(w, *bufs)
+
+
+def project_kernel(picks, near, w, *refs):
+    bufs, outs = refs[:4], refs[4:8]
+    high, low = line_product(w, bufs)
+    high = jnp.concatenate([near[0], high], axis=0)
+    low = jnp.concatenate([near[1], low], axis=0)
+    for s, out in enumerate(outs):
+        out[...] = dot(picks[s], high) + dot(picks[s], low)
+
+
+def project(picks, near, w, bufs):
     return pl.pallas_call(
         project_kernel,
         out_shape=(jax.ShapeDtypeStruct((64, HD), F32),) * 4,
-        in_specs=[SMEM] + [VMEM] * 9,
+        in_specs=[VMEM] * 7,
         out_specs=(VMEM,) * 4,
         compiler_params=params(),
-        cost_estimate=cost(1 << 28, 2 << 20),
+        cost_estimate=cost(1 << 27, 2 << 20),
         name="project",
-    )(owner, w, *bufs)
+    )(picks, near, w, *bufs)
 
 
 def find_places(owner, lengths, blocks, meta):
@@ -525,10 +563,13 @@
     shards = shards + [shifted(b, "c", NC, 1) for b in shards]
     parts = lax.all_to_all(second_part(meta, q, state, shards), "z", 0, 0, tiled=True)
     merged = lax.all_to_all(merge(meta, parts, ro, rm, rl), "z", 0, 0, tiled=True)
+    merged, owner = lax.optimization_barrier((merged, owner))
+    picks = make_picks(owner)
     lines = [merged] + [shifted(merged, "y", NY, s) for s in range(1, NY)]
-    everything = lines + [shifted(b, "c", NC, 1) for b in lines]
-    ctx_out = context_far(meta, ctx_queries, own, lse, everything)
-    mine, *others = project(owner, out_weight, everything)
+    swapped = [shifted(b, "c", NC, 1) for b in lines]
+    near = project_near(out_weight, lines)
+    mine, *others = project(picks, near, out_weight, swapped)
+    ctx_out = context_far(meta, ctx_queries, own, lse, lines + swapped)
     total = mine
     for s, part in enumerate(others):
         total = total + shifted(part, "x", NX, s + 1)

time: 81.9 us -> 81.3 us (level)
  waiting for transfers between devices: 2.47 us -> 1.48 us
    ppermute x17, waiting for transfers between devices: 1.06 us -> 0.07 us  [shifted(): lax.ppermute(value, axis, [(i, (i + shift) % size) for i in range(size)])]
    pallas_call x0 -> x2, Pallas kernels: none -> 0.94 us  [the longest x1 0.65 us: make_picks(): pl.pallas_call(picks_kernel, out_shape=jax.ShapeDtypeStruct((NX, 64, 256)...]
  transfers between devices with their start and end apart: 18 -> 18, of which waited for: 2 -> 1; matrix products, arithmetic and copies ran while one was open for 0% -> 0% of each run, Pallas kernels for 13% -> 14%
where the time goes in v3:
time: 81.3 us; the launch traced here: 81 us
  starting transfers between devices  37.6 us (46%)
  blocking collectives  23.5 us (29%)
  Pallas kernels  17 us (21%)
  waiting for transfers between devices  1.48 us (2%)
  between operations  0.85 us (1%)
    ppermute x17, starting transfers between devices, shifted(): lax.ppermute(value, axis, [(i, (i + shift) % size) for i in range(size)])  29.4 us
    all_to_all x1, blocking collectives, on_device(): lax.all_to_all(second_part(meta, q, state, shards), 'z', 0, 0, tiled=True)  12.7 us
    all_to_all x1, blocking collectives, on_device(): lax.all_to_all(merge(meta, parts, ro, rm, rl), 'z', 0, 0, tiled=True)  10.8 us
    all_to_all x1, starting transfers between devices, on_device(): gathered = lax.all_to_all(packed, 'z', 0, 0, tiled=True)  8.19 us
    pallas_call x1, Pallas kernels, context_own(): pl.pallas_call(own_kernel, out_shape=(pltpu.HBM((ROWS, 2048), F32), pltpu...  5.1 us
    pallas_call x1, Pallas kernels, context_far(): pl.pallas_call(far_kernel, out_shape=jax.ShapeDtypeStruct((ROWS, 2048), B...  3.31 us
    pallas_call x1, Pallas kernels, second_part(): pl.pallas_call(second_kernel, out_shape=jax.ShapeDtypeStruct((NZ, 96, HD)...  2.02 us
    pallas_call x1, Pallas kernels, prep(): pl.pallas_call(prep_kernel, out_shape=(jax.ShapeDtypeStruct((NZ, 80, HD),...  1.96 us
  transfers between devices with their start and end apart: 18, of which 1 were waited for; matrix products, arithmetic and copies ran while one was open for 0% of the time, Pallas kernels for 14%

profile of v3, /device:TPU:1, one launch (start us, length us, event | category | flops | bytes accessed | tf_op | source)
XLA Modules:
  0.0 81.0 jit_solution(8948198762030352020)
XLA Ops:
  0.6 2.0 %prep.1 = (bf16[8,80,128]{2,1,0:T(8,128)(2,1)}, bf16[640,256]{1,0:T(8,128)(2,1)S(1)}, bf16[640,256]{1,0:T(8,128)(2,1)S(1)}, bf16[640,256]{1,0:T(8,128)(2,1)S(1)}, bf16[640,256]{1,0:T(8,128)(2,1)S(1)}) custom-call(bf16[4,2048]{1,0:T(4,128)(2,1)} %bitcast.4, bf16[4,256]{1,0:T(4,128)(2,1)} %bitcast.6, bf16[4,256]{1,0:T(4,128)(2,1)} %bitcast.7, ...), custom_call_target="tpu_custom_call" | custom-call | flops 1048576 | bytes 1048576 | tf_op jit(solution)/shard_map/prep/pallas_call | solution.py:88
  2.6 2.2 %collective-permute-start = (bf16[640,256]{1,0:T(8,128)(2,1)S(1)}, bf16[640,256]{1,0:T(8,128)(2,1)S(1)}, u32[]{:S(2)}, u32[]{:S(2)}) collective-permute-start(bf16[640,256]{1,0:T(8,128)(2,1)S(1)} %get-tuple-element.41), channel_id=1, source_target_pairs={{0,8},{8,16},{16,24},{24,0},{1,9},{9,17},{17,25},{25,1},{2,10},{10... | collective-permute-start | bytes 983048 | tf_op jit(solution)/shard_map/ppermute | solution.py:528
  4.8 2.6 %collective-permute-start.1 = (bf16[640,256]{1,0:T(8,128)(2,1)S(1)}, bf16[640,256]{1,0:T(8,128)(2,1)S(1)}, u32[]{:S(2)}, u32[]{:S(2)}) collective-permute-start(bf16[640,256]{1,0:T(8,128)(2,1)S(1)} %get-tuple-element.42), channel_id=1, source_target_pairs={{0,16},{8,24},{16,0},{24,8},{1,17},{9,25},{17,1},{25,9},{2,18},{10... | collective-permute-start | bytes 983048 | tf_op jit(solution)/shard_map/ppermute | solution.py:528
  7.4 1.1 %collective-permute-start.2 = (bf16[640,256]{1,0:T(8,128)(2,1)S(1)}, bf16[640,256]{1,0:T(8,128)(2,1)S(1)}, u32[]{:S(2)}, u32[]{:S(2)}) collective-permute-start(bf16[640,256]{1,0:T(8,128)(2,1)S(1)} %get-tuple-element.43), channel_id=1, source_target_pairs={{0,24},{8,0},{16,8},{24,16},{1,25},{9,1},{17,9},{25,17},{2,26},{10... | collective-permute-start | bytes 983048 | tf_op jit(solution)/shard_map/ppermute | solution.py:528
  8.5 8.2 %all-to-all-start = ((bf16[8,80,128]{2,1,0:T(8,128)(2,1)}), bf16[8,80,128]{2,1,0:T(8,128)(2,1)S(1)}, u32[]{:S(2)}, u32[]{:S(2)}) async-start(bf16[8,80,128]{2,1,0:T(8,128)(2,1)} %get-tuple-element.33), calls=%async_computation | async-start | bytes 327680 | tf_op jit(solution)/shard_map/all_to_all | solution.py:555
  16.7 1.8 %collective-permute-start.3 = (bf16[640,256]{1,0:T(8,128)(2,1)S(1)}, bf16[640,256]{1,0:T(8,128)(2,1)S(1)}, u32[]{:S(2)}, u32[]{:S(2)}) collective-permute-start(bf16[640,256]{1,0:T(8,128)(2,1)S(1)} %get-tuple-element.48.refs_0_), channel_id=1, source_target_pairs={{0,4},{4,0},{1,5},{5,1},{2,6},{6,2},{3,7},{7,3},{8,12},{12,8},{9,1... | collective-permute-start | bytes 983048 | tf_op jit(solution)/shard_map/ppermute | solution.py:528
  18.5 5.1 %context_own.1 = (f32[256,2048]{1,0:T(8,128)}, f32[256,2048]{1,0:T(8,128)}, s32[16]{0:T(128)S(1)}) custom-call(bf16[256,2048]{1,0:T(8,128)(2,1)} %q.3, bf16[256,256]{1,0:T(8,128)(2,1)} %xk.3, bf16[256,256]{1,0:T(8,128)(2,1)} %xv.3, s32[64]{0:T(128)} %owner.2, s32[64]{0:T(128)} %lengths.1, s32[64]{0:T(128)} %blocks.1), custom_call_target="tpu_custom_call" | custom-call | flops 1073741824 | bytes 6291456 | tf_op jit(solution)/shard_map/context_own/pallas_call | solution.py:442
  23.6 1.4 %all-to-all-done.g = bf16[8,80,128]{2,1,0:T(8,128)(2,1)S(1)} async-done(((bf16[8,80,128]{2,1,0:T(8,128)(2,1)}), bf16[8,80,128]{2,1,0:T(8,128)(2,1)S(1)}, u32[]{:S(2)}, u32[]{:S(2)}) %all-to-all-start) | async-done | bytes 163872 | tf_op jit(solution)/shard_map/all_to_all | solution.py:555
  25.0 0.5 line_part.1
  25.6 3.0 %collective-permute-start.4 = (bf16[640,256]{1,0:T(8,128)(2,1)S(1)}, bf16[640,256]{1,0:T(8,128)(2,1)S(1)}, u32[]{:S(2)}, u32[]{:S(2)}) collective-permute-start(bf16[640,256]{1,0:T(8,128)(2,1)S(1)} %collective-permute-done.refs_1_), channel_id=1, source_target_pairs={{0,4},{4,0},{1,5},{5,1},{2,6},{6,2},{3,7},{7,3},{8,12},{12,8},{9,1... | collective-permute-start | bytes 983048 | tf_op jit(solution)/shard_map/ppermute | solution.py:528
  28.6 0.1 collective-permute-start.5
  28.7 0.4 collective-permute-start.6
  29.1 1.7 %first_part.1 = (f32[512,128]{1,0:T(8,128)S(1)}, f32[512,128]{1,0:T(8,128)S(1)}, f32[512,128]{1,0:T(8,128)S(1)}) custom-call(s32[16]{0:T(128)S(1)} %get-tuple-element.44.meta, bf16[512,128]{1,0:T(8,128)(2,1)S(1)} %get-tuple-element.47.q, bf16[640,256]{1,0:T(8,128)(2,1)S(1)} %get-tuple-element.48.refs_0_, bf16[640,256]{1,0:T(8,128)(2,1)S(1)} %collective-permute-done.refs_1_, ...), custom_call_target="tpu_custom_call" | custom-call | flops 536870912 | bytes 2097152 | tf_op jit(solution)/shard_map/first_part/pallas_call | solution.py:191
  30.8 2.0 %second_part.1 = bf16[8,96,128]{2,1,0:T(8,128)(2,1)S(1)} custom-call(s32[16]{0:T(128)S(1)} %get-tuple-element.44.meta, bf16[512,128]{1,0:T(8,128)(2,1)S(1)} %get-tuple-element.47.q, f32[512,128]{1,0:T(8,128)S(1)} %get-tuple-element.52.o, f32[512,128]{1,0:T(8,128)S(1)} %get-tuple-element.53.m, f32[512,128]{1,0:T(8,128)S(1)} %get-tuple-element.54.l, ...), custom_call_target="tpu_custom_call" | custom-call | flops 536870912 | bytes 2097152 | tf_op jit(solution)/shard_map/second_part/pallas_call | solution.py:244
  32.9 12.7 %all_to_all.15.parts = bf16[8,96,128]{2,1,0:T(8,128)(2,1)S(1)} all-to-all(bf16[8,96,128]{2,1,0:T(8,128)(2,1)S(1)} %second_part.1), channel_id=1, replica_groups=mesh['z'=8,'y'=4,'c'=2,'x'=4] {'z'}, dimensions={0} | all-to-all | bytes 393216 | tf_op jit(solution)/shard_map/all_to_all | solution.py:564
  45.6 0.9 %merge.1 = bf16[8,80,128]{2,1,0:T(8,128)(2,1)S(1)} custom-call(s32[16]{0:T(128)S(1)} %get-tuple-element.44.meta, bf16[8,96,128]{2,1,0:T(8,128)(2,1)S(1)} %all_to_all.15.parts, f32[64,128]{1,0:T(8,128)S(1)} %get-tuple-element.55.ro, f32[64,128]{1,0:T(8,128)S(1)} %get-tuple-element.56.rm, f32[64,128]{1,0:T(8,128)S(1)} %get-tuple-element.57.rl), custom_call_target="tpu_custom_call" | custom-call | flops 1048576 | bytes 524288 | tf_op jit(solution)/shard_map/merge/pallas_call | solution.py:281
  46.5 10.8 %all_to_all.16.refs_0_ = bf16[8,80,128]{2,1,0:T(8,128)(2,1)S(1)} all-to-all(bf16[8,80,128]{2,1,0:T(8,128)(2,1)S(1)} %merge.1), channel_id=1, replica_groups=mesh['z'=8,'y'=4,'c'=2,'x'=4] {'z'}, dimensions={0} | all-to-all | bytes 327680 | tf_op jit(solution)/shard_map/all_to_all | solution.py:565
  57.3 1.5 %collective-permute-start.9 = (bf16[8,80,128]{2,1,0:T(8,128)(2,1)S(1)}, bf16[8,80,128]{2,1,0:T(8,128)(2,1)S(1)}, u32[]{:S(2)}, u32[]{:S(2)}) collective-permute-start(bf16[8,80,128]{2,1,0:T(8,128)(2,1)S(1)} %all_to_all.16.refs_0_), channel_id=1, source_target_pairs={{0,24},{8,0},{16,8},{24,16},{1,25},{9,1},{17,9},{25,17},{2,26},{10... | collective-permute-start | bytes 491528 | tf_op jit(solution)/shard_map/ppermute | solution.py:528
  58.8 0.9 %collective-permute-start.8 = (bf16[8,80,128]{2,1,0:T(8,128)(2,1)S(1)}, bf16[8,80,128]{2,1,0:T(8,128)(2,1)S(1)}, u32[]{:S(2)}, u32[]{:S(2)}) collective-permute-start(bf16[8,80,128]{2,1,0:T(8,128)(2,1)S(1)} %all_to_all.16.refs_0_), channel_id=1, source_target_pairs={{0,16},{8,24},{16,0},{24,8},{1,17},{9,25},{17,1},{25,9},{2,18},{10... | collective-permute-start | bytes 491528 | tf_op jit(solution)/shard_map/ppermute | solution.py:528
  59.7 0.4 collective-permute-start.7
  60.1 3.7 %collective-permute-start.10 = (bf16[8,80,128]{2,1,0:T(8,128)(2,1)S(1)}, bf16[8,80,128]{2,1,0:T(8,128)(2,1)S(1)}, u32[]{:S(2)}, u32[]{:S(2)}) collective-permute-start(bf16[8,80,128]{2,1,0:T(8,128)(2,1)S(1)} %all_to_all.16.refs_0_), channel_id=1, source_target_pairs={{0,4},{4,0},{1,5},{5,1},{2,6},{6,2},{3,7},{7,3},{8,12},{12,8},{9,1... | collective-permute-start | bytes 491528 | tf_op jit(solution)/shard_map/ppermute | solution.py:528
  63.9 2.9 %collective-permute-start.13 = (bf16[8,80,128]{2,1,0:T(8,128)(2,1)S(1)}, bf16[8,80,128]{2,1,0:T(8,128)(2,1)S(1)}, u32[]{:S(2)}, u32[]{:S(2)}) collective-permute-start(bf16[8,80,128]{2,1,0:T(8,128)(2,1)S(1)} %collective-permute-done.9.refs_3_), channel_id=1, source_target_pairs={{0,4},{4,0},{1,5},{5,1},{2,6},{6,2},{3,7},{7,3},{8,12},{12,8},{9,1... | collective-permute-start | bytes 491528 | tf_op jit(solution)/shard_map/ppermute | solution.py:528
  66.8 2.1 %collective-permute-start.12 = (bf16[8,80,128]{2,1,0:T(8,128)(2,1)S(1)}, bf16[8,80,128]{2,1,0:T(8,128)(2,1)S(1)}, u32[]{:S(2)}, u32[]{:S(2)}) collective-permute-start(bf16[8,80,128]{2,1,0:T(8,128)(2,1)S(1)} %collective-permute-done.8.refs_2_), channel_id=1, source_target_pairs={{0,4},{4,0},{1,5},{5,1},{2,6},{6,2},{3,7},{7,3},{8,12},{12,8},{9,1... | collective-permute-start | bytes 491528 | tf_op jit(solution)/shard_map/ppermute | solution.py:528
  68.9 1.7 %collective-permute-start.11 = (bf16[8,80,128]{2,1,0:T(8,128)(2,1)S(1)}, bf16[8,80,128]{2,1,0:T(8,128)(2,1)S(1)}, u32[]{:S(2)}, u32[]{:S(2)}) collective-permute-start(bf16[8,80,128]{2,1,0:T(8,128)(2,1)S(1)} %collective-permute-done.7.refs_1_), channel_id=1, source_target_pairs={{0,4},{4,0},{1,5},{5,1},{2,6},{6,2},{3,7},{7,3},{8,12},{12,8},{9,1... | collective-permute-start | bytes 491528 | tf_op jit(solution)/shard_map/ppermute | solution.py:528
  70.6 0.7 picks.1
  71.3 0.3 project_near.1.near
  71.6 0.5 project.1
  72.1 1.3 %collective-permute-start.14 = (f32[64,128]{1,0:T(8,128)S(1)}, f32[64,128]{1,0:T(8,128)S(1)}, u32[]{:S(2)}, u32[]{:S(2)}) collective-permute-start(f32[64,128]{1,0:T(8,128)S(1)} %get-tuple-element.61), channel_id=1, source_target_pairs={{0,1},{1,2},{2,3},{3,0},{4,5},{5,6},{6,7},{7,4},{8,9},{9,10},{10,1... | collective-permute-start | bytes 98312 | tf_op jit(solution)/shard_map/ppermute | solution.py:528
  73.4 2.5 %collective-permute-start.15 = (f32[64,128]{1,0:T(8,128)S(1)}, f32[64,128]{1,0:T(8,128)S(1)}, u32[]{:S(2)}, u32[]{:S(2)}) collective-permute-start(f32[64,128]{1,0:T(8,128)S(1)} %get-tuple-element.62), channel_id=1, source_target_pairs={{0,2},{1,3},{2,0},{3,1},{4,6},{5,7},{6,4},{7,5},{8,10},{9,11},{10,... | collective-permute-start | bytes 98312 | tf_op jit(solution)/shard_map/ppermute | solution.py:528
  75.9 1.2 %collective-permute-start.16 = (f32[64,128]{1,0:T(8,128)S(1)}, f32[64,128]{1,0:T(8,128)S(1)}, u32[]{:S(2)}, u32[]{:S(2)}) collective-permute-start(f32[64,128]{1,0:T(8,128)S(1)} %get-tuple-element.63), channel_id=1, source_target_pairs={{0,3},{1,0},{2,1},{3,2},{4,7},{5,4},{6,5},{7,6},{8,11},{9,8},{10,9... | collective-permute-start | bytes 98312 | tf_op jit(solution)/shard_map/ppermute | solution.py:528
  77.0 3.3 %context_far.1 = bf16[256,2048]{1,0:T(8,128)(2,1)} custom-call(s32[16]{0:T(128)S(1)} %get-tuple-element.44.meta, bf16[256,2048]{1,0:T(8,128)(2,1)S(1)} %copy-done.3, f32[256,2048]{1,0:T(8,128)S(1)} %copy-done.1, f32[256,2048]{1,0:T(8,128)S(1)} %copy-done.2, bf16[8,80,128]{2,1,0:T(8,128)(2,1)S(1)} %all_to_all.16.refs_0_, ...), custom_call_target="tpu_custom_call" | custom-call | flops 1073741824 | bytes 6291456 | tf_op jit(solution)/shard_map/context_far/pallas_call | solution.py:510
  80.4 0.6 add_convert_fusion
  (27 shorter events, 0.1 us)
Async XLA Ops:
  2.6 22.9 %collective-permute-start = (bf16[640,256]{1,0:T(8,128)(2,1)S(1)}, bf16[640,256]{1,0:T(8,128)(2,1)S(1)}, u32[]{:S(2)}, u32[]{:S(2)}) collective-permute-start(bf16[640,256]{1,0:T(8,128)(2,1)S(1)} %get-tuple-element.41), channel_id=1, source_target_pairs={{0,8},{8,16},{16,24},{24,0},{1,9},{9,17},{17,25},{25,1},{2,10},{10... | collective-permute-start | bytes 983048 | tf_op jit(solution)/shard_map/ppermute | solution.py:528
  4.8 20.7 %collective-permute-start.1 = (bf16[640,256]{1,0:T(8,128)(2,1)S(1)}, bf16[640,256]{1,0:T(8,128)(2,1)S(1)}, u32[]{:S(2)}, u32[]{:S(2)}) collective-permute-start(bf16[640,256]{1,0:T(8,128)(2,1)S(1)} %get-tuple-element.42), channel_id=1, source_target_pairs={{0,16},{8,24},{16,0},{24,8},{1,17},{9,25},{17,1},{25,9},{2,18},{10... | collective-permute-start | bytes 983048 | tf_op jit(solution)/shard_map/ppermute | solution.py:528
  7.4 18.1 %collective-permute-start.2 = (bf16[640,256]{1,0:T(8,128)(2,1)S(1)}, bf16[640,256]{1,0:T(8,128)(2,1)S(1)}, u32[]{:S(2)}, u32[]{:S(2)}) collective-permute-start(bf16[640,256]{1,0:T(8,128)(2,1)S(1)} %get-tuple-element.43), channel_id=1, source_target_pairs={{0,24},{8,0},{16,8},{24,16},{1,25},{9,1},{17,9},{25,17},{2,26},{10... | collective-permute-start | bytes 983048 | tf_op jit(solution)/shard_map/ppermute | solution.py:528
  8.5 16.5 %all-to-all-start = ((bf16[8,80,128]{2,1,0:T(8,128)(2,1)}), bf16[8,80,128]{2,1,0:T(8,128)(2,1)S(1)}, u32[]{:S(2)}, u32[]{:S(2)}) async-start(bf16[8,80,128]{2,1,0:T(8,128)(2,1)} %get-tuple-element.33), calls=%async_computation | async-start | bytes 327680 | tf_op jit(solution)/shard_map/all_to_all | solution.py:555
  16.7 14.1 %collective-permute-start.3 = (bf16[640,256]{1,0:T(8,128)(2,1)S(1)}, bf16[640,256]{1,0:T(8,128)(2,1)S(1)}, u32[]{:S(2)}, u32[]{:S(2)}) collective-permute-start(bf16[640,256]{1,0:T(8,128)(2,1)S(1)} %get-tuple-element.48.refs_0_), channel_id=1, source_target_pairs={{0,4},{4,0},{1,5},{5,1},{2,6},{6,2},{3,7},{7,3},{8,12},{12,8},{9,1... | collective-permute-start | bytes 983048 | tf_op jit(solution)/shard_map/ppermute | solution.py:528
  25.6 5.2 %collective-permute-start.4 = (bf16[640,256]{1,0:T(8,128)(2,1)S(1)}, bf16[640,256]{1,0:T(8,128)(2,1)S(1)}, u32[]{:S(2)}, u32[]{:S(2)}) collective-permute-start(bf16[640,256]{1,0:T(8,128)(2,1)S(1)} %collective-permute-done.refs_1_), channel_id=1, source_target_pairs={{0,4},{4,0},{1,5},{5,1},{2,6},{6,2},{3,7},{7,3},{8,12},{12,8},{9,1... | collective-permute-start | bytes 983048 | tf_op jit(solution)/shard_map/ppermute | solution.py:528
  28.6 2.2 %collective-permute-start.5 = (bf16[640,256]{1,0:T(8,128)(2,1)S(1)}, bf16[640,256]{1,0:T(8,128)(2,1)S(1)}, u32[]{:S(2)}, u32[]{:S(2)}) collective-permute-start(bf16[640,256]{1,0:T(8,128)(2,1)S(1)} %collective-permute-done.1.refs_2_), channel_id=1, source_target_pairs={{0,4},{4,0},{1,5},{5,1},{2,6},{6,2},{3,7},{7,3},{8,12},{12,8},{9,1... | collective-permute-start | bytes 983048 | tf_op jit(solution)/shard_map/ppermute | solution.py:528
  28.7 2.1 %collective-permute-start.6 = (bf16[640,256]{1,0:T(8,128)(2,1)S(1)}, bf16[640,256]{1,0:T(8,128)(2,1)S(1)}, u32[]{:S(2)}, u32[]{:S(2)}) collective-permute-start(bf16[640,256]{1,0:T(8,128)(2,1)S(1)} %collective-permute-done.2.refs_3_), channel_id=1, source_target_pairs={{0,4},{4,0},{1,5},{5,1},{2,6},{6,2},{3,7},{7,3},{8,12},{12,8},{9,1... | collective-permute-start | bytes 983048 | tf_op jit(solution)/shard_map/ppermute | solution.py:528
  30.8 39.8 %copy-start.4 = (s32[64]{0:T(128)S(1)}, s32[64]{0:T(128)}, u32[]{:S(2)}) copy-start(s32[64]{0:T(128)} %owner.2) | copy-start | bytes 772
  30.8 40.5 %copy-start = (bf16[2048,128]{1,0:T(8,128)(2,1)S(1)}, bf16[2048,128]{1,0:T(8,128)(2,1)}, u32[]{:S(2)}) copy-start(bf16[2048,128]{1,0:T(8,128)(2,1)} %w.3) | copy-start | bytes 1572868
  30.8 46.2 %copy-start.2 = (f32[256,2048]{1,0:T(8,128)S(1)}, f32[256,2048]{1,0:T(8,128)}, u32[]{:S(2)}) copy-start(f32[256,2048]{1,0:T(8,128)} %get-tuple-element.46.lse) | copy-start | bytes 6291460
  32.8 44.2 %copy-start.1 = (f32[256,2048]{1,0:T(8,128)S(1)}, f32[256,2048]{1,0:T(8,128)}, u32[]{:S(2)}) copy-start(f32[256,2048]{1,0:T(8,128)} %get-tuple-element.45.own) | copy-start | bytes 6291460
  32.9 44.2 %copy-start.3 = (bf16[256,2048]{1,0:T(8,128)(2,1)S(1)}, bf16[256,2048]{1,0:T(8,128)(2,1)}, u32[]{:S(2)}) copy-start(bf16[256,2048]{1,0:T(8,128)(2,1)} %q.3) | copy-start | bytes 3145732
  57.3 6.6 %collective-permute-start.9 = (bf16[8,80,128]{2,1,0:T(8,128)(2,1)S(1)}, bf16[8,80,128]{2,1,0:T(8,128)(2,1)S(1)}, u32[]{:S(2)}, u32[]{:S(2)}) collective-permute-start(bf16[8,80,128]{2,1,0:T(8,128)(2,1)S(1)} %all_to_all.16.refs_0_), channel_id=1, source_target_pairs={{0,24},{8,0},{16,8},{24,16},{1,25},{9,1},{17,9},{25,17},{2,26},{10... | collective-permute-start | bytes 491528 | tf_op jit(solution)/shard_map/ppermute | solution.py:528
  58.8 8.0 %collective-permute-start.8 = (bf16[8,80,128]{2,1,0:T(8,128)(2,1)S(1)}, bf16[8,80,128]{2,1,0:T(8,128)(2,1)S(1)}, u32[]{:S(2)}, u32[]{:S(2)}) collective-permute-start(bf16[8,80,128]{2,1,0:T(8,128)(2,1)S(1)} %all_to_all.16.refs_0_), channel_id=1, source_target_pairs={{0,16},{8,24},{16,0},{24,8},{1,17},{9,25},{17,1},{25,9},{2,18},{10... | collective-permute-start | bytes 491528 | tf_op jit(solution)/shard_map/ppermute | solution.py:528
  59.7 9.2 %collective-permute-start.7 = (bf16[8,80,128]{2,1,0:T(8,128)(2,1)S(1)}, bf16[8,80,128]{2,1,0:T(8,128)(2,1)S(1)}, u32[]{:S(2)}, u32[]{:S(2)}) collective-permute-start(bf16[8,80,128]{2,1,0:T(8,128)(2,1)S(1)} %all_to_all.16.refs_0_), channel_id=1, source_target_pairs={{0,8},{8,16},{16,24},{24,0},{1,9},{9,17},{17,25},{25,1},{2,10},{10... | collective-permute-start | bytes 491528 | tf_op jit(solution)/shard_map/ppermute | solution.py:528
  60.1 11.5 %collective-permute-start.10 = (bf16[8,80,128]{2,1,0:T(8,128)(2,1)S(1)}, bf16[8,80,128]{2,1,0:T(8,128)(2,1)S(1)}, u32[]{:S(2)}, u32[]{:S(2)}) collective-permute-start(bf16[8,80,128]{2,1,0:T(8,128)(2,1)S(1)} %all_to_all.16.refs_0_), channel_id=1, source_target_pairs={{0,4},{4,0},{1,5},{5,1},{2,6},{6,2},{3,7},{7,3},{8,12},{12,8},{9,1... | collective-permute-start | bytes 491528 | tf_op jit(solution)/shard_map/ppermute | solution.py:528
  63.9 7.7 %collective-permute-start.13 = (bf16[8,80,128]{2,1,0:T(8,128)(2,1)S(1)}, bf16[8,80,128]{2,1,0:T(8,128)(2,1)S(1)}, u32[]{:S(2)}, u32[]{:S(2)}) collective-permute-start(bf16[8,80,128]{2,1,0:T(8,128)(2,1)S(1)} %collective-permute-done.9.refs_3_), channel_id=1, source_target_pairs={{0,4},{4,0},{1,5},{5,1},{2,6},{6,2},{3,7},{7,3},{8,12},{12,8},{9,1... | collective-permute-start | bytes 491528 | tf_op jit(solution)/shard_map/ppermute | solution.py:528
  66.8 4.8 %collective-permute-start.12 = (bf16[8,80,128]{2,1,0:T(8,128)(2,1)S(1)}, bf16[8,80,128]{2,1,0:T(8,128)(2,1)S(1)}, u32[]{:S(2)}, u32[]{:S(2)}) collective-permute-start(bf16[8,80,128]{2,1,0:T(8,128)(2,1)S(1)} %collective-permute-done.8.refs_2_), channel_id=1, source_target_pairs={{0,4},{4,0},{1,5},{5,1},{2,6},{6,2},{3,7},{7,3},{8,12},{12,8},{9,1... | collective-permute-start | bytes 491528 | tf_op jit(solution)/shard_map/ppermute | solution.py:528
  68.9 2.7 %collective-permute-start.11 = (bf16[8,80,128]{2,1,0:T(8,128)(2,1)S(1)}, bf16[8,80,128]{2,1,0:T(8,128)(2,1)S(1)}, u32[]{:S(2)}, u32[]{:S(2)}) collective-permute-start(bf16[8,80,128]{2,1,0:T(8,128)(2,1)S(1)} %collective-permute-done.7.refs_1_), channel_id=1, source_target_pairs={{0,4},{4,0},{1,5},{5,1},{2,6},{6,2},{3,7},{7,3},{8,12},{12,8},{9,1... | collective-permute-start | bytes 491528 | tf_op jit(solution)/shard_map/ppermute | solution.py:528
  72.1 8.2 %collective-permute-start.14 = (f32[64,128]{1,0:T(8,128)S(1)}, f32[64,128]{1,0:T(8,128)S(1)}, u32[]{:S(2)}, u32[]{:S(2)}) collective-permute-start(f32[64,128]{1,0:T(8,128)S(1)} %get-tuple-element.61), channel_id=1, source_target_pairs={{0,1},{1,2},{2,3},{3,0},{4,5},{5,6},{6,7},{7,4},{8,9},{9,10},{10,1... | collective-permute-start | bytes 98312 | tf_op jit(solution)/shard_map/ppermute | solution.py:528
  73.4 7.0 %collective-permute-start.15 = (f32[64,128]{1,0:T(8,128)S(1)}, f32[64,128]{1,0:T(8,128)S(1)}, u32[]{:S(2)}, u32[]{:S(2)}) collective-permute-start(f32[64,128]{1,0:T(8,128)S(1)} %get-tuple-element.62), channel_id=1, source_target_pairs={{0,2},{1,3},{2,0},{3,1},{4,6},{5,7},{6,4},{7,5},{8,10},{9,11},{10,... | collective-permute-start | bytes 98312 | tf_op jit(solution)/shard_map/ppermute | solution.py:528
  75.9 4.5 %collective-permute-start.16 = (f32[64,128]{1,0:T(8,128)S(1)}, f32[64,128]{1,0:T(8,128)S(1)}, u32[]{:S(2)}, u32[]{:S(2)}) collective-permute-start(f32[64,128]{1,0:T(8,128)S(1)} %get-tuple-element.63), channel_id=1, source_target_pairs={{0,3},{1,0},{2,1},{3,2},{4,7},{5,4},{6,5},{7,6},{8,11},{9,8},{10,9... | collective-permute-start | bytes 98312 | tf_op jit(solution)/shard_map/ppermute | solution.py:528

commit v4 on v3

--- a/solution.py
+++ b/solution.py
@@ -371,7 +371,13 @@
     )(picks, near, w, *bufs)
 
 
-def find_places(owner, lengths, blocks, meta):
+def places_kernel(*refs):
+    meta, owner, lengths, blocks, sems = refs[3:]
+    copies = [pltpu.make_async_copy(refs[i], refs[4 + i], sems.at[i]) for i in range(3)]
+    for copy in copies:
+        copy.start()
+    for copy in copies:
+        copy.wait()
     z, y, c = lax.axis_index("z"), lax.axis_index("y"), lax.axis_index("c")
     line = y * NC + c
     root = jnp.int32(0)
@@ -385,35 +391,32 @@
     meta[11] = jnp.where(root == z * 8 + line, 1, 0)
 
 
-def own_kernel(
-    q, xk, xv, owner, lengths, blocks, out, lse, meta, values, staged, lse_v, q_v, xk_v, xv_v, owner_s, lengths_s, blocks_s, sems
-):
-    copies = [(xk, xk_v), (xv, xv_v)]
-    for group in range(4):
-        lanes = slice(group * 512, (group + 1) * 512)
-        copies.append((q.at[:, lanes], q_v.at[:, lanes]))
-    copies += [(owner, owner_s), (lengths, lengths_s), (blocks, blocks_s)]
-    copies = [pltpu.make_async_copy(src, dst, sems.at[i]) for i, (src, dst) in enumerate(copies)]
-    for copy in copies:
-        copy.start()
+def find_places(*args):
+    args = [pltpu.with_memory_space_constraint(a, pltpu.HBM) for a in args]
+    return pl.pallas_call(
+        places_kernel,
+        out_shape=jax.ShapeDtypeStruct((16,), jnp.int32),
+        in_specs=[pl.BlockSpec(memory_space=pltpu.HBM)] * 3,
+        out_specs=SMEM,
+        scratch_shapes=[pltpu.SMEM((SLOTS,), jnp.int32)] * 3 + [pltpu.SemaphoreType.DMA((3,))],
+        compiler_params=params(),
+        cost_estimate=cost(1 << 20, 1 << 19),
+        name="places",
+    )(*args)
+
+
+def own_kernel(after, q, xk, xv, out, lse, values):
     causal = iota((128, 128), 0) >= iota((128, 128), 1)
-    results = []
-    for copy in copies[6:]:
-        copy.wait()
-    find_places(owner_s, lengths_s, blocks_s, meta)
-    copies[0].wait()
-    copies[1].wait()
     for k in range(2):
-        values[k, :, 0:HD] = xv_v[:, k * HD : (k + 1) * HD]
+        values[k, :, 0:HD] = xv[:, k * HD : (k + 1) * HD]
         values[k, :, HD:] = jnp.ones((ROWS, HD), BF16)
     for group in range(4):
         units = [(group * 4 + h, half) for h in range(4) for half in range(2)]
         tiles, tops = [], []
-        copies[2 + group].wait()
         for h, half in units:
             near = (half + 1) * 128
-            keys = xk_v[0:near, (h // 8) * HD : (h // 8 + 1) * HD]
-            own = dot(q_v[near - 128 : near, h * HD : (h + 1) * HD], keys, NT)
+            keys = xk[0:near, (h // 8) * HD : (h // 8 + 1) * HD]
+            own = dot(q[near - 128 : near, h * HD : (h + 1) * HD], keys, NT)
             diagonal = jnp.where(causal, own[:, near - 128 :], LOW)
             tiles.append([own[:, :HD], diagonal] if half else [diagonal])
         for parts in tiles:
@@ -426,44 +429,21 @@
             weights = jnp.concatenate(weights, axis=1) if half else weights[0]
             summed = dot(weights, values[h // 8, 0:near, :])
             rows, lanes = slice(near - 128, near), slice(h * HD, (h + 1) * HD)
-            staged[rows, lanes] = summed[:, :HD] / summed[:, HD:]
-            lse_v[rows, lanes] = top + jnp.log2(summed[:, HD:])
-        lanes = slice(group * 512, (group + 1) * 512)
-        for i, (src, dst) in enumerate(((staged, out), (lse_v, lse))):
-            sem = sems.at[9 + group * 2 + i]
-            results.append(pltpu.make_async_copy(src.at[:, lanes], dst.at[:, lanes], sem))
-            results[-1].start()
-    for copy in results:
-        copy.wait()
-
-
-def context_own(*args):
-    args = [pltpu.with_memory_space_constraint(a, pltpu.HBM) for a in args]
+            out[rows, lanes] = summed[:, :HD] / summed[:, HD:]
+            lse[rows, lanes] = top + jnp.log2(summed[:, HD:])
+
+
+def context_own(after, q, xk, xv):
     return pl.pallas_call(
         own_kernel,
-        out_shape=(
-            pltpu.HBM((ROWS, 2048), F32),
-            pltpu.HBM((ROWS, 2048), F32),
-            jax.ShapeDtypeStruct((16,), jnp.int32),
-        ),
-        in_specs=[pl.BlockSpec(memory_space=pltpu.HBM)] * 6,
-        out_specs=(pl.BlockSpec(memory_space=pltpu.HBM),) * 2 + (SMEM,),
-        scratch_shapes=[
-            pltpu.VMEM((2, ROWS, 2 * HD), BF16),
-            pltpu.VMEM((ROWS, 2048), F32),
-            pltpu.VMEM((ROWS, 2048), F32),
-            pltpu.VMEM((ROWS, 2048), BF16),
-            pltpu.VMEM((ROWS, 256), BF16),
-            pltpu.VMEM((ROWS, 256), BF16),
-            pltpu.SMEM((SLOTS,), jnp.int32),
-            pltpu.SMEM((SLOTS,), jnp.int32),
-            pltpu.SMEM((SLOTS,), jnp.int32),
-            pltpu.SemaphoreType.DMA((17,)),
-        ],
+        out_shape=(jax.ShapeDtypeStruct((ROWS, 2048), F32),) * 2,
+        in_specs=[VMEM] * 4,
+        out_specs=(VMEM,) * 2,
+        scratch_shapes=[pltpu.VMEM((2, ROWS, 2 * HD), BF16)],
         compiler_params=params(),
         cost_estimate=cost(1 << 30, 6 << 20, 1 << 20),
         name="context_own",
-    )(*args)
+    )(after, q, xk, xv)
 
 
 def far_kernel(meta, q, own, lse, *refs):
@@ -553,11 +533,9 @@
     )
     shards = [shifted(payloads[s], "y", NY, s) for s in range(1, NY)]
     gathered = lax.all_to_all(packed, "z", 0, 0, tiled=True)
-    own, lse, meta = context_own(ctx_queries, ctx_keys, ctx_values, owner, cache_lengths, block_map)
+    meta = find_places(owner, cache_lengths, block_map)
     q, ro, rm, rl = line_part(gathered)
-    q, ro, rm, rl, own, lse, meta, *shards = lax.optimization_barrier(
-        (q, ro, rm, rl, own, lse, meta, *shards)
-    )
+    q, ro, rm, rl, meta, *shards = lax.optimization_barrier((q, ro, rm, rl, meta, *shards))
     shards = [payloads[0]] + shards
     state = first_part(meta, q, shards)
     shards = shards + [shifted(b, "c", NC, 1) for b in shards]
@@ -565,7 +543,10 @@
     merged = lax.all_to_all(merge(meta, parts, ro, rm, rl), "z", 0, 0, tiled=True)
     merged, owner = lax.optimization_barrier((merged, owner))
     picks = make_picks(owner)
-    lines = [merged] + [shifted(merged, "y", NY, s) for s in range(1, NY)]
+    one, two, three = [shifted(merged, "y", NY, s) for s in range(1, NY)]
+    own, lse = context_own(merged, ctx_queries, ctx_keys, ctx_values)
+    own, lse, one = lax.optimization_barrier((own, lse, one))
+    lines = [merged, one, two, three]
     swapped = [shifted(b, "c", NC, 1) for b in lines]
     near = project_near(out_weight, lines)
     mine, *others = project(picks, near, out_weight, swapped)

time: 81.3 us -> 79.2 us (0.974)
  starting transfers between devices: 37.6 us -> 33.4 us
  waiting for transfers between devices: 1.48 us -> 5.34 us
  Pallas kernels: 17 us -> 15 us
    ppermute x17, starting transfers between devices: 29.4 us -> 25.2 us  [shifted(): lax.ppermute(value, axis, [(i, (i + shift) % size) for i in range(size)])]
    all_to_all x1, waiting for transfers between devices: 1.41 us -> 5.01 us  [on_device(): gathered = lax.all_to_all(packed, 'z', 0, 0, tiled=True)]
    pallas_call x1 -> x2, Pallas kernels: 5.1 us -> 3.2 us  [the longest x1 1.69 us: context_own(): pl.pallas_call(own_kernel, out_shape=(jax.ShapeDtypeStruct((ROWS, 2048),...]
  transfers between devices with their start and end apart: 18 -> 18, of which waited for: 1 -> 3; matrix products, arithmetic and copies ran while one was open for 0% -> 0% of each run, Pallas kernels for 14% -> 12%
where the time goes in v4:
time: 79.2 us; the launch traced here: 78.1 us
  starting transfers between devices  33.4 us (42%)
  blocking collectives  22.9 us (29%)
  Pallas kernels  15 us (19%)
  waiting for transfers between devices  5.34 us (7%)
  between operations  0.85 us (1%)
    ppermute x17, starting transfers between devices, shifted(): lax.ppermute(value, axis, [(i, (i + shift) % size) for i in range(size)])  25.2 us
    all_to_all x1, blocking collectives, on_device(): lax.all_to_all(second_part(meta, q, state, shards), 'z', 0, 0, tiled=True)  12.1 us
    all_to_all x1, blocking collectives, on_device(): lax.all_to_all(merge(meta, parts, ro, rm, rl), 'z', 0, 0, tiled=True)  10.8 us
    all_to_all x1, starting transfers between devices, on_device(): gathered = lax.all_to_all(packed, 'z', 0, 0, tiled=True)  8.19 us
    all_to_all x1, waiting for transfers between devices, on_device(): gathered = lax.all_to_all(packed, 'z', 0, 0, tiled=True)  5.01 us
    pallas_call x1, Pallas kernels, context_far(): pl.pallas_call(far_kernel, out_shape=jax.ShapeDtypeStruct((ROWS, 2048), B...  3.26 us
    pallas_call x1, Pallas kernels, second_part(): pl.pallas_call(second_kernel, out_shape=jax.ShapeDtypeStruct((NZ, 96, HD)...  2.02 us
    pallas_call x1, Pallas kernels, prep(): pl.pallas_call(prep_kernel, out_shape=(jax.ShapeDtypeStruct((NZ, 80, HD),...  1.96 us
  transfers between devices with their start and end apart: 18, of which 3 were waited for; matrix products, arithmetic and copies ran while one was open for 0% of the time, Pallas kernels for 12%

profile of v4, /device:TPU:1, one launch (start us, length us, event | category | flops | bytes accessed | tf_op | source)
XLA Modules:
  0.0 78.1 jit_solution(10299615819345634043)
XLA Ops:
  0.6 2.0 %prep.1 = (bf16[8,80,128]{2,1,0:T(8,128)(2,1)}, bf16[640,256]{1,0:T(8,128)(2,1)S(1)}, bf16[640,256]{1,0:T(8,128)(2,1)S(1)}, bf16[640,256]{1,0:T(8,128)(2,1)S(1)}, bf16[640,256]{1,0:T(8,128)(2,1)S(1)}) custom-call(bf16[4,2048]{1,0:T(4,128)(2,1)} %bitcast.4, bf16[4,256]{1,0:T(4,128)(2,1)} %bitcast.6, bf16[4,256]{1,0:T(4,128)(2,1)} %bitcast.7, ...), custom_call_target="tpu_custom_call" | custom-call | flops 1048576 | bytes 1048576 | tf_op jit(solution)/shard_map/prep/pallas_call | solution.py:88
  2.6 2.2 %collective-permute-start = (bf16[640,256]{1,0:T(8,128)(2,1)S(1)}, bf16[640,256]{1,0:T(8,128)(2,1)S(1)}, u32[]{:S(2)}, u32[]{:S(2)}) collective-permute-start(bf16[640,256]{1,0:T(8,128)(2,1)S(1)} %get-tuple-element.38), channel_id=1, source_target_pairs={{0,8},{8,16},{16,24},{24,0},{1,9},{9,17},{17,25},{25,1},{2,10},{10... | collective-permute-start | bytes 983048 | tf_op jit(solution)/shard_map/ppermute | solution.py:508
  4.8 2.6 %collective-permute-start.1 = (bf16[640,256]{1,0:T(8,128)(2,1)S(1)}, bf16[640,256]{1,0:T(8,128)(2,1)S(1)}, u32[]{:S(2)}, u32[]{:S(2)}) collective-permute-start(bf16[640,256]{1,0:T(8,128)(2,1)S(1)} %get-tuple-element.39), channel_id=1, source_target_pairs={{0,16},{8,24},{16,0},{24,8},{1,17},{9,25},{17,1},{25,9},{2,18},{10... | collective-permute-start | bytes 983048 | tf_op jit(solution)/shard_map/ppermute | solution.py:508
  7.4 1.1 %collective-permute-start.2 = (bf16[640,256]{1,0:T(8,128)(2,1)S(1)}, bf16[640,256]{1,0:T(8,128)(2,1)S(1)}, u32[]{:S(2)}, u32[]{:S(2)}) collective-permute-start(bf16[640,256]{1,0:T(8,128)(2,1)S(1)} %get-tuple-element.40), channel_id=1, source_target_pairs={{0,24},{8,0},{16,8},{24,16},{1,25},{9,1},{17,9},{25,17},{2,26},{10... | collective-permute-start | bytes 983048 | tf_op jit(solution)/shard_map/ppermute | solution.py:508
  8.5 8.2 %all-to-all-start = ((bf16[8,80,128]{2,1,0:T(8,128)(2,1)}), bf16[8,80,128]{2,1,0:T(8,128)(2,1)S(1)}, u32[]{:S(2)}, u32[]{:S(2)}) async-start(bf16[8,80,128]{2,1,0:T(8,128)(2,1)} %get-tuple-element.33), calls=%async_computation | async-start | bytes 327680 | tf_op jit(solution)/shard_map/all_to_all | solution.py:535
  16.7 1.8 %collective-permute-start.3 = (bf16[640,256]{1,0:T(8,128)(2,1)S(1)}, bf16[640,256]{1,0:T(8,128)(2,1)S(1)}, u32[]{:S(2)}, u32[]{:S(2)}) collective-permute-start(bf16[640,256]{1,0:T(8,128)(2,1)S(1)} %get-tuple-element.43.refs_0_), channel_id=1, source_target_pairs={{0,4},{4,0},{1,5},{5,1},{2,6},{6,2},{3,7},{7,3},{8,12},{12,8},{9,1... | collective-permute-start | bytes 983048 | tf_op jit(solution)/shard_map/ppermute | solution.py:508
  18.5 1.5 %places.1.meta = s32[16]{0:T(128)S(1)} custom-call(s32[64]{0:T(128)} %owner, s32[64]{0:T(128)} %refs_1_.1, s32[64]{0:T(128)} %refs_2_.1), custom_call_target="tpu_custom_call" | custom-call | flops 1048576 | bytes 524288 | tf_op jit(solution)/shard_map/places/pallas_call | solution.py:396
  20.0 5.0 %all-to-all-done.g = bf16[8,80,128]{2,1,0:T(8,128)(2,1)S(1)} async-done(((bf16[8,80,128]{2,1,0:T(8,128)(2,1)}), bf16[8,80,128]{2,1,0:T(8,128)(2,1)S(1)}, u32[]{:S(2)}, u32[]{:S(2)}) %all-to-all-start) | async-done | bytes 163872 | tf_op jit(solution)/shard_map/all_to_all | solution.py:535
  25.0 0.5 line_part.1
  25.6 3.0 %collective-permute-start.4 = (bf16[640,256]{1,0:T(8,128)(2,1)S(1)}, bf16[640,256]{1,0:T(8,128)(2,1)S(1)}, u32[]{:S(2)}, u32[]{:S(2)}) collective-permute-start(bf16[640,256]{1,0:T(8,128)(2,1)S(1)} %collective-permute-done.refs_1_), channel_id=1, source_target_pairs={{0,4},{4,0},{1,5},{5,1},{2,6},{6,2},{3,7},{7,3},{8,12},{12,8},{9,1... | collective-permute-start | bytes 983048 | tf_op jit(solution)/shard_map/ppermute | solution.py:508
  28.7 0.4 collective-permute-start.6
  29.1 1.7 %first_part.1 = (f32[512,128]{1,0:T(8,128)S(1)}, f32[512,128]{1,0:T(8,128)S(1)}, f32[512,128]{1,0:T(8,128)S(1)}) custom-call(s32[16]{0:T(128)S(1)} %places.1.meta, bf16[512,128]{1,0:T(8,128)(2,1)S(1)} %get-tuple-element.42.q, bf16[640,256]{1,0:T(8,128)(2,1)S(1)} %get-tuple-element.43.refs_0_, bf16[640,256]{1,0:T(8,128)(2,1)S(1)} %collective-permute-done.refs_1_, ...), custom_call_target="tpu_custom_call" | custom-call | flops 536870912 | bytes 2097152 | tf_op jit(solution)/shard_map/first_part/pallas_call | solution.py:191
  30.8 2.0 %second_part.1 = bf16[8,96,128]{2,1,0:T(8,128)(2,1)S(1)} custom-call(s32[16]{0:T(128)S(1)} %places.1.meta, bf16[512,128]{1,0:T(8,128)(2,1)S(1)} %get-tuple-element.42.q, f32[512,128]{1,0:T(8,128)S(1)} %get-tuple-element.47.o, f32[512,128]{1,0:T(8,128)S(1)} %get-tuple-element.48.m, f32[512,128]{1,0:T(8,128)S(1)} %get-tuple-element.49.l, ...), custom_call_target="tpu_custom_call" | custom-call | flops 536870912 | bytes 2097152 | tf_op jit(solution)/shard_map/second_part/pallas_call | solution.py:244
  32.9 12.1 %all_to_all.15.parts = bf16[8,96,128]{2,1,0:T(8,128)(2,1)S(1)} all-to-all(bf16[8,96,128]{2,1,0:T(8,128)(2,1)S(1)} %second_part.1), channel_id=1, replica_groups=mesh['z'=8,'y'=4,'c'=2,'x'=4] {'z'}, dimensions={0} | all-to-all | bytes 393216 | tf_op jit(solution)/shard_map/all_to_all | solution.py:542
  44.9 0.9 %merge.1 = bf16[8,80,128]{2,1,0:T(8,128)(2,1)S(1)} custom-call(s32[16]{0:T(128)S(1)} %places.1.meta, bf16[8,96,128]{2,1,0:T(8,128)(2,1)S(1)} %all_to_all.15.parts, f32[64,128]{1,0:T(8,128)S(1)} %get-tuple-element.50.ro, f32[64,128]{1,0:T(8,128)S(1)} %get-tuple-element.51.rm, f32[64,128]{1,0:T(8,128)S(1)} %get-tuple-element.52.rl), custom_call_target="tpu_custom_call" | custom-call | flops 1048576 | bytes 524288 | tf_op jit(solution)/shard_map/merge/pallas_call | solution.py:281
  45.9 10.8 %all_to_all.16.after.refs_0_ = bf16[8,80,128]{2,1,0:T(8,128)(2,1)S(1)} all-to-all(bf16[8,80,128]{2,1,0:T(8,128)(2,1)S(1)} %merge.1), channel_id=1, replica_groups=mesh['z'=8,'y'=4,'c'=2,'x'=4] {'z'}, dimensions={0} | all-to-all | bytes 327680 | tf_op jit(solution)/shard_map/all_to_all | solution.py:543
  56.7 1.0 %collective-permute-start.7 = (bf16[8,80,128]{2,1,0:T(8,128)(2,1)S(1)}, bf16[8,80,128]{2,1,0:T(8,128)(2,1)S(1)}, u32[]{:S(2)}, u32[]{:S(2)}) collective-permute-start(bf16[8,80,128]{2,1,0:T(8,128)(2,1)S(1)} %all_to_all.16.after.refs_0_), channel_id=1, source_target_pairs={{0,8},{8,16},{16,24},{24,0},{1,9},{9,17},{17,25},{25,1},{2,10},{10... | collective-permute-start | bytes 491528 | tf_op jit(solution)/shard_map/ppermute | solution.py:508
  57.6 2.1 %collective-permute-start.8 = (bf16[8,80,128]{2,1,0:T(8,128)(2,1)S(1)}, bf16[8,80,128]{2,1,0:T(8,128)(2,1)S(1)}, u32[]{:S(2)}, u32[]{:S(2)}) collective-permute-start(bf16[8,80,128]{2,1,0:T(8,128)(2,1)S(1)} %all_to_all.16.after.refs_0_), channel_id=1, source_target_pairs={{0,16},{8,24},{16,0},{24,8},{1,17},{9,25},{17,1},{25,9},{2,18},{10... | collective-permute-start | bytes 491528 | tf_op jit(solution)/shard_map/ppermute | solution.py:508
  59.8 1.3 %collective-permute-start.9 = (bf16[8,80,128]{2,1,0:T(8,128)(2,1)S(1)}, bf16[8,80,128]{2,1,0:T(8,128)(2,1)S(1)}, u32[]{:S(2)}, u32[]{:S(2)}) collective-permute-start(bf16[8,80,128]{2,1,0:T(8,128)(2,1)S(1)} %all_to_all.16.after.refs_0_), channel_id=1, source_target_pairs={{0,24},{8,0},{16,8},{24,16},{1,25},{9,1},{17,9},{25,17},{2,26},{10... | collective-permute-start | bytes 491528 | tf_op jit(solution)/shard_map/ppermute | solution.py:508
  61.1 3.7 %collective-permute-start.10 = (bf16[8,80,128]{2,1,0:T(8,128)(2,1)S(1)}, bf16[8,80,128]{2,1,0:T(8,128)(2,1)S(1)}, u32[]{:S(2)}, u32[]{:S(2)}) collective-permute-start(bf16[8,80,128]{2,1,0:T(8,128)(2,1)S(1)} %all_to_all.16.after.refs_0_), channel_id=1, source_target_pairs={{0,4},{4,0},{1,5},{5,1},{2,6},{6,2},{3,7},{7,3},{8,12},{12,8},{9,1... | collective-permute-start | bytes 491528 | tf_op jit(solution)/shard_map/ppermute | solution.py:508
  64.8 1.7 %context_own.1 = (f32[256,2048]{1,0:T(8,128)S(1)}, f32[256,2048]{1,0:T(8,128)S(1)}) custom-call(bf16[8,80,128]{2,1,0:T(8,128)(2,1)S(1)} %all_to_all.16.after.refs_0_, bf16[256,2048]{1,0:T(8,128)(2,1)S(1)} %copy-done.1, bf16[256,256]{1,0:T(8,128)(2,1)S(1)} %copy-done.2, bf16[256,256]{1,0:T(8,128)(2,1)S(1)} %copy-done.3), custom_call_target="tpu_custom_call" | custom-call | flops 1073741824 | bytes 6291456 | tf_op jit(solution)/shard_map/context_own/pallas_call | solution.py:437
  66.7 1.8 %collective-permute-start.12 = (bf16[8,80,128]{2,1,0:T(8,128)(2,1)S(1)}, bf16[8,80,128]{2,1,0:T(8,128)(2,1)S(1)}, u32[]{:S(2)}, u32[]{:S(2)}) collective-permute-start(bf16[8,80,128]{2,1,0:T(8,128)(2,1)S(1)} %collective-permute-done.8.refs_2_), channel_id=1, source_target_pairs={{0,4},{4,0},{1,5},{5,1},{2,6},{6,2},{3,7},{7,3},{8,12},{12,8},{9,1... | collective-permute-start | bytes 491528 | tf_op jit(solution)/shard_map/ppermute | solution.py:508
  68.4 0.3 collective-permute-start.13
  68.7 0.7 picks.1
  69.4 0.3 project_near.1.near
  69.8 0.5 project.1
  70.3 2.6 %collective-permute-start.16 = (f32[64,128]{1,0:T(8,128)S(1)}, f32[64,128]{1,0:T(8,128)S(1)}, u32[]{:S(2)}, u32[]{:S(2)}) collective-permute-start(f32[64,128]{1,0:T(8,128)S(1)} %get-tuple-element.63), channel_id=1, source_target_pairs={{0,3},{1,0},{2,1},{3,2},{4,7},{5,4},{6,5},{7,6},{8,11},{9,8},{10,9... | collective-permute-start | bytes 98312 | tf_op jit(solution)/shard_map/ppermute | solution.py:508
  72.9 0.5 collective-permute-start.15
  73.4 0.6 collective-permute-start.14
  74.0 3.3 %context_far.1 = bf16[256,2048]{1,0:T(8,128)(2,1)} custom-call(s32[16]{0:T(128)S(1)} %places.1.meta, bf16[256,2048]{1,0:T(8,128)(2,1)S(1)} %copy-done.1, f32[256,2048]{1,0:T(8,128)S(1)} %get-tuple-element.56.own, f32[256,2048]{1,0:T(8,128)S(1)} %get-tuple-element.57.lse, bf16[8,80,128]{2,1,0:T(8,128)(2,1)S(1)} %all_to_all.16.after.refs_0_, ...), custom_call_target="tpu_custom_call" | custom-call | flops 1073741824 | bytes 6291456 | tf_op jit(solution)/shard_map/context_far/pallas_call | solution.py:490
  77.3 0.2 collective-permute-done.14
  77.5 0.6 add_convert_fusion
  (28 shorter events, 0.4 us)
Async XLA Ops:
  2.6 22.9 %collective-permute-start = (bf16[640,256]{1,0:T(8,128)(2,1)S(1)}, bf16[640,256]{1,0:T(8,128)(2,1)S(1)}, u32[]{:S(2)}, u32[]{:S(2)}) collective-permute-start(bf16[640,256]{1,0:T(8,128)(2,1)S(1)} %get-tuple-element.38), channel_id=1, source_target_pairs={{0,8},{8,16},{16,24},{24,0},{1,9},{9,17},{17,25},{25,1},{2,10},{10... | collective-permute-start | bytes 983048 | tf_op jit(solution)/shard_map/ppermute | solution.py:508
  4.8 20.7 %collective-permute-start.1 = (bf16[640,256]{1,0:T(8,128)(2,1)S(1)}, bf16[640,256]{1,0:T(8,128)(2,1)S(1)}, u32[]{:S(2)}, u32[]{:S(2)}) collective-permute-start(bf16[640,256]{1,0:T(8,128)(2,1)S(1)} %get-tuple-element.39), channel_id=1, source_target_pairs={{0,16},{8,24},{16,0},{24,8},{1,17},{9,25},{17,1},{25,9},{2,18},{10... | collective-permute-start | bytes 983048 | tf_op jit(solution)/shard_map/ppermute | solution.py:508
  7.4 18.1 %collective-permute-start.2 = (bf16[640,256]{1,0:T(8,128)(2,1)S(1)}, bf16[640,256]{1,0:T(8,128)(2,1)S(1)}, u32[]{:S(2)}, u32[]{:S(2)}) collective-permute-start(bf16[640,256]{1,0:T(8,128)(2,1)S(1)} %get-tuple-element.40), channel_id=1, source_target_pairs={{0,24},{8,0},{16,8},{24,16},{1,25},{9,1},{17,9},{25,17},{2,26},{10... | collective-permute-start | bytes 983048 | tf_op jit(solution)/shard_map/ppermute | solution.py:508
  8.5 16.5 %all-to-all-start = ((bf16[8,80,128]{2,1,0:T(8,128)(2,1)}), bf16[8,80,128]{2,1,0:T(8,128)(2,1)S(1)}, u32[]{:S(2)}, u32[]{:S(2)}) async-start(bf16[8,80,128]{2,1,0:T(8,128)(2,1)} %get-tuple-element.33), calls=%async_computation | async-start | bytes 327680 | tf_op jit(solution)/shard_map/all_to_all | solution.py:535
  16.7 14.1 %collective-permute-start.3 = (bf16[640,256]{1,0:T(8,128)(2,1)S(1)}, bf16[640,256]{1,0:T(8,128)(2,1)S(1)}, u32[]{:S(2)}, u32[]{:S(2)}) collective-permute-start(bf16[640,256]{1,0:T(8,128)(2,1)S(1)} %get-tuple-element.43.refs_0_), channel_id=1, source_target_pairs={{0,4},{4,0},{1,5},{5,1},{2,6},{6,2},{3,7},{7,3},{8,12},{12,8},{9,1... | collective-permute-start | bytes 983048 | tf_op jit(solution)/shard_map/ppermute | solution.py:508
  25.6 5.2 %collective-permute-start.4 = (bf16[640,256]{1,0:T(8,128)(2,1)S(1)}, bf16[640,256]{1,0:T(8,128)(2,1)S(1)}, u32[]{:S(2)}, u32[]{:S(2)}) collective-permute-start(bf16[640,256]{1,0:T(8,128)(2,1)S(1)} %collective-permute-done.refs_1_), channel_id=1, source_target_pairs={{0,4},{4,0},{1,5},{5,1},{2,6},{6,2},{3,7},{7,3},{8,12},{12,8},{9,1... | collective-permute-start | bytes 983048 | tf_op jit(solution)/shard_map/ppermute | solution.py:508
  28.6 2.2 %collective-permute-start.5 = (bf16[640,256]{1,0:T(8,128)(2,1)S(1)}, bf16[640,256]{1,0:T(8,128)(2,1)S(1)}, u32[]{:S(2)}, u32[]{:S(2)}) collective-permute-start(bf16[640,256]{1,0:T(8,128)(2,1)S(1)} %collective-permute-done.1.refs_2_), channel_id=1, source_target_pairs={{0,4},{4,0},{1,5},{5,1},{2,6},{6,2},{3,7},{7,3},{8,12},{12,8},{9,1... | collective-permute-start | bytes 983048 | tf_op jit(solution)/shard_map/ppermute | solution.py:508
  28.7 2.1 %collective-permute-start.6 = (bf16[640,256]{1,0:T(8,128)(2,1)S(1)}, bf16[640,256]{1,0:T(8,128)(2,1)S(1)}, u32[]{:S(2)}, u32[]{:S(2)}) collective-permute-start(bf16[640,256]{1,0:T(8,128)(2,1)S(1)} %collective-permute-done.2.refs_3_), channel_id=1, source_target_pairs={{0,4},{4,0},{1,5},{5,1},{2,6},{6,2},{3,7},{7,3},{8,12},{12,8},{9,1... | collective-permute-start | bytes 983048 | tf_op jit(solution)/shard_map/ppermute | solution.py:508
  30.8 34.0 %copy-start.1 = (bf16[256,2048]{1,0:T(8,128)(2,1)S(1)}, bf16[256,2048]{1,0:T(8,128)(2,1)}, u32[]{:S(2)}) copy-start(bf16[256,2048]{1,0:T(8,128)(2,1)} %q.3) | copy-start | bytes 3145732
  30.8 34.0 %copy-start.2 = (bf16[256,256]{1,0:T(8,128)(2,1)S(1)}, bf16[256,256]{1,0:T(8,128)(2,1)}, u32[]{:S(2)}) copy-start(bf16[256,256]{1,0:T(8,128)(2,1)} %xk.3) | copy-start | bytes 393220
  30.8 34.0 %copy-start.3 = (bf16[256,256]{1,0:T(8,128)(2,1)S(1)}, bf16[256,256]{1,0:T(8,128)(2,1)}, u32[]{:S(2)}) copy-start(bf16[256,256]{1,0:T(8,128)(2,1)} %xv.3) | copy-start | bytes 393220
  45.9 22.9 %copy-start.4 = (s32[64]{0:T(128)S(1)}, s32[64]{0:T(128)}, u32[]{:S(2)}) copy-start(s32[64]{0:T(128)} %owner) | copy-start | bytes 772
  56.7 12.7 %copy-start = (bf16[2048,128]{1,0:T(8,128)(2,1)S(1)}, bf16[2048,128]{1,0:T(8,128)(2,1)}, u32[]{:S(2)}) copy-start(bf16[2048,128]{1,0:T(8,128)(2,1)} %w.3) | copy-start | bytes 1572868
  56.7 9.8 %collective-permute-start.7 = (bf16[8,80,128]{2,1,0:T(8,128)(2,1)S(1)}, bf16[8,80,128]{2,1,0:T(8,128)(2,1)S(1)}, u32[]{:S(2)}, u32[]{:S(2)}) collective-permute-start(bf16[8,80,128]{2,1,0:T(8,128)(2,1)S(1)} %all_to_all.16.after.refs_0_), channel_id=1, source_target_pairs={{0,8},{8,16},{16,24},{24,0},{1,9},{9,17},{17,25},{25,1},{2,10},{10... | collective-permute-start | bytes 491528 | tf_op jit(solution)/shard_map/ppermute | solution.py:508
  57.6 9.0 %collective-permute-start.8 = (bf16[8,80,128]{2,1,0:T(8,128)(2,1)S(1)}, bf16[8,80,128]{2,1,0:T(8,128)(2,1)S(1)}, u32[]{:S(2)}, u32[]{:S(2)}) collective-permute-start(bf16[8,80,128]{2,1,0:T(8,128)(2,1)S(1)} %all_to_all.16.after.refs_0_), channel_id=1, source_target_pairs={{0,16},{8,24},{16,0},{24,8},{1,17},{9,25},{17,1},{25,9},{2,18},{10... | collective-permute-start | bytes 491528 | tf_op jit(solution)/shard_map/ppermute | solution.py:508
  59.8 8.7 %collective-permute-start.9 = (bf16[8,80,128]{2,1,0:T(8,128)(2,1)S(1)}, bf16[8,80,128]{2,1,0:T(8,128)(2,1)S(1)}, u32[]{:S(2)}, u32[]{:S(2)}) collective-permute-start(bf16[8,80,128]{2,1,0:T(8,128)(2,1)S(1)} %all_to_all.16.after.refs_0_), channel_id=1, source_target_pairs={{0,24},{8,0},{16,8},{24,16},{1,25},{9,1},{17,9},{25,17},{2,26},{10... | collective-permute-start | bytes 491528 | tf_op jit(solution)/shard_map/ppermute | solution.py:508
  61.1 8.6 %collective-permute-start.10 = (bf16[8,80,128]{2,1,0:T(8,128)(2,1)S(1)}, bf16[8,80,128]{2,1,0:T(8,128)(2,1)S(1)}, u32[]{:S(2)}, u32[]{:S(2)}) collective-permute-start(bf16[8,80,128]{2,1,0:T(8,128)(2,1)S(1)} %all_to_all.16.after.refs_0_), channel_id=1, source_target_pairs={{0,4},{4,0},{1,5},{5,1},{2,6},{6,2},{3,7},{7,3},{8,12},{12,8},{9,1... | collective-permute-start | bytes 491528 | tf_op jit(solution)/shard_map/ppermute | solution.py:508
  66.5 3.2 %collective-permute-start.11 = (bf16[8,80,128]{2,1,0:T(8,128)(2,1)S(1)}, bf16[8,80,128]{2,1,0:T(8,128)(2,1)S(1)}, u32[]{:S(2)}, u32[]{:S(2)}) collective-permute-start(bf16[8,80,128]{2,1,0:T(8,128)(2,1)S(1)} %collective-permute-done.7.refs_1_), channel_id=1, source_target_pairs={{0,4},{4,0},{1,5},{5,1},{2,6},{6,2},{3,7},{7,3},{8,12},{12,8},{9,1... | collective-permute-start | bytes 491528 | tf_op jit(solution)/shard_map/ppermute | solution.py:508
  66.7 3.1 %collective-permute-start.12 = (bf16[8,80,128]{2,1,0:T(8,128)(2,1)S(1)}, bf16[8,80,128]{2,1,0:T(8,128)(2,1)S(1)}, u32[]{:S(2)}, u32[]{:S(2)}) collective-permute-start(bf16[8,80,128]{2,1,0:T(8,128)(2,1)S(1)} %collective-permute-done.8.refs_2_), channel_id=1, source_target_pairs={{0,4},{4,0},{1,5},{5,1},{2,6},{6,2},{3,7},{7,3},{8,12},{12,8},{9,1... | collective-permute-start | bytes 491528 | tf_op jit(solution)/shard_map/ppermute | solution.py:508
  68.4 1.4 %collective-permute-start.13 = (bf16[8,80,128]{2,1,0:T(8,128)(2,1)S(1)}, bf16[8,80,128]{2,1,0:T(8,128)(2,1)S(1)}, u32[]{:S(2)}, u32[]{:S(2)}) collective-permute-start(bf16[8,80,128]{2,1,0:T(8,128)(2,1)S(1)} %collective-permute-done.9.refs_3_), channel_id=1, source_target_pairs={{0,4},{4,0},{1,5},{5,1},{2,6},{6,2},{3,7},{7,3},{8,12},{12,8},{9,1... | collective-permute-start | bytes 491528 | tf_op jit(solution)/shard_map/ppermute | solution.py:508
  70.3 7.0 %collective-permute-start.16 = (f32[64,128]{1,0:T(8,128)S(1)}, f32[64,128]{1,0:T(8,128)S(1)}, u32[]{:S(2)}, u32[]{:S(2)}) collective-permute-start(f32[64,128]{1,0:T(8,128)S(1)} %get-tuple-element.63), channel_id=1, source_target_pairs={{0,3},{1,0},{2,1},{3,2},{4,7},{5,4},{6,5},{7,6},{8,11},{9,8},{10,9... | collective-permute-start | bytes 98312 | tf_op jit(solution)/shard_map/ppermute | solution.py:508
  72.9 4.4 %collective-permute-start.15 = (f32[64,128]{1,0:T(8,128)S(1)}, f32[64,128]{1,0:T(8,128)S(1)}, u32[]{:S(2)}, u32[]{:S(2)}) collective-permute-start(f32[64,128]{1,0:T(8,128)S(1)} %get-tuple-element.62), channel_id=1, source_target_pairs={{0,2},{1,3},{2,0},{3,1},{4,6},{5,7},{6,4},{7,5},{8,10},{9,11},{10,... | collective-permute-start | bytes 98312 | tf_op jit(solution)/shard_map/ppermute | solution.py:508
  73.4 4.1 %collective-permute-start.14 = (f32[64,128]{1,0:T(8,128)S(1)}, f32[64,128]{1,0:T(8,128)S(1)}, u32[]{:S(2)}, u32[]{:S(2)}) collective-permute-start(f32[64,128]{1,0:T(8,128)S(1)} %get-tuple-element.61), channel_id=1, source_target_pairs={{0,1},{1,2},{2,3},{3,0},{4,5},{5,6},{6,7},{7,4},{8,9},{9,10},{10,1... | collective-permute-start | bytes 98312 | tf_op jit(solution)/shard_map/ppermute | solution.py:508

commit v5 on v4

--- a/solution.py
+++ b/solution.py
@@ -545,14 +545,14 @@
     picks = make_picks(owner)
     one, two, three = [shifted(merged, "y", NY, s) for s in range(1, NY)]
     own, lse = context_own(merged, ctx_queries, ctx_keys, ctx_values)
-    own, lse, one = lax.optimization_barrier((own, lse, one))
+    own, lse, picks, one = lax.optimization_barrier((own, lse, picks, one))
     lines = [merged, one, two, three]
     swapped = [shifted(b, "c", NC, 1) for b in lines]
     near = project_near(out_weight, lines)
     mine, *others = project(picks, near, out_weight, swapped)
     ctx_out = context_far(meta, ctx_queries, own, lse, lines + swapped)
     total = mine
-    for s, part in enumerate(others):
+    for s, part in reversed(list(enumerate(others))):
         total = total + shifted(part, "x", NX, s + 1)
     dec_out = total.astype(BF16).reshape(STEPS, 16, HD)
     return (ctx_out, dec_out)

time: 79.2 us -> 79.2 us (level)
  transfers between devices with their start and end apart: 18 -> 18, of which waited for: 3 -> 4; matrix products, arithmetic and copies ran while one was open for 0% -> 0% of each run, Pallas kernels for 12% -> 12%
where the time goes in v5:
time: 79.2 us; the launch traced here: 78.1 us
  starting transfers between devices  32.7 us (41%)
  blocking collectives  22.9 us (29%)
  Pallas kernels  15 us (19%)
  waiting for transfers between devices  6.02 us (8%)
  between operations  0.88 us (1%)
    ppermute x17, starting transfers between devices, shifted(): lax.ppermute(value, axis, [(i, (i + shift) % size) for i in range(size)])  24.5 us
    all_to_all x1, blocking collectives, on_device(): lax.all_to_all(second_part(meta, q, state, shards), 'z', 0, 0, tiled=True)  12.1 us
    all_to_all x1, blocking collectives, on_device(): lax.all_to_all(merge(meta, parts, ro, rm, rl), 'z', 0, 0, tiled=True)  10.8 us
    all_to_all x1, starting transfers between devices, on_device(): gathered = lax.all_to_all(packed, 'z', 0, 0, tiled=True)  8.19 us
    all_to_all x1, waiting for transfers between devices, on_device(): gathered = lax.all_to_all(packed, 'z', 0, 0, tiled=True)  5.01 us
    pallas_call x1, Pallas kernels, context_far(): pl.pallas_call(far_kernel, out_shape=jax.ShapeDtypeStruct((ROWS, 2048), B...  3.26 us
    pallas_call x1, Pallas kernels, second_part(): pl.pallas_call(second_kernel, out_shape=jax.ShapeDtypeStruct((NZ, 96, HD)...  2.02 us
    pallas_call x1, Pallas kernels, prep(): pl.pallas_call(prep_kernel, out_shape=(jax.ShapeDtypeStruct((NZ, 80, HD),...  1.96 us
  transfers between devices with their start and end apart: 18, of which 4 were waited for; matrix products, arithmetic and copies ran while one was open for 0% of the time, Pallas kernels for 12%

profile of v5, /device:TPU:1, one launch (start us, length us, event | category | flops | bytes accessed | tf_op | source)
XLA Modules:
  0.0 78.1 jit_solution(197747062436820077)
XLA Ops:
  0.6 2.0 %prep.1 = (bf16[8,80,128]{2,1,0:T(8,128)(2,1)}, bf16[640,256]{1,0:T(8,128)(2,1)S(1)}, bf16[640,256]{1,0:T(8,128)(2,1)S(1)}, bf16[640,256]{1,0:T(8,128)(2,1)S(1)}, bf16[640,256]{1,0:T(8,128)(2,1)S(1)}) custom-call(bf16[4,2048]{1,0:T(4,128)(2,1)} %bitcast.4, bf16[4,256]{1,0:T(4,128)(2,1)} %bitcast.6, bf16[4,256]{1,0:T(4,128)(2,1)} %bitcast.7, ...), custom_call_target="tpu_custom_call" | custom-call | flops 1048576 | bytes 1048576 | tf_op jit(solution)/shard_map/prep/pallas_call | solution.py:88
  2.6 2.2 %collective-permute-start = (bf16[640,256]{1,0:T(8,128)(2,1)S(1)}, bf16[640,256]{1,0:T(8,128)(2,1)S(1)}, u32[]{:S(2)}, u32[]{:S(2)}) collective-permute-start(bf16[640,256]{1,0:T(8,128)(2,1)S(1)} %get-tuple-element.39), channel_id=1, source_target_pairs={{0,8},{8,16},{16,24},{24,0},{1,9},{9,17},{17,25},{25,1},{2,10},{10... | collective-permute-start | bytes 983048 | tf_op jit(solution)/shard_map/ppermute | solution.py:508
  4.8 2.6 %collective-permute-start.1 = (bf16[640,256]{1,0:T(8,128)(2,1)S(1)}, bf16[640,256]{1,0:T(8,128)(2,1)S(1)}, u32[]{:S(2)}, u32[]{:S(2)}) collective-permute-start(bf16[640,256]{1,0:T(8,128)(2,1)S(1)} %get-tuple-element.40), channel_id=1, source_target_pairs={{0,16},{8,24},{16,0},{24,8},{1,17},{9,25},{17,1},{25,9},{2,18},{10... | collective-permute-start | bytes 983048 | tf_op jit(solution)/shard_map/ppermute | solution.py:508
  7.4 1.1 %collective-permute-start.2 = (bf16[640,256]{1,0:T(8,128)(2,1)S(1)}, bf16[640,256]{1,0:T(8,128)(2,1)S(1)}, u32[]{:S(2)}, u32[]{:S(2)}) collective-permute-start(bf16[640,256]{1,0:T(8,128)(2,1)S(1)} %get-tuple-element.41), channel_id=1, source_target_pairs={{0,24},{8,0},{16,8},{24,16},{1,25},{9,1},{17,9},{25,17},{2,26},{10... | collective-permute-start | bytes 983048 | tf_op jit(solution)/shard_map/ppermute | solution.py:508
  8.5 8.2 %all-to-all-start = ((bf16[8,80,128]{2,1,0:T(8,128)(2,1)}), bf16[8,80,128]{2,1,0:T(8,128)(2,1)S(1)}, u32[]{:S(2)}, u32[]{:S(2)}) async-start(bf16[8,80,128]{2,1,0:T(8,128)(2,1)} %get-tuple-element.34), calls=%async_computation | async-start | bytes 327680 | tf_op jit(solution)/shard_map/all_to_all | solution.py:535
  16.7 1.8 %collective-permute-start.3 = (bf16[640,256]{1,0:T(8,128)(2,1)S(1)}, bf16[640,256]{1,0:T(8,128)(2,1)S(1)}, u32[]{:S(2)}, u32[]{:S(2)}) collective-permute-start(bf16[640,256]{1,0:T(8,128)(2,1)S(1)} %get-tuple-element.44.refs_0_), channel_id=1, source_target_pairs={{0,4},{4,0},{1,5},{5,1},{2,6},{6,2},{3,7},{7,3},{8,12},{12,8},{9,1... | collective-permute-start | bytes 983048 | tf_op jit(solution)/shard_map/ppermute | solution.py:508
  18.5 1.5 %places.1.meta = s32[16]{0:T(128)S(1)} custom-call(s32[64]{0:T(128)} %owner, s32[64]{0:T(128)} %refs_1_.1, s32[64]{0:T(128)} %refs_2_.1), custom_call_target="tpu_custom_call" | custom-call | flops 1048576 | bytes 524288 | tf_op jit(solution)/shard_map/places/pallas_call | solution.py:396
  20.0 5.0 %all-to-all-done.g = bf16[8,80,128]{2,1,0:T(8,128)(2,1)S(1)} async-done(((bf16[8,80,128]{2,1,0:T(8,128)(2,1)}), bf16[8,80,128]{2,1,0:T(8,128)(2,1)S(1)}, u32[]{:S(2)}, u32[]{:S(2)}) %all-to-all-start) | async-done | bytes 163872 | tf_op jit(solution)/shard_map/all_to_all | solution.py:535
  25.0 0.5 line_part.1
  25.6 3.0 %collective-permute-start.4 = (bf16[640,256]{1,0:T(8,128)(2,1)S(1)}, bf16[640,256]{1,0:T(8,128)(2,1)S(1)}, u32[]{:S(2)}, u32[]{:S(2)}) collective-permute-start(bf16[640,256]{1,0:T(8,128)(2,1)S(1)} %collective-permute-done.refs_1_), channel_id=1, source_target_pairs={{0,4},{4,0},{1,5},{5,1},{2,6},{6,2},{3,7},{7,3},{8,12},{12,8},{9,1... | collective-permute-start | bytes 983048 | tf_op jit(solution)/shard_map/ppermute | solution.py:508
  28.7 0.4 collective-permute-start.6
  29.1 1.7 %first_part.1 = (f32[512,128]{1,0:T(8,128)S(1)}, f32[512,128]{1,0:T(8,128)S(1)}, f32[512,128]{1,0:T(8,128)S(1)}) custom-call(s32[16]{0:T(128)S(1)} %places.1.meta, bf16[512,128]{1,0:T(8,128)(2,1)S(1)} %get-tuple-element.43.q, bf16[640,256]{1,0:T(8,128)(2,1)S(1)} %get-tuple-element.44.refs_0_, bf16[640,256]{1,0:T(8,128)(2,1)S(1)} %collective-permute-done.refs_1_, ...), custom_call_target="tpu_custom_call" | custom-call | flops 536870912 | bytes 2097152 | tf_op jit(solution)/shard_map/first_part/pallas_call | solution.py:191
  30.8 2.0 %second_part.1 = bf16[8,96,128]{2,1,0:T(8,128)(2,1)S(1)} custom-call(s32[16]{0:T(128)S(1)} %places.1.meta, bf16[512,128]{1,0:T(8,128)(2,1)S(1)} %get-tuple-element.43.q, f32[512,128]{1,0:T(8,128)S(1)} %get-tuple-element.48.o, f32[512,128]{1,0:T(8,128)S(1)} %get-tuple-element.49.m, f32[512,128]{1,0:T(8,128)S(1)} %get-tuple-element.50.l, ...), custom_call_target="tpu_custom_call" | custom-call | flops 536870912 | bytes 2097152 | tf_op jit(solution)/shard_map/second_part/pallas_call | solution.py:244
  32.9 12.1 %all_to_all.15.parts = bf16[8,96,128]{2,1,0:T(8,128)(2,1)S(1)} all-to-all(bf16[8,96,128]{2,1,0:T(8,128)(2,1)S(1)} %second_part.1), channel_id=1, replica_groups=mesh['z'=8,'y'=4,'c'=2,'x'=4] {'z'}, dimensions={0} | all-to-all | bytes 393216 | tf_op jit(solution)/shard_map/all_to_all | solution.py:542
  44.9 0.9 %merge.1 = bf16[8,80,128]{2,1,0:T(8,128)(2,1)S(1)} custom-call(s32[16]{0:T(128)S(1)} %places.1.meta, bf16[8,96,128]{2,1,0:T(8,128)(2,1)S(1)} %all_to_all.15.parts, f32[64,128]{1,0:T(8,128)S(1)} %get-tuple-element.51.ro, f32[64,128]{1,0:T(8,128)S(1)} %get-tuple-element.52.rm, f32[64,128]{1,0:T(8,128)S(1)} %get-tuple-element.53.rl), custom_call_target="tpu_custom_call" | custom-call | flops 1048576 | bytes 524288 | tf_op jit(solution)/shard_map/merge/pallas_call | solution.py:281
  45.9 10.8 %all_to_all.16.after.refs_0_ = bf16[8,80,128]{2,1,0:T(8,128)(2,1)S(1)} all-to-all(bf16[8,80,128]{2,1,0:T(8,128)(2,1)S(1)} %merge.1), channel_id=1, replica_groups=mesh['z'=8,'y'=4,'c'=2,'x'=4] {'z'}, dimensions={0} | all-to-all | bytes 327680 | tf_op jit(solution)/shard_map/all_to_all | solution.py:543
  56.7 1.0 %collective-permute-start.7 = (bf16[8,80,128]{2,1,0:T(8,128)(2,1)S(1)}, bf16[8,80,128]{2,1,0:T(8,128)(2,1)S(1)}, u32[]{:S(2)}, u32[]{:S(2)}) collective-permute-start(bf16[8,80,128]{2,1,0:T(8,128)(2,1)S(1)} %all_to_all.16.after.refs_0_), channel_id=1, source_target_pairs={{0,8},{8,16},{16,24},{24,0},{1,9},{9,17},{17,25},{25,1},{2,10},{10... | collective-permute-start | bytes 491528 | tf_op jit(solution)/shard_map/ppermute | solution.py:508
  57.6 2.1 %collective-permute-start.8 = (bf16[8,80,128]{2,1,0:T(8,128)(2,1)S(1)}, bf16[8,80,128]{2,1,0:T(8,128)(2,1)S(1)}, u32[]{:S(2)}, u32[]{:S(2)}) collective-permute-start(bf16[8,80,128]{2,1,0:T(8,128)(2,1)S(1)} %all_to_all.16.after.refs_0_), channel_id=1, source_target_pairs={{0,16},{8,24},{16,0},{24,8},{1,17},{9,25},{17,1},{25,9},{2,18},{10... | collective-permute-start | bytes 491528 | tf_op jit(solution)/shard_map/ppermute | solution.py:508
  59.8 1.3 %collective-permute-start.9 = (bf16[8,80,128]{2,1,0:T(8,128)(2,1)S(1)}, bf16[8,80,128]{2,1,0:T(8,128)(2,1)S(1)}, u32[]{:S(2)}, u32[]{:S(2)}) collective-permute-start(bf16[8,80,128]{2,1,0:T(8,128)(2,1)S(1)} %all_to_all.16.after.refs_0_), channel_id=1, source_target_pairs={{0,24},{8,0},{16,8},{24,16},{1,25},{9,1},{17,9},{25,17},{2,26},{10... | collective-permute-start | bytes 491528 | tf_op jit(solution)/shard_map/ppermute | solution.py:508
  61.1 3.7 %collective-permute-start.10 = (bf16[8,80,128]{2,1,0:T(8,128)(2,1)S(1)}, bf16[8,80,128]{2,1,0:T(8,128)(2,1)S(1)}, u32[]{:S(2)}, u32[]{:S(2)}) collective-permute-start(bf16[8,80,128]{2,1,0:T(8,128)(2,1)S(1)} %all_to_all.16.after.refs_0_), channel_id=1, source_target_pairs={{0,4},{4,0},{1,5},{5,1},{2,6},{6,2},{3,7},{7,3},{8,12},{12,8},{9,1... | collective-permute-start | bytes 491528 | tf_op jit(solution)/shard_map/ppermute | solution.py:508
  64.8 0.7 picks.1
  65.5 1.7 %context_own.1 = (f32[256,2048]{1,0:T(8,128)S(1)}, f32[256,2048]{1,0:T(8,128)S(1)}) custom-call(bf16[8,80,128]{2,1,0:T(8,128)(2,1)S(1)} %all_to_all.16.after.refs_0_, bf16[256,2048]{1,0:T(8,128)(2,1)S(1)} %copy-done.1, bf16[256,256]{1,0:T(8,128)(2,1)S(1)} %copy-done.2, bf16[256,256]{1,0:T(8,128)(2,1)S(1)} %copy-done.3), custom_call_target="tpu_custom_call" | custom-call | flops 1073741824 | bytes 6291456 | tf_op jit(solution)/shard_map/context_own/pallas_call | solution.py:437
  67.3 1.1 %collective-permute-start.12 = (bf16[8,80,128]{2,1,0:T(8,128)(2,1)S(1)}, bf16[8,80,128]{2,1,0:T(8,128)(2,1)S(1)}, u32[]{:S(2)}, u32[]{:S(2)}) collective-permute-start(bf16[8,80,128]{2,1,0:T(8,128)(2,1)S(1)} %collective-permute-done.8.refs_2_), channel_id=1, source_target_pairs={{0,4},{4,0},{1,5},{5,1},{2,6},{6,2},{3,7},{7,3},{8,12},{12,8},{9,1... | collective-permute-start | bytes 491528 | tf_op jit(solution)/shard_map/ppermute | solution.py:508
  68.4 0.3 collective-permute-start.13
  69.0 0.4 collective-permute-done.12.refs_6_.refs_2_
  69.4 0.4 collective-permute-done.13.refs_7_.refs_3_
  69.8 0.5 project.1
  70.3 2.6 %collective-permute-start.14 = (f32[64,128]{1,0:T(8,128)S(1)}, f32[64,128]{1,0:T(8,128)S(1)}, u32[]{:S(2)}, u32[]{:S(2)}) collective-permute-start(f32[64,128]{1,0:T(8,128)S(1)} %get-tuple-element.63), channel_id=1, source_target_pairs={{0,3},{1,0},{2,1},{3,2},{4,7},{5,4},{6,5},{7,6},{8,11},{9,8},{10,9... | collective-permute-start | bytes 98312 | tf_op jit(solution)/shard_map/ppermute | solution.py:508
  72.9 0.5 collective-permute-start.15
  73.4 0.6 collective-permute-start.16
  74.0 3.3 %context_far.1 = bf16[256,2048]{1,0:T(8,128)(2,1)} custom-call(s32[16]{0:T(128)S(1)} %places.1.meta, bf16[256,2048]{1,0:T(8,128)(2,1)S(1)} %copy-done.1, f32[256,2048]{1,0:T(8,128)S(1)} %get-tuple-element.58.own, f32[256,2048]{1,0:T(8,128)S(1)} %get-tuple-element.59.lse, bf16[8,80,128]{2,1,0:T(8,128)(2,1)S(1)} %all_to_all.16.after.refs_0_, ...), custom_call_target="tpu_custom_call" | custom-call | flops 1073741824 | bytes 6291456 | tf_op jit(solution)/shard_map/context_far/pallas_call | solution.py:490
  77.5 0.6 add_convert_fusion
  (28 shorter events, 0.8 us)
Async XLA Ops:
  2.6 22.9 %collective-permute-start = (bf16[640,256]{1,0:T(8,128)(2,1)S(1)}, bf16[640,256]{1,0:T(8,128)(2,1)S(1)}, u32[]{:S(2)}, u32[]{:S(2)}) collective-permute-start(bf16[640,256]{1,0:T(8,128)(2,1)S(1)} %get-tuple-element.39), channel_id=1, source_target_pairs={{0,8},{8,16},{16,24},{24,0},{1,9},{9,17},{17,25},{25,1},{2,10},{10... | collective-permute-start | bytes 983048 | tf_op jit(solution)/shard_map/ppermute | solution.py:508
  4.8 20.7 %collective-permute-start.1 = (bf16[640,256]{1,0:T(8,128)(2,1)S(1)}, bf16[640,256]{1,0:T(8,128)(2,1)S(1)}, u32[]{:S(2)}, u32[]{:S(2)}) collective-permute-start(bf16[640,256]{1,0:T(8,128)(2,1)S(1)} %get-tuple-element.40), channel_id=1, source_target_pairs={{0,16},{8,24},{16,0},{24,8},{1,17},{9,25},{17,1},{25,9},{2,18},{10... | collective-permute-start | bytes 983048 | tf_op jit(solution)/shard_map/ppermute | solution.py:508
  7.4 18.1 %collective-permute-start.2 = (bf16[640,256]{1,0:T(8,128)(2,1)S(1)}, bf16[640,256]{1,0:T(8,128)(2,1)S(1)}, u32[]{:S(2)}, u32[]{:S(2)}) collective-permute-start(bf16[640,256]{1,0:T(8,128)(2,1)S(1)} %get-tuple-element.41), channel_id=1, source_target_pairs={{0,24},{8,0},{16,8},{24,16},{1,25},{9,1},{17,9},{25,17},{2,26},{10... | collective-permute-start | bytes 983048 | tf_op jit(solution)/shard_map/ppermute | solution.py:508
  8.5 16.5 %all-to-all-start = ((bf16[8,80,128]{2,1,0:T(8,128)(2,1)}), bf16[8,80,128]{2,1,0:T(8,128)(2,1)S(1)}, u32[]{:S(2)}, u32[]{:S(2)}) async-start(bf16[8,80,128]{2,1,0:T(8,128)(2,1)} %get-tuple-element.34), calls=%async_computation | async-start | bytes 327680 | tf_op jit(solution)/shard_map/all_to_all | solution.py:535
  16.7 14.1 %collective-permute-start.3 = (bf16[640,256]{1,0:T(8,128)(2,1)S(1)}, bf16[640,256]{1,0:T(8,128)(2,1)S(1)}, u32[]{:S(2)}, u32[]{:S(2)}) collective-permute-start(bf16[640,256]{1,0:T(8,128)(2,1)S(1)} %get-tuple-element.44.refs_0_), channel_id=1, source_target_pairs={{0,4},{4,0},{1,5},{5,1},{2,6},{6,2},{3,7},{7,3},{8,12},{12,8},{9,1... | collective-permute-start | bytes 983048 | tf_op jit(solution)/shard_map/ppermute | solution.py:508
  25.6 5.2 %collective-permute-start.4 = (bf16[640,256]{1,0:T(8,128)(2,1)S(1)}, bf16[640,256]{1,0:T(8,128)(2,1)S(1)}, u32[]{:S(2)}, u32[]{:S(2)}) collective-permute-start(bf16[640,256]{1,0:T(8,128)(2,1)S(1)} %collective-permute-done.refs_1_), channel_id=1, source_target_pairs={{0,4},{4,0},{1,5},{5,1},{2,6},{6,2},{3,7},{7,3},{8,12},{12,8},{9,1... | collective-permute-start | bytes 983048 | tf_op jit(solution)/shard_map/ppermute | solution.py:508
  28.6 2.2 %collective-permute-start.5 = (bf16[640,256]{1,0:T(8,128)(2,1)S(1)}, bf16[640,256]{1,0:T(8,128)(2,1)S(1)}, u32[]{:S(2)}, u32[]{:S(2)}) collective-permute-start(bf16[640,256]{1,0:T(8,128)(2,1)S(1)} %collective-permute-done.1.refs_2_), channel_id=1, source_target_pairs={{0,4},{4,0},{1,5},{5,1},{2,6},{6,2},{3,7},{7,3},{8,12},{12,8},{9,1... | collective-permute-start | bytes 983048 | tf_op jit(solution)/shard_map/ppermute | solution.py:508
  28.7 2.1 %collective-permute-start.6 = (bf16[640,256]{1,0:T(8,128)(2,1)S(1)}, bf16[640,256]{1,0:T(8,128)(2,1)S(1)}, u32[]{:S(2)}, u32[]{:S(2)}) collective-permute-start(bf16[640,256]{1,0:T(8,128)(2,1)S(1)} %collective-permute-done.2.refs_3_), channel_id=1, source_target_pairs={{0,4},{4,0},{1,5},{5,1},{2,6},{6,2},{3,7},{7,3},{8,12},{12,8},{9,1... | collective-permute-start | bytes 983048 | tf_op jit(solution)/shard_map/ppermute | solution.py:508
  30.8 34.0 %copy-start.4 = (s32[64]{0:T(128)S(1)}, s32[64]{0:T(128)}, u32[]{:S(2)}) copy-start(s32[64]{0:T(128)} %owner) | copy-start | bytes 772
  30.8 34.7 %copy-start.1 = (bf16[256,2048]{1,0:T(8,128)(2,1)S(1)}, bf16[256,2048]{1,0:T(8,128)(2,1)}, u32[]{:S(2)}) copy-start(bf16[256,2048]{1,0:T(8,128)(2,1)} %q.3) | copy-start | bytes 3145732
  30.8 34.7 %copy-start.2 = (bf16[256,256]{1,0:T(8,128)(2,1)S(1)}, bf16[256,256]{1,0:T(8,128)(2,1)}, u32[]{:S(2)}) copy-start(bf16[256,256]{1,0:T(8,128)(2,1)} %xk.3) | copy-start | bytes 393220
  30.8 34.7 %copy-start.3 = (bf16[256,256]{1,0:T(8,128)(2,1)S(1)}, bf16[256,256]{1,0:T(8,128)(2,1)}, u32[]{:S(2)}) copy-start(bf16[256,256]{1,0:T(8,128)(2,1)} %xv.3) | copy-start | bytes 393220
  56.7 12.0 %copy-start = (bf16[2048,128]{1,0:T(8,128)(2,1)S(1)}, bf16[2048,128]{1,0:T(8,128)(2,1)}, u32[]{:S(2)}) copy-start(bf16[2048,128]{1,0:T(8,128)(2,1)} %w.3) | copy-start | bytes 1572868
  56.7 10.5 %collective-permute-start.7 = (bf16[8,80,128]{2,1,0:T(8,128)(2,1)S(1)}, bf16[8,80,128]{2,1,0:T(8,128)(2,1)S(1)}, u32[]{:S(2)}, u32[]{:S(2)}) collective-permute-start(bf16[8,80,128]{2,1,0:T(8,128)(2,1)S(1)} %all_to_all.16.after.refs_0_), channel_id=1, source_target_pairs={{0,8},{8,16},{16,24},{24,0},{1,9},{9,17},{17,25},{25,1},{2,10},{10... | collective-permute-start | bytes 491528 | tf_op jit(solution)/shard_map/ppermute | solution.py:508
  57.6 9.7 %collective-permute-start.8 = (bf16[8,80,128]{2,1,0:T(8,128)(2,1)S(1)}, bf16[8,80,128]{2,1,0:T(8,128)(2,1)S(1)}, u32[]{:S(2)}, u32[]{:S(2)}) collective-permute-start(bf16[8,80,128]{2,1,0:T(8,128)(2,1)S(1)} %all_to_all.16.after.refs_0_), channel_id=1, source_target_pairs={{0,16},{8,24},{16,0},{24,8},{1,17},{9,25},{17,1},{25,9},{2,18},{10... | collective-permute-start | bytes 491528 | tf_op jit(solution)/shard_map/ppermute | solution.py:508
  59.8 8.7 %collective-permute-start.9 = (bf16[8,80,128]{2,1,0:T(8,128)(2,1)S(1)}, bf16[8,80,128]{2,1,0:T(8,128)(2,1)S(1)}, u32[]{:S(2)}, u32[]{:S(2)}) collective-permute-start(bf16[8,80,128]{2,1,0:T(8,128)(2,1)S(1)} %all_to_all.16.after.refs_0_), channel_id=1, source_target_pairs={{0,24},{8,0},{16,8},{24,16},{1,25},{9,1},{17,9},{25,17},{2,26},{10... | collective-permute-start | bytes 491528 | tf_op jit(solution)/shard_map/ppermute | solution.py:508
  61.1 8.0 %collective-permute-start.10 = (bf16[8,80,128]{2,1,0:T(8,128)(2,1)S(1)}, bf16[8,80,128]{2,1,0:T(8,128)(2,1)S(1)}, u32[]{:S(2)}, u32[]{:S(2)}) collective-permute-start(bf16[8,80,128]{2,1,0:T(8,128)(2,1)S(1)} %all_to_all.16.after.refs_0_), channel_id=1, source_target_pairs={{0,4},{4,0},{1,5},{5,1},{2,6},{6,2},{3,7},{7,3},{8,12},{12,8},{9,1... | collective-permute-start | bytes 491528 | tf_op jit(solution)/shard_map/ppermute | solution.py:508
  67.2 1.8 %collective-permute-start.11 = (bf16[8,80,128]{2,1,0:T(8,128)(2,1)S(1)}, bf16[8,80,128]{2,1,0:T(8,128)(2,1)S(1)}, u32[]{:S(2)}, u32[]{:S(2)}) collective-permute-start(bf16[8,80,128]{2,1,0:T(8,128)(2,1)S(1)} %collective-permute-done.7.refs_1_), channel_id=1, source_target_pairs={{0,4},{4,0},{1,5},{5,1},{2,6},{6,2},{3,7},{7,3},{8,12},{12,8},{9,1... | collective-permute-start | bytes 491528 | tf_op jit(solution)/shard_map/ppermute | solution.py:508
  67.3 2.1 %collective-permute-start.12 = (bf16[8,80,128]{2,1,0:T(8,128)(2,1)S(1)}, bf16[8,80,128]{2,1,0:T(8,128)(2,1)S(1)}, u32[]{:S(2)}, u32[]{:S(2)}) collective-permute-start(bf16[8,80,128]{2,1,0:T(8,128)(2,1)S(1)} %collective-permute-done.8.refs_2_), channel_id=1, source_target_pairs={{0,4},{4,0},{1,5},{5,1},{2,6},{6,2},{3,7},{7,3},{8,12},{12,8},{9,1... | collective-permute-start | bytes 491528 | tf_op jit(solution)/shard_map/ppermute | solution.py:508
  68.4 1.4 %collective-permute-start.13 = (bf16[8,80,128]{2,1,0:T(8,128)(2,1)S(1)}, bf16[8,80,128]{2,1,0:T(8,128)(2,1)S(1)}, u32[]{:S(2)}, u32[]{:S(2)}) collective-permute-start(bf16[8,80,128]{2,1,0:T(8,128)(2,1)S(1)} %collective-permute-done.9.refs_3_), channel_id=1, source_target_pairs={{0,4},{4,0},{1,5},{5,1},{2,6},{6,2},{3,7},{7,3},{8,12},{12,8},{9,1... | collective-permute-start | bytes 491528 | tf_op jit(solution)/shard_map/ppermute | solution.py:508
  70.3 7.0 %collective-permute-start.14 = (f32[64,128]{1,0:T(8,128)S(1)}, f32[64,128]{1,0:T(8,128)S(1)}, u32[]{:S(2)}, u32[]{:S(2)}) collective-permute-start(f32[64,128]{1,0:T(8,128)S(1)} %get-tuple-element.63), channel_id=1, source_target_pairs={{0,3},{1,0},{2,1},{3,2},{4,7},{5,4},{6,5},{7,6},{8,11},{9,8},{10,9... | collective-permute-start | bytes 98312 | tf_op jit(solution)/shard_map/ppermute | solution.py:508
  72.9 4.4 %collective-permute-start.15 = (f32[64,128]{1,0:T(8,128)S(1)}, f32[64,128]{1,0:T(8,128)S(1)}, u32[]{:S(2)}, u32[]{:S(2)}) collective-permute-start(f32[64,128]{1,0:T(8,128)S(1)} %get-tuple-element.64), channel_id=1, source_target_pairs={{0,2},{1,3},{2,0},{3,1},{4,6},{5,7},{6,4},{7,5},{8,10},{9,11},{10,... | collective-permute-start | bytes 98312 | tf_op jit(solution)/shard_map/ppermute | solution.py:508
  73.4 4.1 %collective-permute-start.16 = (f32[64,128]{1,0:T(8,128)S(1)}, f32[64,128]{1,0:T(8,128)S(1)}, u32[]{:S(2)}, u32[]{:S(2)}) collective-permute-start(f32[64,128]{1,0:T(8,128)S(1)} %get-tuple-element.65), channel_id=1, source_target_pairs={{0,1},{1,2},{2,3},{3,0},{4,5},{5,6},{6,7},{7,4},{8,9},{9,10},{10,1... | collective-permute-start | bytes 98312 | tf_op jit(solution)/shard_map/ppermute | solution.py:508
